TPU v7x, 256 devices: a whole 4x4x8 slice. The times are simulated.
256 devices in a mesh: dom: 16 (over x, y), row: 8 (over z), rep: 2 (over core).
Axes of the slice: x: 4, y: 4, z: 8, core: 2. Of those that a mesh axis runs over, the one named last changes fastest.
Arguments:
- features: float32 [65536, 128], P(('dom', 'row', 'rep')), may hold values from -6 to 6
- send_rows: int32 [16, 8, 16, 128], P('dom', 'row'), may hold values from 0 to 511
- tile_values: float32 [16, 8, 128, 128, 128], P('dom', 'row', 'rep'), may hold values from -0.125 to 0.125
- tile_rows: int32 [16, 8, 128], P('dom', 'row', 'rep'), may hold values from 0 to 3
- tile_cols: int32 [16, 8, 128], P('dom', 'row', 'rep'), may hold values from 0 to 47
- tile_counts: int32 [16, 8, 2], P('dom', 'row', 'rep'), may hold values from 1 to 64, as said below
- history: float32 [262144, 256], P(('dom', 'row')), may hold values from -4 to 4
- weight_one: float32 [128, 256], replicated, may hold values from -0.5 to 0.5
- weight_two: float32 [256, 256], replicated, may hold values from -0.375 to 0.375
- cotangent: float32 [65536, 256], P(('dom', 'row')), may hold values from -0.0234375 to 0.0234375
Outputs:
- output: float32 [65536, 256], P(('dom', 'row', 'rep'))
- grad_one: float32 [128, 256], replicated
- grad_two: float32 [256, 256], replicated
- fresh_halo: float32 [262144, 256], P(('dom', 'row'))
Inputs may be any that keep to these rules, and one draw needn't show every extreme that they name: `send_rows`: each entry names a node of the sending panel; entries may repeat. `tile_counts`: some device has all 64 slots live.
All inputs are finite; a program needn't handle non-finite values.
Results may differ from a plain program's by a relative error of at most 0.0003.
Values sent between devices are 32-bit elements; how exact they have to be, the bound alone decides.
No kernel may reach another device: no remote copies, remote signals or barrier semaphores. Data moves between devices by JAX's collectives and lax.ppermute only.
A program may use at most 128 MiB of HBM per device.

v0:
```python
import jax
import jax.numpy as jnp
from jax import lax
from jax.sharding import PartitionSpec as P

highest = lax.Precision.HIGHEST


def silu_grad(pre_act):
    sigmoid_value = jax.nn.sigmoid(pre_act)
    return sigmoid_value * (1.0 + pre_act * (1.0 - sigmoid_value))


def forward_terms(values, row_ids, col_ids, live_tiles, column_blocks, blocks):
    picked = jnp.take(column_blocks, col_ids, axis=0)
    product = (
        jnp.einsum("tij,tjw->tiw", values, picked, precision=highest) * live_tiles[:, None, None]
    )
    onehot = (row_ids[:, None] == jnp.arange(blocks, dtype=jnp.int32)[None, :]).astype(jnp.float32)
    return jnp.einsum("tb,tiw->biw", onehot, product, precision=highest)


def backward_terms(values, row_ids, col_ids, live_tiles, upstream_blocks, blocks):
    picked = jnp.take(upstream_blocks, row_ids, axis=0)
    product = (
        jnp.einsum("tji,tjw->tiw", values, picked, precision=highest) * live_tiles[:, None, None]
    )
    onehot = (col_ids[:, None] == jnp.arange(blocks, dtype=jnp.int32)[None, :]).astype(jnp.float32)
    return jnp.einsum("tc,tiw->ciw", onehot, product, precision=highest)


def tile_pass(terms_fn, values, row_ids, col_ids, count, data_blocks, blocks):
    live_tiles = (jnp.arange(values.shape[0], dtype=jnp.int32) < count).astype(jnp.float32)
    return terms_fn(values, row_ids, col_ids, live_tiles, data_blocks, blocks)


def whole_partition(node_rows):
    return lax.all_gather(node_rows, ("row", "rep"), axis=0, tiled=True)


def boundary_send(panel, targets):
    outgoing = jnp.take(panel, targets, axis=0)
    return lax.all_to_all(outgoing, "dom", split_axis=0, concat_axis=0, tiled=True)


def replica_reduce(partial_value):
    return lax.psum_scatter(partial_value, "rep", scatter_dimension=0, tiled=True)


def local(
    features,
    send_rows,
    tile_values,
    tile_rows,
    tile_cols,
    tile_counts,
    history,
    weight_one,
    weight_two,
    cotangent,
):
    tile_size = tile_values.shape[-1]
    domains = lax.axis_size("dom")
    panel_rows = cotangent.shape[0]
    half_rows = features.shape[0]
    row_blocks = panel_rows // tile_size
    values = tile_values.reshape(-1, tile_size, tile_size)
    row_ids = tile_rows.reshape(-1)
    col_ids = tile_cols.reshape(-1)
    count = tile_counts.reshape(())
    targets = send_rows.reshape(domains, tile_size)
    panel_start = lax.axis_index("row") * panel_rows
    half_start = lax.axis_index("rep") * half_rows
    feature_width = features.shape[1]
    hidden_width = weight_one.shape[1]
    whole_features = whole_partition(features)
    own_blocks = whole_features.shape[0] // tile_size
    own_panel = lax.dynamic_slice_in_dim(whole_features, panel_start, panel_rows, 0)
    halo_features = boundary_send(own_panel, targets)
    extended_one = jnp.concatenate(
        [whole_features, halo_features.reshape(-1, feature_width)], axis=0
    )
    partial_one = tile_pass(
        forward_terms,
        values,
        row_ids,
        col_ids,
        count,
        extended_one.reshape(-1, tile_size, feature_width),
        row_blocks,
    )
    agg_one = replica_reduce(partial_one.reshape(panel_rows, feature_width))
    pre_act = jnp.dot(agg_one, weight_one, precision=highest, preferred_element_type=jnp.float32)
    whole_hidden = whole_partition(jax.nn.silu(pre_act))
    hidden_panel = lax.dynamic_slice_in_dim(whole_hidden, panel_start, panel_rows, 0)
    fresh_halo = boundary_send(hidden_panel, targets).reshape(-1, hidden_width)
    extended_two = jnp.concatenate([whole_hidden, history], axis=0)
    partial_two = tile_pass(
        forward_terms,
        values,
        row_ids,
        col_ids,
        count,
        extended_two.reshape(-1, tile_size, hidden_width),
        row_blocks,
    )
    agg_two = replica_reduce(partial_two.reshape(panel_rows, hidden_width))
    output = jnp.dot(agg_two, weight_two, precision=highest, preferred_element_type=jnp.float32)
    cotangent_half = lax.dynamic_slice_in_dim(cotangent, half_start, half_rows, 0)
    grad_two_local = jnp.einsum("nf,nh->fh", agg_two, cotangent_half, precision=highest)
    upstream = jnp.einsum("nh,fh->nf", cotangent, weight_two, precision=highest)
    column_terms = tile_pass(
        backward_terms,
        values,
        row_ids,
        col_ids,
        count,
        upstream.reshape(row_blocks, tile_size, hidden_width),
        own_blocks,
    )
    flat_terms = column_terms.reshape(-1, hidden_width)
    grad_hidden = lax.psum_scatter(flat_terms, ("row", "rep"), scatter_dimension=0, tiled=True)
    grad_pre = grad_hidden * silu_grad(pre_act)
    grad_one_local = jnp.einsum("nf,nh->fh", agg_one, grad_pre, precision=highest)
    grad_one, grad_two = lax.psum((grad_one_local, grad_two_local), ("dom", "row", "rep"))
    return (output, grad_one, grad_two, fresh_halo)


def solution(mesh):
    return jax.shard_map(
        local,
        mesh=mesh,
        in_specs=(
            P(("dom", "row", "rep"), None),
            P("dom", "row", None, None),
            P("dom", "row", "rep", None, None),
            P("dom", "row", "rep"),
            P("dom", "row", "rep"),
            P("dom", "row", "rep"),
            P(("dom", "row"), None),
            P(),
            P(),
            P(("dom", "row"), None),
        ),
        out_specs=(P(("dom", "row", "rep"), None), P(), P(), P(("dom", "row"), None)),
        check_vma=False,
    )
```

profile of v0, /device:TPU:1, one launch (start us, length us, event | category | flops | bytes accessed | tf_op | source)
XLA Modules:
  0.0 530.8 jit_solution(2697605541671295728)
XLA Ops:
  9.3 44.5 %all-gather.3.cloned.1.call-done = f32[4096,128]{1,0:T(8,128)} async-done(((f32[256,128]{1,0:T(8,128)}), f32[4096,128]{1,0:T(8,128)}) %all-gather.3.cloned.1.call-update) | async-done | bytes 2097168 | tf_op jit(solution)/shard_map/all_gather | solution.py:38
  54.8 5.5 %gather_fusion = f32[2048,128]{1,0:T(8,128)S(1)} fusion(f32[512,128]{1,0:T(8,128)S(1)} %constant_dynamic-slice_fusion.1, s32[2048]{0:T(1024)S(1)} %fusion.40), kind=kCustom, calls=%fused_computation | custom fusion | bytes 2105344 | tf_op jit(solution)/shard_map/jit(_take)/gather | solution.py:42
  61.6 6.5 %all-to-all-start = ((f32[16,128,128]{2,1,0:T(8,128)}), f32[16,128,128]{2,1,0:T(8,128)S(1)}, u32[]{:S(2)}, u32[]{:S(2)}) async-start(f32[16,128,128]{2,1,0:T(8,128)} %broadcast_select_fusion.1), calls=%async_computation | async-start | bytes 2097152 | tf_op jit(solution)/shard_map/all_to_all | solution.py:43
  68.9 15.0 %all-to-all-done = f32[16,128,128]{2,1,0:T(8,128)S(1)} async-done(((f32[16,128,128]{2,1,0:T(8,128)}), f32[16,128,128]{2,1,0:T(8,128)S(1)}, u32[]{:S(2)}, u32[]{:S(2)}) %all-to-all-start) | async-done | bytes 1048608 | tf_op jit(solution)/shard_map/all_to_all | solution.py:43
  84.0 3.5 pad_maximum_fusion.1
  87.4 4.6 gather_fusion.1
  92.1 13.2 %fusion.14 = f32[64,128,128]{2,1,0:T(8,128)} fusion(f32[1,1,64,128,128]{4,3,2,1,0:T(8,128)} %param.12, f32[64,128,128]{2,1,0:T(8,128)} %gather_fusion.1, pred[64]{0:T(512)(128)(4,1)S(1)} %get-tuple-element.9), kind=kOutput, calls=%fused_computation.20 | convolution fusion | flops 1611661312 | bytes 12582976 | tf_op jit(solution)/shard_map/tij,tjw->tiw/dot_general | solution.py:17
  105.3 5.4 %copy.18 = f32[64,128,128]{1,0,2:T(8,128)} copy(f32[64,128,128]{2,1,0:T(8,128)} %fusion.14) | data formatting | bytes 8388608 | tf_op jit(solution)/shard_map/tij,tjw->tiw/dot_general | solution.py:17
  110.7 3.9 fusion.10
  115.4 11.1 %reduce-scatter.4.cloned.1.call-done = f32[256,128]{1,0:T(8,128)} async-done(((f32[512,128]{1,0:T(8,128)}), f32[256,128]{1,0:T(8,128)}) %reduce-scatter.4.cloned.1.call-update) | async-done | bytes 131088 | tf_op jit(solution)/shard_map/reduce_scatter | solution.py:47
  129.3 4.3 gather_fusion.3
  133.7 29.3 %fusion.5 = f32[64,256,128]{2,1,0:T(8,128)} fusion(f32[64,128,256]{2,1,0:T(8,128)} %gather_fusion.3, f32[1,1,64,128,128]{4,3,2,1,0:T(8,128)} %param.12, pred[64]{0:T(512)(128)(4,1)S(1)} %get-tuple-element.8), kind=kOutput, calls=%fused_computation.10 | convolution fusion | flops 3223322624 | bytes 20971584 | tf_op jit(solution)/shard_map/tji,tjw->tiw/dot_general | solution.py:26
  163.0 9.2 %copy.20 = f32[64,256,128]{1,0,2:T(8,128)} copy(f32[64,256,128]{2,1,0:T(8,128)} %fusion.5) | data formatting | bytes 16777216 | tf_op jit(solution)/shard_map/tji,tjw->tiw/dot_general | solution.py:26
  172.2 6.3 %fusion = f32[32,128,256]{2,0,1:T(8,128)S(1)} fusion(f32[64,256,128]{1,0,2:T(8,128)} %copy.20, f32[64]{0:T(128)S(1)} %compare_convert_fusion, s32[64]{0:T(128)S(1)} %bitcast.77), kind=kOutput, calls=%fused_computation.5 | convolution fusion | flops 807405568 | bytes 12583424 | tf_op jit(solution)/shard_map/tc,tiw->ciw/dot_general | solution.py:29
  178.5 4.4 copy.17
  184.0 6.6 %gather_fusion.4 = f32[2048,256]{1,0:T(8,128)S(1)} fusion(f32[512,256]{1,0:T(8,128)S(1)} %constant_dynamic-slice_fusion, s32[2048]{0:T(1024)S(1)} %fusion.40), kind=kCustom, calls=%fused_computation.4 | custom fusion | bytes 4202496 | tf_op jit(solution)/shard_map/jit(_take)/gather | solution.py:42
  192.3 6.3 %all-to-all-start.1 = ((f32[16,128,256]{2,1,0:T(8,128)}), f32[16,128,256]{2,1,0:T(8,128)S(1)}, u32[]{:S(2)}, u32[]{:S(2)}) async-start(f32[16,128,256]{2,1,0:T(8,128)} %broadcast_select_fusion), calls=%async_computation.4 | async-start | bytes 4194304 | tf_op jit(solution)/shard_map/all_to_all | solution.py:43
  198.7 6.0 %pad_maximum_fusion = f32[6144,256]{1,0:T(8,128)} fusion(f32[2048,256]{1,0:T(8,128)} %param.16, f32[4096,256]{1,0:T(8,128)} %all-gather.5.cloned.1.call-done), kind=kLoop, calls=%fused_computation.15 | loop fusion | flops 1572864 | bytes 12582912 | tf_op jit(solution)/shard_map/concatenate | solution.py:97
  204.7 7.1 %gather_fusion.2 = f32[64,128,256]{2,1,0:T(8,128)} fusion(f32[48,128,256]{2,1,0:T(8,128)} %bitcast.66, s32[1024]{0:T(1024)S(1)} %pad_clamp_fusion.1), kind=kCustom, calls=%fused_computation.2 | custom fusion | bytes 16777472 | tf_op jit(solution)/shard_map/jit(_take)/gather | solution.py:15
  211.8 19.7 %fusion.8 = f32[64,256,128]{2,1,0:T(8,128)} fusion(f32[64,128,256]{2,1,0:T(8,128)} %gather_fusion.2, f32[1,1,64,128,128]{4,3,2,1,0:T(8,128)} %param.12, pred[64]{0:T(512)(128)(4,1)S(1)} %get-tuple-element.9), kind=kOutput, calls=%fused_computation.13 | convolution fusion | flops 3223322624 | bytes 20971584 | tf_op jit(solution)/shard_map/tij,tjw->tiw/dot_general | solution.py:17
  231.5 9.2 %copy.19 = f32[64,256,128]{1,0,2:T(8,128)} copy(f32[64,256,128]{2,1,0:T(8,128)} %fusion.8) | data formatting | bytes 16777216 | tf_op jit(solution)/shard_map/tij,tjw->tiw/dot_general | solution.py:17
  240.7 6.7 %fusion.2 = f32[4,128,256]{2,0,1:T(4,128)S(1)} fusion(f32[64,256,128]{1,0,2:T(8,128)} %copy.19, f32[64]{0:T(128)S(1)} %compare_convert_fusion, s32[64]{0:T(128)S(1)} %bitcast.76), kind=kOutput, calls=%fused_computation.7 | convolution fusion | flops 102760704 | bytes 8913408 | tf_op jit(solution)/shard_map/tb,tiw->biw/dot_general | solution.py:20
  250.5 13.5 %reduce-scatter.6.cloned.1.call-done = f32[256,256]{1,0:T(8,128)} async-done(((f32[512,256]{1,0:T(8,128)}), f32[256,256]{1,0:T(8,128)}) %reduce-scatter.6.cloned.1.call-update) | async-done | bytes 262160 | tf_op jit(solution)/shard_map/reduce_scatter | solution.py:47
  268.3 250.7 %all-reduce.3.cloned.1.call-done = (f32[128,256]{1,0:T(8,128)}, f32[256,256]{1,0:T(8,128)}) async-done(((f32[128,256]{1,0:T(8,128)}, f32[256,256]{1,0:T(8,128)}), (f32[128,256]{1,0:T(8,128)}, f32[256,256]{1,0:T(8,128)})) %all-reduce.3.cloned.1.call-update) | async-done | bytes 393232 | tf_op jit(solution)/shard_map/psum | solution.py:125
  (51 shorter events, 22.7 us)
Async XLA Ops:
  7.2 121.5 %copy-start = (f32[512,256]{1,0:T(8,128)S(1)}, f32[512,256]{1,0:T(8,128)}, u32[]{:S(2)}) copy-start(f32[512,256]{1,0:T(8,128)} %param.19) | copy-start | bytes 1572868
  7.2 46.6 %all-gather.3.cloned.1.call-start = ((), (), s32[]{:S(2)}) async-start(), calls=%async_computation.5 | async-start | bytes 2228224 | tf_op jit(solution)/shard_map/all_gather | solution.py:38
  60.3 8.6 %copy-start.3 = (s32[1,1,64]{2,1,0:T(1,128)S(1)}, s32[1,1,64]{2,1,0:T(1,128)}, u32[]{:S(2)}) copy-start(s32[1,1,64]{2,1,0:T(1,128)} %param.14) | copy-start | bytes 772
  60.3 8.6 %copy-start.2 = (s32[1,1,64]{2,1,0:T(1,128)S(1)}, s32[1,1,64]{2,1,0:T(1,128)}, u32[]{:S(2)}) copy-start(s32[1,1,64]{2,1,0:T(1,128)} %param.13) | copy-start | bytes 772
  61.6 22.3 %all-to-all-start = ((f32[16,128,128]{2,1,0:T(8,128)}), f32[16,128,128]{2,1,0:T(8,128)S(1)}, u32[]{:S(2)}, u32[]{:S(2)}) async-start(f32[16,128,128]{2,1,0:T(8,128)} %broadcast_select_fusion.1), calls=%async_computation | async-start | bytes 2097152 | tf_op jit(solution)/shard_map/all_to_all | solution.py:43
  68.1 58.4 %reduce-scatter.4.cloned.1.call-start = ((), (), s32[]{:S(2)}) async-start(), calls=%async_computation.6 | async-start | bytes 393216 | tf_op jit(solution)/shard_map/reduce_scatter | solution.py:47
  110.7 15.8 %copy-start.4 = (f32[128,256]{1,0:T(8,128)S(1)}, f32[128,256]{1,0:T(8,128)}, u32[]{:S(2)}) copy-start(f32[128,256]{1,0:T(8,128)} %param.17) | copy-start | bytes 393220
  110.7 18.0 %copy-start.1 = (f32[256,256]{1,0:T(8,128)S(1)}, f32[256,256]{1,0:T(8,128)}, u32[]{:S(2)}) copy-start(f32[256,256]{1,0:T(8,128)} %param.18) | copy-start | bytes 786436
  115.3 67.6 %all-gather.5.cloned.1.call-start = ((), (), s32[]{:S(2)}) async-start(), calls=%async_computation.7 | async-start | bytes 4456448 | tf_op jit(solution)/shard_map/all_gather | solution.py:38
  128.6 119.8 %reduce-scatter.8.cloned.1.call-start = ((), (), s32[]{:S(2)}) async-start(), calls=%async_computation.9 | async-start | bytes 4456448 | tf_op jit(solution)/shard_map/reduce_scatter | solution.py:122
  192.3 75.9 %all-to-all-start.1 = ((f32[16,128,256]{2,1,0:T(8,128)}), f32[16,128,256]{2,1,0:T(8,128)S(1)}, u32[]{:S(2)}, u32[]{:S(2)}) async-start(f32[16,128,256]{2,1,0:T(8,128)} %broadcast_select_fusion), calls=%async_computation.4 | async-start | bytes 4194304 | tf_op jit(solution)/shard_map/all_to_all | solution.py:43
  198.6 65.3 %reduce-scatter.6.cloned.1.call-start = ((), (), s32[]{:S(2)}) async-start(), calls=%async_computation.8 | async-start | bytes 786432 | tf_op jit(solution)/shard_map/reduce_scatter | solution.py:47
  240.7 7.7 %copy-start.5 = (f32[256,128]{1,0:T(8,128)S(1)}, f32[256,128]{1,0:T(8,128)}, u32[]{:S(2)}) copy-start(f32[256,128]{1,0:T(8,128)} %reduce-scatter.4.cloned.1.call-done) | copy-start | bytes 393220
  240.7 7.7 %copy-start.6 = (f32[256,256]{1,0:T(8,128)S(1)}, f32[256,256]{1,0:T(8,128)}, u32[]{:S(2)}) copy-start(f32[256,256]{1,0:T(8,128)} %get-tuple-element.7) | copy-start | bytes 786436
  248.3 270.7 %all-reduce.3.cloned.1.call-start = ((), (), s32[]{:S(2)}) async-start(), calls=%async_computation.10 | async-start | bytes 786432 | tf_op jit(solution)/shard_map/psum | solution.py:125
Sparse Core Ops, SparseCore 0:
  9.8 43.9 all-gather.2
  115.5 11.0 reduce-scatter.3
  129.1 43.0 all-gather.4
  183.0 61.0 reduce-scatter.7
  248.4 15.4 reduce-scatter.5
  270.0 248.9 all-reduce.2
where the time goes:
time: 541 us; the launch traced here: 531 us
  waiting for transfers between devices  336 us (62%)
  matrix products  88.1 us (16%)
  local copies, waits for them, and re-layouts  64.7 us (12%)
  between operations  15.4 us (3%)
  other arithmetic  13.9 us (3%)
  starting transfers between devices  13.1 us (2%)
    psum x1, waiting for transfers between devices, local(): lax.psum((grad_one_local, grad_two_local), ('dom', 'row', 'rep'))  251 us
    all_gather x2, waiting for transfers between devices, whole_partition(): return lax.all_gather(node_rows, ('row', 'rep'), axis=0, tiled=True)  44.5 us
    dot_general x2, matrix products, forward_terms(): jnp.einsum('tij,tjw->tiw', values, picked, precision=highest)  32.9 us
    dot_general x1, matrix products, backward_terms(): jnp.einsum('tji,tjw->tiw', values, picked, precision=highest)  29.3 us
    reduce_scatter x2, waiting for transfers between devices, replica_reduce(): lax.psum_scatter(partial_value, 'rep', scatter_dimension=0, tiled=True)  24.7 us
    all_to_all x2, waiting for transfers between devices, boundary_send(): lax.all_to_all(outgoing, 'dom', split_axis=0, concat_axis=0, tiled=True)  15 us
    dot_general x2, local copies, waits for them, and re-layouts, forward_terms(): jnp.einsum('tij,tjw->tiw', values, picked, precision=highest)  14.6 us
    all_to_all x2, starting transfers between devices, boundary_send(): lax.all_to_all(outgoing, 'dom', split_axis=0, concat_axis=0, tiled=True)  12.8 us
  transfers between devices with their start and end apart: 8, of which 5 were waited for; matrix products, arithmetic and copies ran while one was open for 23% of the time, Pallas kernels for 0%

commit v1 on v0

v1 whole, which is shorter than its diff:
```python
import jax
import jax.numpy as jnp
from jax import lax
from jax.experimental import pallas as pl
from jax.experimental.pallas import tpu as pltpu
from jax.sharding import PartitionSpec as P

f32 = jnp.float32
bf16 = jnp.bfloat16
TILE = 128
N_DOM, N_ROW, N_REP = 16, 8, 2
OWN = 32
COLS = 48
SLOTS = 64
GROUP = 8
NN = (((1,), (0,)), ((), ()))
TN = (((0,), (0,)), ((), ()))
NT = (((1,), (1,)), ((), ()))
VMEM_LIMIT = 56 * 1024 * 1024
SHIFTS = (0, 1, 7, 4, 2, 6, 3, 5)


def split2(x):
    hi = x.astype(bf16)
    lo = (x - hi.astype(f32)).astype(bf16)
    return hi, lo


def split3(x):
    hi = x.astype(bf16)
    rest = x - hi.astype(f32)
    mid = rest.astype(bf16)
    lo = (rest - mid.astype(f32)).astype(bf16)
    return hi, mid, lo


def mm(a, b, dims):
    return lax.dot_general(a, b, dims, preferred_element_type=f32)


def dot3(a, b, dims):
    a_hi, a_lo = split2(a)
    b_hi, b_lo = split2(b)
    return mm(a_hi, b_hi, dims) + (mm(a_hi, b_lo, dims) + mm(a_lo, b_hi, dims))


def pick_rows(panel, idx_ref, out_ref):
    rhs = jnp.concatenate(split3(panel), axis=1)
    lane = lax.broadcasted_iota(jnp.int32, (TILE, TILE), 1).astype(f32)
    for b in range(idx_ref.shape[0]):
        row = jnp.broadcast_to(idx_ref[b : b + 1, :].astype(f32), (TILE, TILE))
        col = row.T
        marks = [
            jnp.where(col == lane + float(k * TILE), 1.0, 0.0).astype(bf16)
            for k in range(panel.shape[0] // TILE)
        ]
        got = mm(jnp.concatenate(marks, axis=1), rhs, NN)
        out_ref[pl.ds(b * TILE, TILE), :] = (
            got[:, :TILE] + got[:, TILE : 2 * TILE]
        ) + got[:, 2 * TILE :]


def pick_features_kernel(place, mine, other, idx_ref, out_ref):
    q = place[0]
    a, b = mine[...], other[...]
    panel = jnp.concatenate([jnp.where(q == 0, a, b), jnp.where(q == 0, b, a)], axis=0)
    pick_rows(panel, idx_ref, out_ref)


def pick_agg_kernel(place, mine, other, idx_ref, panel_ref, half_ref, out_ref):
    q = place[0]
    panel = mine[...] + other[...]
    panel_ref[...] = panel
    half = panel.shape[0] // 2
    half_ref[...] = jnp.where(q == 0, panel[:half], panel[half:])
    pick_rows(panel, idx_ref, out_ref)


def backward_kernel(rows_s, cols_s, count_s, cot, w2, tiles, out, u_scr):
    g = pl.program_id(0)

    @pl.when(g == 0)
    def _():
        out[...] = jnp.zeros_like(out)
        for b in range(4):
            up = dot3(cot[pl.ds(b * TILE, TILE), :], w2[...], NT)
            hi, lo = split2(up)
            u_scr[b, :TILE, :] = hi
            u_scr[b, TILE:, :] = lo

    count = count_s[0, 0]

    @pl.when(g * GROUP < count)
    def _():
        for i in range(GROUP):
            t = g * GROUP + i
            live = jnp.where(t < count, 1.0, 0.0).astype(f32)
            a_hi, a_lo = split2((tiles[i] * live).T)
            u = u_scr[rows_s[0, t]]
            term = mm(jnp.concatenate([a_hi, a_hi], axis=1), u, NN) + mm(a_lo, u[:TILE], NN)
            c = jnp.minimum(cols_s[0, t], OWN)
            out[c] += term


def forward_tiles(g, rows_s, cols_s, count, tiles, x_scr, acc):
    @pl.when(g * GROUP < count)
    def _():
        for i in range(GROUP):
            t = g * GROUP + i
            live = jnp.where(t < count, 1.0, 0.0).astype(f32)
            a_hi, a_lo = split2(tiles[i] * live)
            x = x_scr[cols_s[0, t]]
            term = mm(jnp.concatenate([a_hi, a_hi], axis=1), x, NN) + mm(a_lo, x[:TILE], NN)
            acc[rows_s[0, t]] += term


def piece_copies(place, mine, theirs, dst, sems):
    q, r = place[0], place[1]
    copies = []
    for n, s in enumerate(SHIFTS):
        base = lax.rem(r + (N_ROW - s), N_ROW) * 4
        for m, (refs, half) in enumerate(((mine, q), (theirs, 1 - q))):
            if refs[n] is None:
                continue
            copies.append(
                pltpu.make_async_copy(
                    refs[n], dst.at[pl.ds(base + half * 2, 2)], sems.at[2 * n + m]
                )
            )
    return copies


def pass_one_kernel(place, rows_s, cols_s, count_s, *refs):
    mine, theirs = refs[:8], refs[8:16]
    halo_mine, halo_theirs, tiles, acc, xf, x_scr, sems = refs[16:]
    g = pl.program_id(0)
    q = place[0]

    @pl.when(g == 0)
    def _():
        copies = piece_copies(place, mine, theirs, xf, sems)
        for m, (ref, half) in enumerate(((halo_mine, q), (halo_theirs, 1 - q))):
            at = pl.multiple_of(half * 64, 64)
            copies.append(
                pltpu.make_async_copy(
                    ref, xf.at[pl.ds(OWN, N_DOM), pl.ds(at, 64), :], sems.at[16 + m]
                )
            )
        for c in copies:
            c.start()
        acc[...] = jnp.zeros_like(acc)
        for c in copies:
            c.wait()

        def body(j, carry):
            for k in range(4):
                hi, lo = split2(xf[j * 4 + k])
                x_scr[j * 4 + k, :TILE, :] = hi
                x_scr[j * 4 + k, TILE:, :] = lo
            return carry

        lax.fori_loop(0, COLS // 4, body, 0)

    forward_tiles(g, rows_s, cols_s, count_s[0, 0], tiles, x_scr, acc)


def layer_two_kernel(place, rows_s, cols_s, count_s, *refs):
    own, mine, theirs = refs[0], refs[1:8], refs[8:15]
    (w1, w2, cot, hist, c_terms, tiles) = refs[15:21]
    (g_keep, g_send, p_keep, p_send) = refs[21:25]
    (xf, h_scr, acc, g_one, sems) = refs[25:]
    g = pl.program_id(0)
    q, r = place[0], place[1]

    @pl.when(g == 0)
    def _():
        copies = piece_copies(place, (None,) + mine, (None,) + theirs, xf, sems)
        copies.append(pltpu.make_async_copy(own, xf.at[pl.ds(r * 4, 4)], sems.at[0]))
        for c in copies:
            c.start()
        acc[...] = jnp.zeros_like(acc)
        g_one[...] = jnp.zeros_like(g_one)
        for c in copies:
            c.wait()

    @pl.when(g < N_ROW)
    def _():
        w_hi, w_lo = split2(w1[...])
        total = jnp.zeros((TILE, w1.shape[1]), f32)
        for b in range(4):
            x = xf[g * 4 + b]
            x_hi, x_lo = split2(x)
            pre = mm(x_hi, w_hi, NN) + (mm(x_hi, w_lo, NN) + mm(x_lo, w_hi, NN))
            sig = 1.0 / (1.0 + jnp.exp(-pre))
            hi, lo = split2(pre * sig)
            h_scr[g * 4 + b, :TILE, :] = hi
            h_scr[g * 4 + b, TILE:, :] = lo
            grad = c_terms[b] * (sig * (1.0 + pre * (1.0 - sig)))
            total += dot3(x, grad, TN)
        g_one[...] += total
        for b in range(2):
            hi, lo = split2(hist[b])
            h_scr[OWN + g * 2 + b, :TILE, :] = hi
            h_scr[OWN + g * 2 + b, TILE:, :] = lo

    @pl.when(g >= N_ROW)
    def _():
        forward_tiles(g - N_ROW, rows_s, cols_s, count_s[0, 0], tiles, h_scr, acc)

    @pl.when(g == 2 * N_ROW - 1)
    def _():
        agg = acc[...].reshape(4 * TILE, -1)
        g_two = dot3(agg, cot[...], TN)
        left = jnp.concatenate([g_one[:, :TILE], g_two[:, :TILE]], axis=0)
        right = jnp.concatenate([g_one[:, TILE:], g_two[:, TILE:]], axis=0)
        g_keep[...] = jnp.where(q == 0, left, right)
        g_send[...] = jnp.where(q == 0, right, left)
        prod = dot3(agg, w2[...], NN)
        low, high = prod[: 2 * TILE], prod[2 * TILE :]
        p_keep[...] = jnp.where(q == 0, low, high)
        p_send[...] = jnp.where(q == 0, high, low)


def fresh_kernel(place, mine, theirs, w1, out):
    q = place[0]
    w_hi, w_lo = split2(w1[...])
    for s in range(mine.shape[0]):
        a, b = mine[s], theirs[s]
        x = jnp.concatenate([jnp.where(q == 0, a, b), jnp.where(q == 0, b, a)], axis=0)
        x_hi, x_lo = split2(x)
        pre = mm(x_hi, w_hi, NN) + (mm(x_hi, w_lo, NN) + mm(x_lo, w_hi, NN))
        out[pl.ds(s * TILE, TILE), :] = pre / (1.0 + jnp.exp(-pre))


SMEM = pl.BlockSpec(memory_space=pltpu.SMEM)
VMEM = pl.BlockSpec(memory_space=pltpu.VMEM)
ANY = pl.BlockSpec(memory_space=pl.ANY)


def params():
    return pltpu.CompilerParams(vmem_limit_bytes=VMEM_LIMIT)


def cost(flops, moved):
    return pl.CostEstimate(flops=flops, bytes_accessed=moved, transcendentals=0)


def swap(x):
    return lax.ppermute(x, "rep", [(0, 1), (1, 0)])


def shift(x, k):
    return lax.ppermute(x, "row", [(i, (i + k) % N_ROW) for i in range(N_ROW)])


def ring_pieces(x):
    a = shift(x, 1)
    b = shift(x, 7)
    f = shift(x, 4)
    a2 = shift(a, 1)
    b2 = shift(b, 7)
    a3 = shift(a, 2)
    b3 = shift(b, 6)
    return [a, b, f, a2, b2, a3, b3]


def blocks(x):
    return x.reshape(-1, TILE, x.shape[-1])


def to_all(x):
    return lax.all_to_all(x, "dom", split_axis=0, concat_axis=0, tiled=True)


def reduce_all(keep, send):
    part = (keep + swap(send)).reshape(N_DOM, -1, TILE)
    part = jnp.sum(to_all(part), axis=0)
    part = jnp.broadcast_to(part[None], (N_ROW,) + part.shape)
    part = lax.all_to_all(part, "row", split_axis=0, concat_axis=0, tiled=True)
    part = jnp.sum(part, axis=0)
    part = jnp.broadcast_to(part[None], (N_DOM,) + part.shape)
    mine = to_all(part).reshape(-1, TILE)
    theirs = swap(mine)
    return mine, theirs


def local(
    features,
    send_rows,
    tile_values,
    tile_rows,
    tile_cols,
    tile_counts,
    history,
    weight_one,
    weight_two,
    cotangent,
):
    f_dim, h_dim = weight_one.shape
    tiles = tile_values.reshape(SLOTS, TILE, TILE)
    rows_s = tile_rows.reshape(1, SLOTS)
    cols_s = tile_cols.reshape(1, SLOTS)
    count_s = tile_counts.reshape(1, 1)
    q = lax.axis_index("rep")
    place = jnp.stack([q, lax.axis_index("row")]).astype(jnp.int32)
    idx = lax.dynamic_slice_in_dim(send_rows.reshape(N_DOM, TILE), q * 64, 64, 1).reshape(8, TILE)

    mine = [features] + ring_pieces(features)
    theirs = [swap(x) for x in mine]
    outgoing = pl.pallas_call(
        pick_features_kernel,
        name="pick_features",
        out_shape=jax.ShapeDtypeStruct((N_DOM * 64, f_dim), f32),
        in_specs=[SMEM, VMEM, VMEM, VMEM],
        out_specs=VMEM,
        compiler_params=params(),
    )(place, features, theirs[0], idx)
    halo_mine = to_all(outgoing.reshape(N_DOM, 64, f_dim))
    halo_theirs = swap(halo_mine)

    tile_spec = pl.BlockSpec((GROUP, TILE, TILE), lambda g: (g, 0, 0))

    c_terms = pl.pallas_call(
        backward_kernel,
        name="backward",
        grid=(SLOTS // GROUP,),
        out_shape=jax.ShapeDtypeStruct((OWN + 1, TILE, h_dim), f32),
        in_specs=[SMEM, SMEM, SMEM, VMEM, VMEM, tile_spec],
        out_specs=pl.BlockSpec((OWN + 1, TILE, h_dim), lambda g: (0, 0, 0)),
        scratch_shapes=[pltpu.VMEM((4, 2 * TILE, h_dim), bf16)],
        compiler_params=params(),
        cost_estimate=cost(6 * SLOTS * TILE * TILE * h_dim, 9 << 20),
    )(rows_s, cols_s, count_s, cotangent, weight_two, tiles)

    part_one = pl.pallas_call(
        pass_one_kernel,
        name="pass_one",
        grid=(SLOTS // GROUP,),
        out_shape=jax.ShapeDtypeStruct((4, TILE, f_dim), f32),
        in_specs=[SMEM] * 4 + [ANY] * 18 + [tile_spec],
        out_specs=pl.BlockSpec((4, TILE, f_dim), lambda g: (0, 0, 0)),
        scratch_shapes=[
            pltpu.VMEM((COLS, TILE, f_dim), f32),
            pltpu.VMEM((COLS, 2 * TILE, f_dim), bf16),
            pltpu.SemaphoreType.DMA((18,)),
        ],
        compiler_params=params(),
    )(
        place,
        rows_s,
        cols_s,
        count_s,
        *[blocks(x) for x in mine],
        *[blocks(x) for x in theirs],
        halo_mine,
        halo_theirs,
        tiles,
    ).reshape(4 * TILE, f_dim)

    panel, half, outgoing_two = pl.pallas_call(
        pick_agg_kernel,
        name="pick_agg",
        out_shape=(
            jax.ShapeDtypeStruct((4 * TILE, f_dim), f32),
            jax.ShapeDtypeStruct((2 * TILE, f_dim), f32),
            jax.ShapeDtypeStruct((N_DOM * 64, f_dim), f32),
        ),
        in_specs=[SMEM, VMEM, VMEM, VMEM],
        out_specs=(VMEM, VMEM, VMEM),
        compiler_params=params(),
    )(place, part_one, swap(part_one), idx)
    agg_mine = ring_pieces(half)
    agg_theirs = [swap(x) for x in agg_mine]
    fresh_mine = to_all(outgoing_two.reshape(N_DOM, 64, f_dim))
    fresh_theirs = swap(fresh_mine)

    last = N_ROW - 1
    g_keep, g_send, p_keep, p_send = pl.pallas_call(
        layer_two_kernel,
        name="layer_two",
        grid=(2 * N_ROW,),
        out_shape=(
            jax.ShapeDtypeStruct((f_dim + h_dim, TILE), f32),
            jax.ShapeDtypeStruct((f_dim + h_dim, TILE), f32),
            jax.ShapeDtypeStruct((2 * TILE, h_dim), f32),
            jax.ShapeDtypeStruct((2 * TILE, h_dim), f32),
        ),
        in_specs=[SMEM] * 4
        + [ANY] * 15
        + [
            VMEM,
            VMEM,
            VMEM,
            pl.BlockSpec((2, TILE, h_dim), lambda g: (jnp.minimum(g, last), 0, 0)),
            pl.BlockSpec((4, TILE, h_dim), lambda g: (jnp.minimum(g, last), 0, 0)),
            pl.BlockSpec((GROUP, TILE, TILE), lambda g: (jnp.maximum(g - N_ROW, 0), 0, 0)),
        ],
        out_specs=(VMEM, VMEM, VMEM, VMEM),
        scratch_shapes=[
            pltpu.VMEM((OWN, TILE, f_dim), f32),
            pltpu.VMEM((COLS, 2 * TILE, h_dim), bf16),
            pltpu.VMEM((4, TILE, h_dim), f32),
            pltpu.VMEM((f_dim, h_dim), f32),
            pltpu.SemaphoreType.DMA((16,)),
        ],
        compiler_params=params(),
    )(
        place,
        rows_s,
        cols_s,
        count_s,
        blocks(panel),
        *[blocks(x) for x in agg_mine],
        *[blocks(x) for x in agg_theirs],
        weight_one,
        weight_two,
        cotangent,
        blocks(history),
        c_terms,
        tiles,
    )

    output = p_keep + swap(p_send)
    mine_g, theirs_g = reduce_all(g_keep, g_send)
    low = jnp.where(q == 0, mine_g, theirs_g)
    high = jnp.where(q == 0, theirs_g, mine_g)
    grads = jnp.concatenate([low, high], axis=1)

    fresh = pl.pallas_call(
        fresh_kernel,
        name="fresh",
        out_shape=jax.ShapeDtypeStruct((N_DOM * TILE, h_dim), f32),
        in_specs=[SMEM, VMEM, VMEM, VMEM],
        out_specs=VMEM,
        compiler_params=params(),
        cost_estimate=cost(6 * N_DOM * TILE * f_dim * h_dim, 4 << 20),
    )(place, fresh_mine, fresh_theirs, weight_one)
    return (output, grads[:f_dim], grads[f_dim:], fresh)


def solution(mesh):
    return jax.shard_map(
        local,
        mesh=mesh,
        in_specs=(
            P(("dom", "row", "rep"), None),
            P("dom", "row", None, None),
            P("dom", "row", "rep", None, None),
            P("dom", "row", "rep"),
            P("dom", "row", "rep"),
            P("dom", "row", "rep"),
            P(("dom", "row"), None),
            P(),
            P(),
            P(("dom", "row"), None),
        ),
        out_specs=(P(("dom", "row", "rep"), None), P(), P(), P(("dom", "row"), None)),
        check_vma=False,
    )
```

time: 541 us -> 176 us (0.33); the launches traced: 531 us -> 176 us
  waiting for transfers between devices: 336 us -> 21.8 us
  matrix products: 88.1 us -> 0 us
  starting transfers between devices: 13.1 us -> 84.4 us
  local copies, waits for them, and re-layouts: 64.7 us -> 5.15 us
  Pallas kernels: 0 us -> 43.5 us
  blocking collectives: 0 us -> 13.9 us
  between operations: 15.4 us -> 1.68 us
  other arithmetic: 13.9 us -> 5.38 us
    psum x1 -> x0, waiting for transfers between devices: 251 us -> none  [local(): lax.psum((grad_one_local, grad_two_local), ('dom', 'row', 'rep'))]
    dot_general x11 -> x0, matrix products: 88.1 us -> none  [the longest x2 32.9 us: forward_terms(): jnp.einsum('tij,tjw->tiw', values, picked, precision=highest)]
    ppermute x0 -> x35, starting transfers between devices: none -> 63.2 us  [the longest x14 35.5 us: shift(): return lax.ppermute(x, 'row', [(i, (i + k) % N_ROW) for i in range(N_ROW)])]
    all_gather x2 -> x0, waiting for transfers between devices: 44.5 us -> none  [whole_partition(): return lax.all_gather(node_rows, ('row', 'rep'), axis=0, tiled=True)]
    pallas_call x0 -> x6, Pallas kernels: none -> 43.5 us  [the longest x1 17.9 us: local(): pl.pallas_call(layer_two_kernel, name='layer_two', grid=(2 * N_ROW,), out...]
    dot_general x6 -> x0, local copies, waits for them, and re-layouts: 29.8 us -> none  [the longest x2 14.6 us: forward_terms(): jnp.einsum('tij,tjw->tiw', values, picked, precision=highest)]
    gather x5 -> x0, local copies, waits for them, and re-layouts: 28.2 us -> none  [the longest x2 12.1 us: boundary_send(): outgoing = jnp.take(panel, targets, axis=0)]
    reduce_scatter x3 -> x0, waiting for transfers between devices: 24.7 us -> none  [the longest x2 24.7 us: replica_reduce(): lax.psum_scatter(partial_value, 'rep', scatter_dimension=0, tiled=True)]
  transfers between devices with their start and end apart: 8 -> 39, of which waited for: 5 -> 10; matrix products, arithmetic and copies ran while one was open for 23% -> 3% of each run, Pallas kernels for 0% -> 17%
where the time goes in v1:
time: 176 us
  starting transfers between devices  84.4 us (48%)
  Pallas kernels  43.5 us (25%)
  waiting for transfers between devices  21.8 us (12%)
  blocking collectives  13.9 us (8%)
  other arithmetic  5.38 us (3%)
  local copies, waits for them, and re-layouts  5.15 us (3%)
    ppermute x14, starting transfers between devices, shift(): return lax.ppermute(x, 'row', [(i, (i + k) % N_ROW) for i in range(N_ROW)])  35.5 us
    ppermute x21, starting transfers between devices, swap(): return lax.ppermute(x, 'rep', [(0, 1), (1, 0)])  27.7 us
    all_to_all x4, starting transfers between devices, to_all(): return lax.all_to_all(x, 'dom', split_axis=0, concat_axis=0, tiled=True)  21.2 us
    pallas_call x1, Pallas kernels, local(): pl.pallas_call(layer_two_kernel, name='layer_two', grid=(2 * N_ROW,), out...  17.9 us
    all_to_all x4, waiting for transfers between devices, to_all(): return lax.all_to_all(x, 'dom', split_axis=0, concat_axis=0, tiled=True)  14.9 us
    all_to_all x1, blocking collectives, reduce_all(): part = lax.all_to_all(part, 'row', split_axis=0, concat_axis=0, tiled=True)  13.9 us
    pallas_call x1, Pallas kernels, local(): pl.pallas_call(backward_kernel, name='backward', grid=(SLOTS // GROUP,),...  8.63 us
    pallas_call x1, Pallas kernels, local(): pl.pallas_call(pass_one_kernel, name='pass_one', grid=(SLOTS // GROUP,),...  8.3 us
  transfers between devices with their start and end apart: 39, of which 10 were waited for; matrix products, arithmetic and copies ran while one was open for 3% of the time, Pallas kernels for 17%

profile of v1, /device:TPU:1, one launch (start us, length us, event | category | flops | bytes accessed | tf_op | source)
XLA Modules:
  0.0 175.8 jit_solution(13934061391288661715)
XLA Ops:
  0.6 3.3 %collective-permute-start.7 = (f32[256,128]{1,0:T(8,128)}, f32[256,128]{1,0:T(8,128)S(1)}, u32[]{:S(2)}, u32[]{:S(2)}) collective-permute-start(f32[256,128]{1,0:T(8,128)} %mine.1), channel_id=1, source_target_pairs={{0,1},{1,0},{2,3},{3,2},{4,5},{5,4},{6,7},{7,6},{8,9},{9,8},{10,11... | collective-permute-start | bytes 393224 | tf_op jit(solution)/shard_map/ppermute | solution.py:249
  6.0 2.5 %pick_features.1 = f32[1024,128]{1,0:T(8,128)} custom-call(s32[2]{0:T(128)} %pad_add_fusion.place, f32[256,128]{1,0:T(8,128)} %mine.1, f32[256,128]{1,0:T(8,128)} %copy-done.3, s32[8,128]{1,0:T(8,128)} %reshape.158.idx_ref), custom_call_target="tpu_custom_call" | custom-call | tf_op jit(solution)/shard_map/pick_features/pallas_call | solution.py:310
  8.5 5.0 %all-to-all-start = ((f32[16,64,128]{2,1,0:T(8,128)}), f32[16,64,128]{2,1,0:T(8,128)S(1)}, u32[]{:S(2)}, u32[]{:S(2)}) async-start(f32[16,64,128]{2,1,0:T(8,128)} %bitcast.53), calls=%async_computation | async-start | bytes 1048576 | tf_op jit(solution)/shard_map/all_to_all | solution.py:272
  15.3 4.0 %collective-permute-start.1 = (f32[256,128]{1,0:T(8,128)}, f32[256,128]{1,0:T(8,128)S(1)}, u32[]{:S(2)}, u32[]{:S(2)}) collective-permute-start(f32[256,128]{1,0:T(8,128)} %mine.1), channel_id=1, source_target_pairs={{0,14},{2,0},{4,2},{6,4},{8,6},{10,8},{12,10},{14,12},{1,15},{3,1}... | collective-permute-start | bytes 393224 | tf_op jit(solution)/shard_map/ppermute | solution.py:253
  19.3 4.6 %all-to-all-done.refs_16_ = f32[16,64,128]{2,1,0:T(8,128)S(1)} async-done(((f32[16,64,128]{2,1,0:T(8,128)}), f32[16,64,128]{2,1,0:T(8,128)S(1)}, u32[]{:S(2)}, u32[]{:S(2)}) %all-to-all-start) | async-done | bytes 524320 | tf_op jit(solution)/shard_map/all_to_all | solution.py:272
  26.0 6.9 %collective-permute-start.2 = (f32[256,128]{1,0:T(8,128)}, f32[256,128]{1,0:T(8,128)S(1)}, u32[]{:S(2)}, u32[]{:S(2)}) collective-permute-start(f32[256,128]{1,0:T(8,128)} %mine.1), channel_id=1, source_target_pairs={{0,8},{2,10},{4,12},{6,14},{8,0},{10,2},{12,4},{14,6},{1,9},{3,11}... | collective-permute-start | bytes 393224 | tf_op jit(solution)/shard_map/ppermute | solution.py:253
  37.0 6.9 %collective-permute-start.6 = (f32[256,128]{1,0:T(8,128)S(1)}, f32[256,128]{1,0:T(8,128)S(1)}, u32[]{:S(2)}, u32[]{:S(2)}) collective-permute-start(f32[256,128]{1,0:T(8,128)S(1)} %collective-permute-done.1), channel_id=1, source_target_pairs={{0,12},{2,14},{4,0},{6,2},{8,4},{10,6},{12,8},{14,10},{1,13},{3,15... | collective-permute-start | bytes 393224 | tf_op jit(solution)/shard_map/ppermute | solution.py:253
  52.4 8.3 %pass_one.1 = f32[4,128,128]{2,1,0:T(8,128)} custom-call(s32[2]{0:T(128)} %pad_add_fusion.place, s32[1,64]{1,0:T(1,128)} %bitcast.90, s32[1,64]{1,0:T(1,128)} %bitcast.93, s32[1,1]{1,0:T(1,128)} %bitcast.47.count_s, f32[2,128,128]{2,1,0:T(8,128)} %bitcast.58, f32[2,128,128]{2,1,0:T(8,128)} %bitcast.62, f32[2,128,128]{2,1,0:T(8,128)} %bitcast.64, ...), custom_call_target="tpu_custom_call" | custom-call | tf_op jit(solution)/shard_map/pass_one/pallas_call | solution.py:335
  63.4 2.6 %pick_agg.1 = (f32[512,128]{1,0:T(8,128)}, f32[256,128]{1,0:T(8,128)}, f32[1024,128]{1,0:T(8,128)}) custom-call(s32[2]{0:T(128)} %pad_add_fusion.place, f32[512,128]{1,0:T(8,128)} %bitcast.56, f32[512,128]{1,0:T(8,128)} %copy-done.6, s32[8,128]{1,0:T(8,128)} %reshape.158.idx_ref), custom_call_target="tpu_custom_call" | custom-call | tf_op jit(solution)/shard_map/pick_agg/pallas_call | solution.py:360
  68.7 3.5 %collective-permute-start.19 = (f32[256,128]{1,0:T(8,128)}, f32[256,128]{1,0:T(8,128)S(1)}, u32[]{:S(2)}, u32[]{:S(2)}) collective-permute-start(f32[256,128]{1,0:T(8,128)} %get-tuple-element.12), channel_id=1, source_target_pairs={{0,8},{2,10},{4,12},{6,14},{8,0},{10,2},{12,4},{14,6},{1,9},{3,11}... | collective-permute-start | bytes 393224 | tf_op jit(solution)/shard_map/ppermute | solution.py:253
  73.1 3.7 %all-to-all-start.4 = ((f32[16,64,128]{2,1,0:T(8,128)}), f32[16,64,128]{2,1,0:T(8,128)S(1)}, u32[]{:S(2)}, u32[]{:S(2)}) async-start(f32[16,64,128]{2,1,0:T(8,128)} %bitcast.60), calls=%async_computation.4 | async-start | bytes 1048576 | tf_op jit(solution)/shard_map/all_to_all | solution.py:272
  79.6 3.8 %collective-permute-start.23 = (f32[256,128]{1,0:T(8,128)S(1)}, f32[256,128]{1,0:T(8,128)S(1)}, u32[]{:S(2)}, u32[]{:S(2)}) collective-permute-start(f32[256,128]{1,0:T(8,128)S(1)} %collective-permute-done.18), channel_id=1, source_target_pairs={{0,12},{2,14},{4,0},{6,2},{8,4},{10,6},{12,8},{14,10},{1,13},{3,15... | collective-permute-start | bytes 393224 | tf_op jit(solution)/shard_map/ppermute | solution.py:253
  83.4 3.8 %collective-permute-start.24 = (f32[256,128]{1,0:T(8,128)S(1)}, f32[256,128]{1,0:T(8,128)S(1)}, u32[]{:S(2)}, u32[]{:S(2)}) collective-permute-start(f32[256,128]{1,0:T(8,128)S(1)} %collective-permute-done.17), channel_id=1, source_target_pairs={{0,1},{1,0},{2,3},{3,2},{4,5},{5,4},{6,7},{7,6},{8,9},{9,8},{10,11... | collective-permute-start | bytes 393224 | tf_op jit(solution)/shard_map/ppermute | solution.py:249
  88.2 3.4 %collective-permute-start.27 = (f32[256,128]{1,0:T(8,128)S(1)}, f32[256,128]{1,0:T(8,128)S(1)}, u32[]{:S(2)}, u32[]{:S(2)}) collective-permute-start(f32[256,128]{1,0:T(8,128)S(1)} %collective-permute-done.20), channel_id=1, source_target_pairs={{0,1},{1,0},{2,3},{3,2},{4,5},{5,4},{6,7},{7,6},{8,9},{9,8},{10,11... | collective-permute-start | bytes 393224 | tf_op jit(solution)/shard_map/ppermute | solution.py:249
  92.4 8.6 %backward.1.refs_19_ = f32[33,128,256]{2,1,0:T(8,128)} custom-call(s32[1,64]{1,0:T(1,128)} %bitcast.91, s32[1,64]{1,0:T(1,128)} %bitcast.94, s32[1,1]{1,0:T(1,128)} %bitcast.48.count_s, f32[512,256]{1,0:T(8,128)} %refs_17_.1, f32[256,256]{1,0:T(8,128)} %refs_16_.1, f32[64,128,128]{2,1,0:T(8,128)} %bitcast.51), custom_call_target="tpu_custom_call" | custom-call | flops 1610612736 | bytes 9437184 | tf_op jit(solution)/shard_map/backward/pallas_call | solution.py:323
  101.9 17.9 %layer_two.1 = (f32[384,128]{1,0:T(8,128)}, f32[384,128]{1,0:T(8,128)}, f32[256,256]{1,0:T(8,128)}, f32[256,256]{1,0:T(8,128)}) custom-call(s32[2]{0:T(128)} %pad_add_fusion.place, s32[1,64]{1,0:T(1,128)} %bitcast.92, s32[1,64]{1,0:T(1,128)} %bitcast.95, s32[1,1]{1,0:T(1,128)} %bitcast.49.count_s, f32[4,128,128]{2,1,0:T(8,128)} %bitcast.61, ...), custom_call_target="tpu_custom_call" | custom-call | tf_op jit(solution)/shard_map/layer_two/pallas_call | solution.py:378
  123.2 8.7 %all-to-all-start.1 = ((f32[16,24,128]{2,1,0:T(8,128)}), f32[16,24,128]{2,1,0:T(8,128)S(1)}, u32[]{:S(2)}, u32[]{:S(2)}) async-start(f32[16,24,128]{2,1,0:T(8,128)} %bitcast.40), calls=%async_computation.1 | async-start | bytes 393216 | tf_op jit(solution)/shard_map/all_to_all | solution.py:272
  132.4 6.5 %all-to-all-done.1 = f32[16,24,128]{2,1,0:T(8,128)S(1)} async-done(((f32[16,24,128]{2,1,0:T(8,128)}), f32[16,24,128]{2,1,0:T(8,128)S(1)}, u32[]{:S(2)}, u32[]{:S(2)}) %all-to-all-start.1) | async-done | bytes 196640 | tf_op jit(solution)/shard_map/all_to_all | solution.py:272
  138.9 13.9 %all_to_all.25 = f32[8,24,128]{2,1,0:T(8,128)S(1)} all-to-all(f32[8,24,128]{2,1,0:T(8,128)S(1)} %broadcast_in_dim.4), channel_id=1, replica_groups=mesh['dom'=16,'row'=8,'rep'=2] {'row'}, dimensions={0} | all-to-all | bytes 196608 | tf_op jit(solution)/shard_map/all_to_all | solution.py:279
  153.5 3.7 %all-to-all-start.3 = ((f32[16,24,128]{2,1,0:T(8,128)}), f32[16,24,128]{2,1,0:T(8,128)S(1)}, u32[]{:S(2)}, u32[]{:S(2)}) async-start(f32[16,24,128]{2,1,0:T(8,128)} %broadcast_in_dim.5), calls=%async_computation.3 | async-start | bytes 393216 | tf_op jit(solution)/shard_map/all_to_all | solution.py:272
  157.3 3.1 %collective-permute-start.31 = (f32[256,256]{1,0:T(8,128)}, f32[256,256]{1,0:T(8,128)S(1)}, u32[]{:S(2)}, u32[]{:S(2)}) collective-permute-start(f32[256,256]{1,0:T(8,128)} %get-tuple-element.14), channel_id=1, source_target_pairs={{0,1},{1,0},{2,3},{3,2},{4,5},{5,4},{6,7},{7,6},{8,9},{9,8},{10,11... | collective-permute-start | bytes 786440 | tf_op jit(solution)/shard_map/ppermute | solution.py:249
  160.3 3.9 %all-to-all-done.3 = f32[16,24,128]{2,1,0:T(8,128)S(1)} async-done(((f32[16,24,128]{2,1,0:T(8,128)}), f32[16,24,128]{2,1,0:T(8,128)S(1)}, u32[]{:S(2)}, u32[]{:S(2)}) %all-to-all-start.3) | async-done | bytes 196640 | tf_op jit(solution)/shard_map/all_to_all | solution.py:272
  164.2 4.1 %collective-permute-start.33 = (f32[384,128]{1,0:T(8,128)S(1)}, f32[384,128]{1,0:T(8,128)S(1)}, u32[]{:S(2)}, u32[]{:S(2)}) collective-permute-start(f32[384,128]{1,0:T(8,128)S(1)} %bitcast.57), channel_id=1, source_target_pairs={{0,1},{1,0},{2,3},{3,2},{4,5},{5,4},{6,7},{7,6},{8,9},{9,8},{10,11... | collective-permute-start | bytes 589832 | tf_op jit(solution)/shard_map/ppermute | solution.py:249
  170.8 3.6 %fresh.1 = f32[2048,256]{1,0:T(8,128)} custom-call(s32[2]{0:T(128)} %pad_add_fusion.place, f32[16,64,128]{2,1,0:T(8,128)} %copy-done.2, f32[16,64,128]{2,1,0:T(8,128)} %copy-done.5, f32[128,256]{1,0:T(8,128)} %w1.1), custom_call_target="tpu_custom_call" | custom-call | flops 402653184 | bytes 4194304 | tf_op jit(solution)/shard_map/fresh/pallas_call | solution.py:429
  (143 shorter events, 37.8 us)
Async XLA Ops:
  8.5 15.3 %all-to-all-start = ((f32[16,64,128]{2,1,0:T(8,128)}), f32[16,64,128]{2,1,0:T(8,128)S(1)}, u32[]{:S(2)}, u32[]{:S(2)}) async-start(f32[16,64,128]{2,1,0:T(8,128)} %bitcast.53), calls=%async_computation | async-start | bytes 1048576 | tf_op jit(solution)/shard_map/all_to_all | solution.py:272
  13.5 19.4 %collective-permute-start = (f32[256,128]{1,0:T(8,128)}, f32[256,128]{1,0:T(8,128)S(1)}, u32[]{:S(2)}, u32[]{:S(2)}) collective-permute-start(f32[256,128]{1,0:T(8,128)} %mine.1), channel_id=1, source_target_pairs={{0,2},{2,4},{4,6},{6,8},{8,10},{10,12},{12,14},{14,0},{1,3},{3,5},... | collective-permute-start | bytes 393224 | tf_op jit(solution)/shard_map/ppermute | solution.py:253
  15.3 18.4 %collective-permute-start.1 = (f32[256,128]{1,0:T(8,128)}, f32[256,128]{1,0:T(8,128)S(1)}, u32[]{:S(2)}, u32[]{:S(2)}) collective-permute-start(f32[256,128]{1,0:T(8,128)} %mine.1), channel_id=1, source_target_pairs={{0,14},{2,0},{4,2},{6,4},{8,6},{10,8},{12,10},{14,12},{1,15},{3,1}... | collective-permute-start | bytes 393224 | tf_op jit(solution)/shard_map/ppermute | solution.py:253
  23.9 27.7 %collective-permute-start.15 = (f32[16,64,128]{2,1,0:T(8,128)S(1)}, f32[16,64,128]{2,1,0:T(8,128)S(1)}, u32[]{:S(2)}, u32[]{:S(2)}) collective-permute-start(f32[16,64,128]{2,1,0:T(8,128)S(1)} %all-to-all-done.refs_16_), channel_id=1, source_target_pairs={{0,1},{1,0},{2,3},{3,2},{4,5},{5,4},{6,7},{7,6},{8,9},{9,8},{10,11... | collective-permute-start | bytes 1572872 | tf_op jit(solution)/shard_map/ppermute | solution.py:249
  26.0 11.0 %collective-permute-start.2 = (f32[256,128]{1,0:T(8,128)}, f32[256,128]{1,0:T(8,128)S(1)}, u32[]{:S(2)}, u32[]{:S(2)}) collective-permute-start(f32[256,128]{1,0:T(8,128)} %mine.1), channel_id=1, source_target_pairs={{0,8},{2,10},{4,12},{6,14},{8,0},{10,2},{12,4},{14,6},{1,9},{3,11}... | collective-permute-start | bytes 393224 | tf_op jit(solution)/shard_map/ppermute | solution.py:253
  32.9 11.0 %collective-permute-start.3 = (f32[256,128]{1,0:T(8,128)S(1)}, f32[256,128]{1,0:T(8,128)S(1)}, u32[]{:S(2)}, u32[]{:S(2)}) collective-permute-start(f32[256,128]{1,0:T(8,128)S(1)} %collective-permute-done), channel_id=1, source_target_pairs={{0,2},{2,4},{4,6},{6,8},{8,10},{10,12},{12,14},{14,0},{1,3},{3,5},... | collective-permute-start | bytes 393224 | tf_op jit(solution)/shard_map/ppermute | solution.py:253
  33.7 11.9 %collective-permute-start.4 = (f32[256,128]{1,0:T(8,128)S(1)}, f32[256,128]{1,0:T(8,128)S(1)}, u32[]{:S(2)}, u32[]{:S(2)}) collective-permute-start(f32[256,128]{1,0:T(8,128)S(1)} %collective-permute-done.1), channel_id=1, source_target_pairs={{0,14},{2,0},{4,2},{6,4},{8,6},{10,8},{12,10},{14,12},{1,15},{3,1}... | collective-permute-start | bytes 393224 | tf_op jit(solution)/shard_map/ppermute | solution.py:253
  35.6 10.1 %collective-permute-start.5 = (f32[256,128]{1,0:T(8,128)S(1)}, f32[256,128]{1,0:T(8,128)S(1)}, u32[]{:S(2)}, u32[]{:S(2)}) collective-permute-start(f32[256,128]{1,0:T(8,128)S(1)} %collective-permute-done), channel_id=1, source_target_pairs={{0,4},{2,6},{4,8},{6,10},{8,12},{10,14},{12,0},{14,2},{1,5},{3,7},... | collective-permute-start | bytes 393224 | tf_op jit(solution)/shard_map/ppermute | solution.py:253
  37.0 10.6 %collective-permute-start.6 = (f32[256,128]{1,0:T(8,128)S(1)}, f32[256,128]{1,0:T(8,128)S(1)}, u32[]{:S(2)}, u32[]{:S(2)}) collective-permute-start(f32[256,128]{1,0:T(8,128)S(1)} %collective-permute-done.1), channel_id=1, source_target_pairs={{0,12},{2,14},{4,0},{6,2},{8,4},{10,6},{12,8},{14,10},{1,13},{3,15... | collective-permute-start | bytes 393224 | tf_op jit(solution)/shard_map/ppermute | solution.py:253
  67.4 9.4 %collective-permute-start.18 = (f32[256,128]{1,0:T(8,128)}, f32[256,128]{1,0:T(8,128)S(1)}, u32[]{:S(2)}, u32[]{:S(2)}) collective-permute-start(f32[256,128]{1,0:T(8,128)} %get-tuple-element.12), channel_id=1, source_target_pairs={{0,14},{2,0},{4,2},{6,4},{8,6},{10,8},{12,10},{14,12},{1,15},{3,1}... | collective-permute-start | bytes 393224 | tf_op jit(solution)/shard_map/ppermute | solution.py:253
  68.7 14.7 %collective-permute-start.19 = (f32[256,128]{1,0:T(8,128)}, f32[256,128]{1,0:T(8,128)S(1)}, u32[]{:S(2)}, u32[]{:S(2)}) collective-permute-start(f32[256,128]{1,0:T(8,128)} %get-tuple-element.12), channel_id=1, source_target_pairs={{0,8},{2,10},{4,12},{6,14},{8,0},{10,2},{12,4},{14,6},{1,9},{3,11}... | collective-permute-start | bytes 393224 | tf_op jit(solution)/shard_map/ppermute | solution.py:253
  72.4 14.8 %collective-permute-start.20 = (f32[256,128]{1,0:T(8,128)S(1)}, f32[256,128]{1,0:T(8,128)S(1)}, u32[]{:S(2)}, u32[]{:S(2)}) collective-permute-start(f32[256,128]{1,0:T(8,128)S(1)} %collective-permute-done.17), channel_id=1, source_target_pairs={{0,2},{2,4},{4,6},{6,8},{8,10},{10,12},{12,14},{14,0},{1,3},{3,5},... | collective-permute-start | bytes 393224 | tf_op jit(solution)/shard_map/ppermute | solution.py:253
  73.1 50.1 %all-to-all-start.4 = ((f32[16,64,128]{2,1,0:T(8,128)}), f32[16,64,128]{2,1,0:T(8,128)S(1)}, u32[]{:S(2)}, u32[]{:S(2)}) async-start(f32[16,64,128]{2,1,0:T(8,128)} %bitcast.60), calls=%async_computation.4 | async-start | bytes 1048576 | tf_op jit(solution)/shard_map/all_to_all | solution.py:272
  76.9 10.5 %collective-permute-start.21 = (f32[256,128]{1,0:T(8,128)S(1)}, f32[256,128]{1,0:T(8,128)S(1)}, u32[]{:S(2)}, u32[]{:S(2)}) collective-permute-start(f32[256,128]{1,0:T(8,128)S(1)} %collective-permute-done.18), channel_id=1, source_target_pairs={{0,14},{2,0},{4,2},{6,4},{8,6},{10,8},{12,10},{14,12},{1,15},{3,1}... | collective-permute-start | bytes 393224 | tf_op jit(solution)/shard_map/ppermute | solution.py:253
  79.6 12.0 %collective-permute-start.23 = (f32[256,128]{1,0:T(8,128)S(1)}, f32[256,128]{1,0:T(8,128)S(1)}, u32[]{:S(2)}, u32[]{:S(2)}) collective-permute-start(f32[256,128]{1,0:T(8,128)S(1)} %collective-permute-done.18), channel_id=1, source_target_pairs={{0,12},{2,14},{4,0},{6,2},{8,4},{10,6},{12,8},{14,10},{1,13},{3,15... | collective-permute-start | bytes 393224 | tf_op jit(solution)/shard_map/ppermute | solution.py:253
  87.3 13.8 %collective-permute-start.26 = (f32[256,128]{1,0:T(8,128)S(1)}, f32[256,128]{1,0:T(8,128)S(1)}, u32[]{:S(2)}, u32[]{:S(2)}) collective-permute-start(f32[256,128]{1,0:T(8,128)S(1)} %collective-permute-done.19), channel_id=1, source_target_pairs={{0,1},{1,0},{2,3},{3,2},{4,5},{5,4},{6,7},{7,6},{8,9},{9,8},{10,11... | collective-permute-start | bytes 393224 | tf_op jit(solution)/shard_map/ppermute | solution.py:249
  88.2 12.9 %collective-permute-start.27 = (f32[256,128]{1,0:T(8,128)S(1)}, f32[256,128]{1,0:T(8,128)S(1)}, u32[]{:S(2)}, u32[]{:S(2)}) collective-permute-start(f32[256,128]{1,0:T(8,128)S(1)} %collective-permute-done.20), channel_id=1, source_target_pairs={{0,1},{1,0},{2,3},{3,2},{4,5},{5,4},{6,7},{7,6},{8,9},{9,8},{10,11... | collective-permute-start | bytes 393224 | tf_op jit(solution)/shard_map/ppermute | solution.py:249
  91.5 9.6 %collective-permute-start.28 = (f32[256,128]{1,0:T(8,128)S(1)}, f32[256,128]{1,0:T(8,128)S(1)}, u32[]{:S(2)}, u32[]{:S(2)}) collective-permute-start(f32[256,128]{1,0:T(8,128)S(1)} %collective-permute-done.21), channel_id=1, source_target_pairs={{0,1},{1,0},{2,3},{3,2},{4,5},{5,4},{6,7},{7,6},{8,9},{9,8},{10,11... | collective-permute-start | bytes 393224 | tf_op jit(solution)/shard_map/ppermute | solution.py:249
  91.7 9.5 %collective-permute-start.29 = (f32[256,128]{1,0:T(8,128)S(1)}, f32[256,128]{1,0:T(8,128)S(1)}, u32[]{:S(2)}, u32[]{:S(2)}) collective-permute-start(f32[256,128]{1,0:T(8,128)S(1)} %collective-permute-done.22), channel_id=1, source_target_pairs={{0,1},{1,0},{2,3},{3,2},{4,5},{5,4},{6,7},{7,6},{8,9},{9,8},{10,11... | collective-permute-start | bytes 393224 | tf_op jit(solution)/shard_map/ppermute | solution.py:249
  123.2 15.7 %all-to-all-start.1 = ((f32[16,24,128]{2,1,0:T(8,128)}), f32[16,24,128]{2,1,0:T(8,128)S(1)}, u32[]{:S(2)}, u32[]{:S(2)}) async-start(f32[16,24,128]{2,1,0:T(8,128)} %bitcast.40), calls=%async_computation.1 | async-start | bytes 393216 | tf_op jit(solution)/shard_map/all_to_all | solution.py:272
  131.9 38.2 %collective-permute-start.34 = (f32[16,64,128]{2,1,0:T(8,128)S(1)}, f32[16,64,128]{2,1,0:T(8,128)S(1)}, u32[]{:S(2)}, u32[]{:S(2)}) collective-permute-start(f32[16,64,128]{2,1,0:T(8,128)S(1)} %all-to-all-done.4.mine), channel_id=1, source_target_pairs={{0,1},{1,0},{2,3},{3,2},{4,5},{5,4},{6,7},{7,6},{8,9},{9,8},{10,11... | collective-permute-start | bytes 1572872 | tf_op jit(solution)/shard_map/ppermute | solution.py:249
  153.5 10.7 %all-to-all-start.3 = ((f32[16,24,128]{2,1,0:T(8,128)}), f32[16,24,128]{2,1,0:T(8,128)S(1)}, u32[]{:S(2)}, u32[]{:S(2)}) async-start(f32[16,24,128]{2,1,0:T(8,128)} %broadcast_in_dim.5), calls=%async_computation.3 | async-start | bytes 393216 | tf_op jit(solution)/shard_map/all_to_all | solution.py:272
  157.3 11.1 %collective-permute-start.31 = (f32[256,256]{1,0:T(8,128)}, f32[256,256]{1,0:T(8,128)S(1)}, u32[]{:S(2)}, u32[]{:S(2)}) collective-permute-start(f32[256,256]{1,0:T(8,128)} %get-tuple-element.14), channel_id=1, source_target_pairs={{0,1},{1,0},{2,3},{3,2},{4,5},{5,4},{6,7},{7,6},{8,9},{9,8},{10,11... | collective-permute-start | bytes 786440 | tf_op jit(solution)/shard_map/ppermute | solution.py:249
  164.2 10.2 %collective-permute-start.33 = (f32[384,128]{1,0:T(8,128)S(1)}, f32[384,128]{1,0:T(8,128)S(1)}, u32[]{:S(2)}, u32[]{:S(2)}) collective-permute-start(f32[384,128]{1,0:T(8,128)S(1)} %bitcast.57), channel_id=1, source_target_pairs={{0,1},{1,0},{2,3},{3,2},{4,5},{5,4},{6,7},{7,6},{8,9},{9,8},{10,11... | collective-permute-start | bytes 589832 | tf_op jit(solution)/shard_map/ppermute | solution.py:249
  (50 other events, 374.0 us)

commit v2 on v1

v2 whole, which is shorter than its diff:
```python
import jax
import jax.numpy as jnp
from jax import lax
from jax.experimental import pallas as pl
from jax.experimental.pallas import tpu as pltpu
from jax.sharding import PartitionSpec as P

f32 = jnp.float32
bf16 = jnp.bfloat16
TILE = 128
HALF = 64
N_DOM, N_ROW, N_REP = 16, 8, 2
OWN = 32
COLS = 48
SLOTS = 64
GROUP = 8
NN = (((1,), (0,)), ((), ()))
TN = (((0,), (0,)), ((), ()))
NT = (((1,), (1,)), ((), ()))
VMEM_LIMIT = 56 * 1024 * 1024


def split2(x):
    hi = x.astype(bf16)
    lo = (x - hi.astype(f32)).astype(bf16)
    return hi, lo


def split3(x):
    hi = x.astype(bf16)
    rest = x - hi.astype(f32)
    mid = rest.astype(bf16)
    lo = (rest - mid.astype(f32)).astype(bf16)
    return hi, mid, lo


def mm(a, b, dims):
    return lax.dot_general(a, b, dims, preferred_element_type=f32)


def dot3(a, b, dims):
    a_hi, a_lo = split2(a)
    b_hi, b_lo = split2(b)
    return mm(a_hi, b_hi, dims) + (mm(a_hi, b_lo, dims) + mm(a_lo, b_hi, dims))


def pick_rows(q, panel, idx_ref, out_ref):
    rhs = jnp.concatenate(split3(panel), axis=1)
    lane = lax.broadcasted_iota(jnp.int32, (TILE, TILE), 1).astype(f32)
    for b in range(N_DOM // 2):
        cols = []
        for p in (2 * b, 2 * b + 1):
            col = jnp.broadcast_to(idx_ref[p : p + 1, :].astype(f32), (TILE, TILE)).T
            cols.append(jnp.where(q == 0, col[:HALF], col[HALF:]))
        col = jnp.concatenate(cols, axis=0)
        marks = [
            jnp.where(col == lane + float(k * TILE), 1.0, 0.0).astype(bf16)
            for k in range(panel.shape[0] // TILE)
        ]
        got = mm(jnp.concatenate(marks, axis=1), rhs, NN)
        out_ref[pl.ds(b * TILE, TILE), :] = (
            got[:, :TILE] + got[:, TILE : 2 * TILE]
        ) + got[:, 2 * TILE :]


def pick_features_kernel(place, mine, other, idx_ref, out_ref):
    q = place[0]
    a, b = mine[...], other[...]
    panel = jnp.concatenate([jnp.where(q == 0, a, b), jnp.where(q == 0, b, a)], axis=0)
    pick_rows(q, panel, idx_ref, out_ref)


def pick_agg_kernel(place, mine, other, idx_ref, panel_ref, out_ref):
    q = place[0]
    panel = mine[...] + other[...]
    size = panel.shape[0] // 2
    panel_ref[:size, :] = jnp.where(q == 0, panel[:size], panel[size:])
    panel_ref[size:, :] = jnp.where(q == 0, panel[size:], panel[:size])
    pick_rows(q, panel, idx_ref, out_ref)


def tile_copies(tiles_hbm, tiles, sems):
    return [
        pltpu.make_async_copy(
            tiles_hbm.at[pl.ds(k * GROUP, GROUP)], tiles.at[pl.ds(k * GROUP, GROUP)], sems.at[k]
        )
        for k in range(SLOTS // GROUP)
    ]


def each_tile(count_s, tiles_hbm, tiles, sems, one_tile):
    count = count_s[0, 0]

    def body(g, carry):
        part = pl.ds(g * GROUP, GROUP)
        pltpu.make_async_copy(tiles_hbm.at[part], tiles.at[part], sems.at[g]).wait()

        @pl.when(g * GROUP < count)
        def _():
            for i in range(GROUP):
                t = g * GROUP + i
                live = jnp.where(t < count, 1.0, 0.0).astype(f32)
                one_tile(t, tiles[t] * live)

        return carry

    lax.fori_loop(0, SLOTS // GROUP, body, 0)


def backward_kernel(rows_s, cols_s, count_s, cot, w2, tiles_hbm, out, u_scr, tiles, sems):
    for c in tile_copies(tiles_hbm, tiles, sems):
        c.start()
    out[...] = jnp.zeros_like(out)
    for b in range(4):
        hi, lo = split2(dot3(cot[pl.ds(b * TILE, TILE), :], w2[...], NT))
        u_scr[b, :TILE, :] = hi
        u_scr[b, TILE:, :] = lo

    def one_tile(t, a):
        a_hi, a_lo = split2(a)
        u = u_scr[rows_s[0, t]]
        term = mm(jnp.concatenate([a_hi, a_hi], axis=0), u, TN) + mm(a_lo, u[:TILE], TN)
        out[jnp.minimum(cols_s[0, t], OWN)] += term

    each_tile(count_s, tiles_hbm, tiles, sems, one_tile)


def forward_tiles(rows_s, cols_s, count_s, tiles_hbm, tiles, sems, x_scr, acc):
    def one_tile(t, a):
        a_hi, a_lo = split2(a)
        x = x_scr[cols_s[0, t]]
        term = mm(jnp.concatenate([a_hi, a_hi], axis=1), x, NN) + mm(a_lo, x[:TILE], NN)
        acc[rows_s[0, t]] += term

    each_tile(count_s, tiles_hbm, tiles, sems, one_tile)


def piece_copies(place, own, mine, theirs, dst, sems):
    q, r = place[0], place[1]
    side = 1 - 2 * q
    parts = [(own[0], r, q), (own[1], r, 1 - q)]
    for refs, way, half in ((mine, side, q), (theirs, -side, 1 - q)):
        for s in (1, 2, 3):
            row = lax.rem(r + N_ROW - way * s, N_ROW)
            parts.append((refs[s - 1].at[pl.ds(0, 2)], row, half))
            parts.append((refs[s - 1].at[pl.ds(2, 2)], row, 1 - half))
        parts.append((refs[3], lax.rem(r + 4, N_ROW), half))
    return [
        pltpu.make_async_copy(ref, dst.at[pl.ds(row * 4 + half * 2, 2)], sems.at[k])
        for k, (ref, row, half) in enumerate(parts)
    ]


def pass_one_kernel(place, rows_s, cols_s, count_s, *refs):
    own, other, mine, theirs = refs[0], refs[1], refs[2:6], refs[6:10]
    halo_mine, halo_theirs, tiles_hbm, acc, xf, x_scr, tiles, sems, tile_sems = refs[10:]
    q = place[0]
    copies = piece_copies(place, (own, other), mine, theirs, xf, sems)
    for m, (ref, half) in enumerate(((halo_mine, q), (halo_theirs, 1 - q))):
        at = pl.multiple_of(half * HALF, HALF)
        copies.append(
            pltpu.make_async_copy(
                ref, xf.at[pl.ds(OWN, N_DOM), pl.ds(at, HALF), :], sems.at[16 + m]
            )
        )
    for c in copies + tile_copies(tiles_hbm, tiles, tile_sems):
        c.start()
    acc[...] = jnp.zeros_like(acc)
    for c in copies:
        c.wait()

    def body(j, carry):
        for k in range(4):
            hi, lo = split2(xf[j * 4 + k])
            x_scr[j * 4 + k, :TILE, :] = hi
            x_scr[j * 4 + k, TILE:, :] = lo
        return carry

    lax.fori_loop(0, COLS // 4, body, 0)
    forward_tiles(rows_s, cols_s, count_s, tiles_hbm, tiles, tile_sems, x_scr, acc)


def layer_two_kernel(place, rows_s, cols_s, count_s, *refs):
    own, mine, theirs = refs[0], refs[1:5], refs[5:9]
    (w1, w2, cot, hist_hbm, c_hbm, tiles_hbm) = refs[9:15]
    (g_keep, g_send, p_keep, p_send) = refs[15:19]
    (xf, h_scr, acc, g_one, hist, c_terms, tiles, sems, tile_sems, c_sems) = refs[19:]
    q = place[0]

    def c_copy(g):
        part = pl.ds(g * 4, 4)
        return pltpu.make_async_copy(c_hbm.at[part], c_terms.at[part], c_sems.at[g])

    copies = piece_copies(place, (own.at[pl.ds(0, 2)], own.at[pl.ds(2, 2)]), mine, theirs, xf, sems)
    hist_copy = pltpu.make_async_copy(hist_hbm, hist, sems.at[16])
    for c in copies:
        c.start()
    for g in range(N_ROW):
        c_copy(g).start()
    hist_copy.start()
    for c in tile_copies(tiles_hbm, tiles, tile_sems):
        c.start()
    acc[...] = jnp.zeros_like(acc)
    g_one[...] = jnp.zeros_like(g_one)
    for c in copies:
        c.wait()

    def panel_step(g, carry):
        c_copy(g).wait()
        w_hi, w_lo = split2(w1[...])
        total = jnp.zeros((TILE, w1.shape[1]), f32)
        for b in range(4):
            x = xf[g * 4 + b]
            x_hi, x_lo = split2(x)
            pre = mm(x_hi, w_hi, NN) + (mm(x_hi, w_lo, NN) + mm(x_lo, w_hi, NN))
            sig = 1.0 / (1.0 + jnp.exp(-pre))
            hi, lo = split2(pre * sig)
            h_scr[g * 4 + b, :TILE, :] = hi
            h_scr[g * 4 + b, TILE:, :] = lo
            grad = c_terms[g * 4 + b] * (sig * (1.0 + pre * (1.0 - sig)))
            total += dot3(x, grad, TN)
        g_one[...] += total
        return carry

    lax.fori_loop(0, N_ROW, panel_step, 0)
    hist_copy.wait()

    def hist_step(g, carry):
        for b in range(2):
            hi, lo = split2(hist[g * 2 + b])
            h_scr[OWN + g * 2 + b, :TILE, :] = hi
            h_scr[OWN + g * 2 + b, TILE:, :] = lo
        return carry

    lax.fori_loop(0, N_DOM // 2, hist_step, 0)
    forward_tiles(rows_s, cols_s, count_s, tiles_hbm, tiles, tile_sems, h_scr, acc)

    agg = acc[...].reshape(4 * TILE, -1)
    g_two = dot3(agg, cot[...], TN)
    left = jnp.concatenate([g_one[:, :TILE], g_two[:, :TILE]], axis=0)
    right = jnp.concatenate([g_one[:, TILE:], g_two[:, TILE:]], axis=0)
    g_keep[...] = jnp.where(q == 0, left, right)
    g_send[...] = jnp.where(q == 0, right, left)
    prod = dot3(agg, w2[...], NN)
    low, high = prod[: 2 * TILE], prod[2 * TILE :]
    p_keep[...] = jnp.where(q == 0, low, high)
    p_send[...] = jnp.where(q == 0, high, low)


def fresh_kernel(place, mine, theirs, w1, out):
    q = place[0]
    w_hi, w_lo = split2(w1[...])
    for s in range(mine.shape[0]):
        a, b = mine[s], theirs[s]
        x = jnp.concatenate([jnp.where(q == 0, a, b), jnp.where(q == 0, b, a)], axis=0)
        x_hi, x_lo = split2(x)
        pre = mm(x_hi, w_hi, NN) + (mm(x_hi, w_lo, NN) + mm(x_lo, w_hi, NN))
        out[pl.ds(s * TILE, TILE), :] = pre / (1.0 + jnp.exp(-pre))


SMEM = pl.BlockSpec(memory_space=pltpu.SMEM)
VMEM = pl.BlockSpec(memory_space=pltpu.VMEM)
ANY = pl.BlockSpec(memory_space=pl.ANY)


def params():
    return pltpu.CompilerParams(vmem_limit_bytes=VMEM_LIMIT)


def cost(flops, moved):
    return pl.CostEstimate(flops=flops, bytes_accessed=moved, transcendentals=0)


def swap(x):
    return lax.ppermute(x, "rep", [(0, 1), (1, 0)])


def along(x, k):
    pairs = []
    for row in range(N_ROW):
        for core in range(N_REP):
            to = row - k if core else row + k
            pairs.append((row * N_REP + core, to % N_ROW * N_REP + core))
    return lax.ppermute(x, ("row", "rep"), pairs)


def together(*xs):
    return lax.optimization_barrier(xs)


def blocks(x):
    return x.reshape(-1, TILE, x.shape[-1])


def to_all(x):
    return lax.all_to_all(x, "dom", split_axis=0, concat_axis=0, tiled=True)


def local(
    features,
    send_rows,
    tile_values,
    tile_rows,
    tile_cols,
    tile_counts,
    history,
    weight_one,
    weight_two,
    cotangent,
):
    f_dim, h_dim = weight_one.shape
    half_rows = features.shape[0]
    tiles = tile_values.reshape(SLOTS, TILE, TILE)
    rows_s = tile_rows.reshape(1, SLOTS)
    cols_s = tile_cols.reshape(1, SLOTS)
    count_s = tile_counts.reshape(1, 1)
    idx = send_rows.reshape(N_DOM, TILE)
    q = lax.axis_index("rep")
    place = jnp.stack([q, lax.axis_index("row")]).astype(jnp.int32)
    tile_scr = [pltpu.VMEM((SLOTS, TILE, TILE), f32)]
    tile_sems = [pltpu.SemaphoreType.DMA((SLOTS // GROUP,))]

    def backward(count_s):
        return pl.pallas_call(
            backward_kernel,
            name="backward",
            out_shape=jax.ShapeDtypeStruct((OWN + 1, TILE, h_dim), f32),
            in_specs=[SMEM, SMEM, SMEM, VMEM, VMEM, ANY],
            out_specs=VMEM,
            scratch_shapes=[pltpu.VMEM((4, 2 * TILE, h_dim), bf16)] + tile_scr + tile_sems,
            compiler_params=params(),
            cost_estimate=cost(6 * SLOTS * TILE * TILE * h_dim, 9 << 20),
        )(rows_s, cols_s, count_s, cotangent, weight_two, tiles)

    other = swap(features)
    first, second = along(features, 1), along(other, 1)
    outgoing = pl.pallas_call(
        pick_features_kernel,
        name="pick_features",
        out_shape=jax.ShapeDtypeStruct((N_DOM * HALF, f_dim), f32),
        in_specs=[SMEM, VMEM, VMEM, VMEM],
        out_specs=VMEM,
        compiler_params=params(),
        cost_estimate=cost(1 << 20, 1 << 20),
    )(place, features, other, idx)
    first, second, outgoing = together(first, second, outgoing)
    one = jnp.concatenate([first, second])
    halo_mine = to_all(outgoing.reshape(N_DOM, HALF, f_dim))
    two, three, four, theirs_one = together(
        along(one, 1),
        along(one, 2),
        along(first, 3),
        swap(one),
    )
    mine = [one, two, three, four]
    theirs = [theirs_one, swap(two), swap(three), swap(four)]
    halo_mine, *theirs = together(halo_mine, *theirs)
    halo_theirs = swap(halo_mine)

    part_one = pl.pallas_call(
        pass_one_kernel,
        name="pass_one",
        out_shape=jax.ShapeDtypeStruct((4, TILE, f_dim), f32),
        in_specs=[SMEM] * 4 + [ANY] * 13,
        out_specs=VMEM,
        scratch_shapes=[
            pltpu.VMEM((COLS, TILE, f_dim), f32),
            pltpu.VMEM((COLS, 2 * TILE, f_dim), bf16),
        ]
        + tile_scr
        + [pltpu.SemaphoreType.DMA((18,))]
        + tile_sems,
        compiler_params=params(),
    )(
        place,
        rows_s,
        cols_s,
        count_s,
        *[blocks(x) for x in [features, other] + mine + theirs],
        halo_mine,
        halo_theirs,
        tiles,
    ).reshape(4 * TILE, f_dim)

    panel, outgoing_two = pl.pallas_call(
        pick_agg_kernel,
        name="pick_agg",
        out_shape=(
            jax.ShapeDtypeStruct((4 * TILE, f_dim), f32),
            jax.ShapeDtypeStruct((N_DOM * HALF, f_dim), f32),
        ),
        in_specs=[SMEM, VMEM, VMEM, VMEM],
        out_specs=(VMEM, VMEM),
        compiler_params=params(),
    )(place, part_one, swap(part_one), idx)
    fresh_mine = to_all(outgoing_two.reshape(N_DOM, HALF, f_dim))
    one, count_b = together(along(panel, 1), count_s)
    c_terms = backward(count_b)
    two, three, four, theirs_one, c_terms = together(
        along(one, 1),
        along(one, 2),
        along(one[:half_rows], 3),
        swap(one),
        c_terms,
    )
    agg_mine = [one, two, three, four]
    agg_theirs = [theirs_one, swap(two), swap(three), swap(four)]
    fresh_mine, *agg_theirs = together(fresh_mine, *agg_theirs)
    g_keep, g_send, p_keep, p_send = pl.pallas_call(
        layer_two_kernel,
        name="layer_two",
        out_shape=(
            jax.ShapeDtypeStruct((f_dim + h_dim, TILE), f32),
            jax.ShapeDtypeStruct((f_dim + h_dim, TILE), f32),
            jax.ShapeDtypeStruct((2 * TILE, h_dim), f32),
            jax.ShapeDtypeStruct((2 * TILE, h_dim), f32),
        ),
        in_specs=[SMEM] * 4 + [ANY] * 9 + [VMEM] * 3 + [ANY] * 3,
        out_specs=(VMEM, VMEM, VMEM, VMEM),
        scratch_shapes=[
            pltpu.VMEM((OWN, TILE, f_dim), f32),
            pltpu.VMEM((COLS, 2 * TILE, h_dim), bf16),
            pltpu.VMEM((4, TILE, h_dim), f32),
            pltpu.VMEM((f_dim, h_dim), f32),
            pltpu.VMEM((N_DOM, TILE, h_dim), f32),
            pltpu.VMEM((OWN, TILE, h_dim), f32),
        ]
        + tile_scr
        + [pltpu.SemaphoreType.DMA((18,))]
        + tile_sems
        + [pltpu.SemaphoreType.DMA((N_ROW,))],
        compiler_params=params(),
        cost_estimate=cost(8 << 30, 16 << 20),
    )(
        place,
        rows_s,
        cols_s,
        count_s,
        *[blocks(x) for x in [panel] + agg_mine + agg_theirs],
        weight_one,
        weight_two,
        cotangent,
        blocks(history),
        c_terms,
        tiles,
    )

    fresh_mine, g_keep = together(fresh_mine, g_keep)
    fresh_theirs = swap(fresh_mine)
    output = p_keep + swap(p_send)
    fresh = pl.pallas_call(
        fresh_kernel,
        name="fresh",
        out_shape=jax.ShapeDtypeStruct((N_DOM * TILE, h_dim), f32),
        in_specs=[SMEM, VMEM, VMEM, VMEM],
        out_specs=VMEM,
        compiler_params=params(),
        cost_estimate=cost(6 * N_DOM * TILE * f_dim * h_dim, 4 << 20),
    )(place, fresh_mine, fresh_theirs, weight_one)
    part = to_all((g_keep + swap(g_send)).reshape(N_DOM, -1, TILE))
    part = jnp.sum(part, axis=0)
    part = jnp.broadcast_to(part[None], (N_ROW,) + part.shape)
    part = lax.all_to_all(part, "row", split_axis=0, concat_axis=0, tiled=True)
    part, fresh = together(part, fresh)
    part = jnp.sum(part, axis=0)
    part = jnp.broadcast_to(part[None], (N_DOM,) + part.shape)
    mine_g, output = together(to_all(part).reshape(-1, TILE), output)
    theirs_g = swap(mine_g)
    low = jnp.where(q == 0, mine_g, theirs_g)
    high = jnp.where(q == 0, theirs_g, mine_g)
    grads = jnp.concatenate([low, high], axis=1)
    return (output, grads[:f_dim], grads[f_dim:], fresh)


def solution(mesh):
    return jax.shard_map(
        local,
        mesh=mesh,
        in_specs=(
            P(("dom", "row", "rep"), None),
            P("dom", "row", None, None),
            P("dom", "row", "rep", None, None),
            P("dom", "row", "rep"),
            P("dom", "row", "rep"),
            P("dom", "row", "rep"),
            P(("dom", "row"), None),
            P(),
            P(),
            P(("dom", "row"), None),
        ),
        out_specs=(P(("dom", "row", "rep"), None), P(), P(), P(("dom", "row"), None)),
        check_vma=False,
    )
```

time: 176 us -> 146 us (0.83)
  starting transfers between devices: 84.4 us -> 61.9 us
  Pallas kernels: 43.5 us -> 34.6 us
  waiting for transfers between devices: 21.8 us -> 23.6 us
    ppermute x14 -> x9, starting transfers between devices: 35.5 us -> 15 us  [along(): return lax.ppermute(x, ('row', 'rep'), pairs)]
    pallas_call x3, Pallas kernels: 34.8 us -> 25.8 us  [the longest x1 14.4 us: local(): pl.pallas_call(layer_two_kernel, name='layer_two', out_shape=(jax.ShapeDt...]
    all_to_all x4 -> x3, waiting for transfers between devices: 14.9 us -> 7.51 us  [to_all(): return lax.all_to_all(x, 'dom', split_axis=0, concat_axis=0, tiled=True)]
    ppermute x14 -> x9, waiting for transfers between devices: 3.26 us -> 8.41 us  [along(): return lax.ppermute(x, ('row', 'rep'), pairs)]
    all_to_all x0 -> x1, starting transfers between devices: none -> 5.07 us  [local(): part = lax.all_to_all(part, 'row', split_axis=0, concat_axis=0, tiled=True)]
    ppermute x21 -> x15, starting transfers between devices: 27.7 us -> 23.4 us  [swap(): return lax.ppermute(x, 'rep', [(0, 1), (1, 0)])]
    ppermute x21 -> x15, waiting for transfers between devices: 3.65 us -> 6.5 us  [swap(): return lax.ppermute(x, 'rep', [(0, 1), (1, 0)])]
    all_to_all x4 -> x3, starting transfers between devices: 21.2 us -> 18.5 us  [to_all(): return lax.all_to_all(x, 'dom', split_axis=0, concat_axis=0, tiled=True)]
  transfers between devices with their start and end apart: 39 -> 28, of which waited for: 10 -> 11; matrix products, arithmetic and copies ran while one was open for 3% -> 3% of each run, Pallas kernels for 17% -> 8%
where the time goes in v2:
time: 146 us; the launch traced here: 145 us
  starting transfers between devices  61.9 us (42%)
  Pallas kernels  34.6 us (24%)
  waiting for transfers between devices  23.6 us (16%)
  blocking collectives  15 us (10%)
  local copies, waits for them, and re-layouts  4.47 us (3%)
  other arithmetic  3.74 us (3%)
  between operations  1.64 us (1%)
    ppermute x15, starting transfers between devices, swap(): return lax.ppermute(x, 'rep', [(0, 1), (1, 0)])  23.4 us
    all_to_all x3, starting transfers between devices, to_all(): return lax.all_to_all(x, 'dom', split_axis=0, concat_axis=0, tiled=True)  18.5 us
    all_to_all x1, blocking collectives, to_all(): return lax.all_to_all(x, 'dom', split_axis=0, concat_axis=0, tiled=True)  15 us
    ppermute x9, starting transfers between devices, along(): return lax.ppermute(x, ('row', 'rep'), pairs)  15 us
    pallas_call x1, Pallas kernels, local(): pl.pallas_call(layer_two_kernel, name='layer_two', out_shape=(jax.ShapeDt...  14.4 us
    ppermute x9, waiting for transfers between devices, along(): return lax.ppermute(x, ('row', 'rep'), pairs)  8.41 us
    all_to_all x3, waiting for transfers between devices, to_all(): return lax.all_to_all(x, 'dom', split_axis=0, concat_axis=0, tiled=True)  7.51 us
    ppermute x15, waiting for transfers between devices, swap(): return lax.ppermute(x, 'rep', [(0, 1), (1, 0)])  6.5 us
  transfers between devices with their start and end apart: 28, of which 11 were waited for; matrix products, arithmetic and copies ran while one was open for 3% of the time, Pallas kernels for 8%

profile of v2, /device:TPU:1, one launch (start us, length us, event | category | flops | bytes accessed | tf_op | source)
XLA Modules:
  0.0 144.9 jit_solution(6201112034899345868)
XLA Ops:
  0.6 3.3 %collective-permute-start = (f32[256,128]{1,0:T(8,128)}, f32[256,128]{1,0:T(8,128)S(1)}, u32[]{:S(2)}, u32[]{:S(2)}) collective-permute-start(f32[256,128]{1,0:T(8,128)} %mine.1), channel_id=1, source_target_pairs={{0,1},{1,0},{2,3},{3,2},{4,5},{5,4},{6,7},{7,6},{8,9},{9,8},{10,11... | collective-permute-start | bytes 393224 | tf_op jit(solution)/shard_map/ppermute | solution.py:275
  4.0 3.8 %collective-permute-start.1 = (f32[256,128]{1,0:T(8,128)}, f32[256,128]{1,0:T(8,128)S(1)}, u32[]{:S(2)}, u32[]{:S(2)}) collective-permute-start(f32[256,128]{1,0:T(8,128)} %mine.1), channel_id=1, source_target_pairs={{0,2},{1,15},{2,4},{3,1},{4,6},{5,3},{6,8},{7,5},{8,10},{9,7},{10,... | collective-permute-start | bytes 393224 | tf_op jit(solution)/shard_map/ppermute | solution.py:284
  9.6 2.6 %pick_features.1 = f32[1024,128]{1,0:T(8,128)} custom-call(s32[2]{0:T(128)} %pad_add_fusion.place, f32[256,128]{1,0:T(8,128)} %mine.1, f32[256,128]{1,0:T(8,128)} %copy-done.3, s32[16,128]{1,0:T(8,128)} %bitcast.56), custom_call_target="tpu_custom_call" | custom-call | flops 1048576 | bytes 1048576 | tf_op jit(solution)/shard_map/pick_features/pallas_call | solution.py:337
  12.9 2.2 %collective-permute-start.4 = (f32[512,128]{1,0:T(8,128)S(1)}, f32[512,128]{1,0:T(8,128)S(1)}, u32[]{:S(2)}, u32[]{:S(2)}) collective-permute-start(f32[512,128]{1,0:T(8,128)S(1)} %constant_dynamic-update-slice_fusion), channel_id=1, source_target_pairs={{0,4},{1,13},{2,6},{3,15},{4,8},{5,1},{6,10},{7,3},{8,12},{9,5},{1... | collective-permute-start | bytes 786440 | tf_op jit(solution)/shard_map/ppermute | solution.py:284
  15.8 6.8 %all-to-all-start = ((f32[16,64,128]{2,1,0:T(8,128)}), f32[16,64,128]{2,1,0:T(8,128)S(1)}, u32[]{:S(2)}, u32[]{:S(2)}) async-start(f32[16,64,128]{2,1,0:T(8,128)} %bitcast.38), calls=%async_computation | async-start | bytes 1048576 | tf_op jit(solution)/shard_map/all_to_all | solution.py:296
  22.5 1.7 %collective-permute-start.5 = (f32[256,128]{1,0:T(8,128)S(1)}, f32[256,128]{1,0:T(8,128)S(1)}, u32[]{:S(2)}, u32[]{:S(2)}) collective-permute-start(f32[256,128]{1,0:T(8,128)S(1)} %collective-permute-done.1), channel_id=1, source_target_pairs={{0,6},{1,11},{2,8},{3,13},{4,10},{5,15},{6,12},{7,1},{8,14},{9,3},... | collective-permute-start | bytes 393224 | tf_op jit(solution)/shard_map/ppermute | solution.py:284
  24.3 4.1 %collective-permute-done.5 = f32[256,128]{1,0:T(8,128)S(1)} collective-permute-done((f32[256,128]{1,0:T(8,128)S(1)}, f32[256,128]{1,0:T(8,128)S(1)}, u32[]{:S(2)}, u32[]{:S(2)}) %collective-permute-start.5) | collective-permute-done | bytes 131104 | tf_op jit(solution)/shard_map/ppermute | solution.py:284
  28.4 5.2 %collective-permute-start.7 = (f32[512,128]{1,0:T(8,128)S(1)}, f32[512,128]{1,0:T(8,128)S(1)}, u32[]{:S(2)}, u32[]{:S(2)}) collective-permute-start(f32[512,128]{1,0:T(8,128)S(1)} %collective-permute-done.3), channel_id=1, source_target_pairs={{0,1},{1,0},{2,3},{3,2},{4,5},{5,4},{6,7},{7,6},{8,9},{9,8},{10,11... | collective-permute-start | bytes 786440 | tf_op jit(solution)/shard_map/ppermute | solution.py:275
  38.2 6.0 %pass_one.1 = f32[4,128,128]{2,1,0:T(8,128)} custom-call(s32[2]{0:T(128)} %pad_add_fusion.place, s32[1,64]{1,0:T(1,128)} %bitcast.58, s32[1,64]{1,0:T(1,128)} %bitcast.61, s32[1,1]{1,0:T(1,128)} %bitcast.33.count_s, f32[2,128,128]{2,1,0:T(8,128)} %bitcast.45, f32[2,128,128]{2,1,0:T(8,128)} %bitcast.46, f32[4,128,128]{2,1,0:T(8,128)} %bitcast.44, ...), custom_call_target="tpu_custom_call" | custom-call | tf_op jit(solution)/shard_map/pass_one/pallas_call | solution.py:360
  47.1 2.6 %pick_agg.1 = (f32[512,128]{1,0:T(8,128)}, f32[1024,128]{1,0:T(8,128)}) custom-call(s32[2]{0:T(128)} %pad_add_fusion.place, f32[512,128]{1,0:T(8,128)} %bitcast.40, f32[512,128]{1,0:T(8,128)} %copy-done.12, s32[16,128]{1,0:T(8,128)} %bitcast.57), custom_call_target="tpu_custom_call" | custom-call | tf_op jit(solution)/shard_map/pick_agg/pallas_call | solution.py:385
  51.3 4.2 %collective-permute-done.12 = f32[512,128]{1,0:T(8,128)S(1)} collective-permute-done((f32[512,128]{1,0:T(8,128)}, f32[512,128]{1,0:T(8,128)S(1)}, u32[]{:S(2)}, u32[]{:S(2)}) %collective-permute-start.12) | collective-permute-done | bytes 262176 | tf_op jit(solution)/shard_map/ppermute | solution.py:284
  55.4 2.4 %collective-permute-start.16 = (f32[512,128]{1,0:T(8,128)S(1)}, f32[512,128]{1,0:T(8,128)S(1)}, u32[]{:S(2)}, u32[]{:S(2)}) collective-permute-start(f32[512,128]{1,0:T(8,128)S(1)} %collective-permute-done.12), channel_id=1, source_target_pairs={{0,1},{1,0},{2,3},{3,2},{4,5},{5,4},{6,7},{7,6},{8,9},{9,8},{10,11... | collective-permute-start | bytes 786440 | tf_op jit(solution)/shard_map/ppermute | solution.py:275
  59.2 8.0 %all-to-all-start.1 = ((f32[16,64,128]{2,1,0:T(8,128)}), f32[16,64,128]{2,1,0:T(8,128)S(1)}, u32[]{:S(2)}, u32[]{:S(2)}) async-start(f32[16,64,128]{2,1,0:T(8,128)} %bitcast.47), calls=%async_computation.1 | async-start | bytes 1048576 | tf_op jit(solution)/shard_map/all_to_all | solution.py:296
  67.2 2.3 %collective-permute-start.15 = (f32[256,128]{1,0:T(8,128)S(1)}, f32[256,128]{1,0:T(8,128)S(1)}, u32[]{:S(2)}, u32[]{:S(2)}) collective-permute-start(f32[256,128]{1,0:T(8,128)S(1)} %slice.9), channel_id=1, source_target_pairs={{0,6},{1,11},{2,8},{3,13},{4,10},{5,15},{6,12},{7,1},{8,14},{9,3},... | collective-permute-start | bytes 393224 | tf_op jit(solution)/shard_map/ppermute | solution.py:284
  69.6 5.4 %backward.1.refs_13_ = f32[33,128,256]{2,1,0:T(8,128)} custom-call(s32[1,64]{1,0:T(1,128)} %bitcast.59, s32[1,64]{1,0:T(1,128)} %bitcast.62, s32[1,1]{1,0:T(1,128)} %bitcast.32.count_s, f32[512,256]{1,0:T(8,128)} %refs_11_.1, f32[256,256]{1,0:T(8,128)} %refs_10_.1, f32[64,128,128]{2,1,0:T(8,128)} %bitcast.36), custom_call_target="tpu_custom_call" | custom-call | flops 1610612736 | bytes 9437184 | tf_op jit(solution)/shard_map/backward/pallas_call | solution.py:324
  79.6 14.4 %layer_two.1 = (f32[384,128]{1,0:T(8,128)}, f32[384,128]{1,0:T(8,128)}, f32[256,256]{1,0:T(8,128)}, f32[256,256]{1,0:T(8,128)}) custom-call(s32[2]{0:T(128)} %pad_add_fusion.place, s32[1,64]{1,0:T(1,128)} %bitcast.60, s32[1,64]{1,0:T(1,128)} %bitcast.63, s32[1,1]{1,0:T(1,128)} %bitcast.34.count_s, f32[4,128,128]{2,1,0:T(8,128)} %bitcast.65, ...), custom_call_target="tpu_custom_call" | custom-call | flops 8589934592 | bytes 16777216 | tf_op jit(solution)/shard_map/layer_two/pallas_call | solution.py:409
  95.6 1.9 %collective-permute-done.20 = f32[384,128]{1,0:T(8,128)S(1)} collective-permute-done((f32[384,128]{1,0:T(8,128)}, f32[384,128]{1,0:T(8,128)S(1)}, u32[]{:S(2)}, u32[]{:S(2)}) %collective-permute-start.20) | collective-permute-done | bytes 196640 | tf_op jit(solution)/shard_map/ppermute | solution.py:275
  98.5 15.0 %all_to_all.25 = f32[16,24,128]{2,1,0:T(8,128)S(1)} all-to-all(f32[16,24,128]{2,1,0:T(8,128)S(1)} %bitcast.43), channel_id=1, replica_groups=mesh['dom'=16,'row'=8,'rep'=2] {'dom'}, dimensions={0} | all-to-all | bytes 393216 | tf_op jit(solution)/shard_map/all_to_all | solution.py:296
  114.2 5.1 %all-to-all-start.3 = ((f32[8,24,128]{2,1,0:T(8,128)}), f32[8,24,128]{2,1,0:T(8,128)S(1)}, u32[]{:S(2)}, u32[]{:S(2)}) async-start(f32[8,24,128]{2,1,0:T(8,128)} %broadcast_in_dim.4), calls=%async_computation.3 | async-start | bytes 196608 | tf_op jit(solution)/shard_map/all_to_all | solution.py:463
  119.2 2.1 %collective-permute-start.22 = (f32[256,256]{1,0:T(8,128)}, f32[256,256]{1,0:T(8,128)S(1)}, u32[]{:S(2)}, u32[]{:S(2)}) collective-permute-start(f32[256,256]{1,0:T(8,128)} %get-tuple-element.72), channel_id=1, source_target_pairs={{0,1},{1,0},{2,3},{3,2},{4,5},{5,4},{6,7},{7,6},{8,9},{9,8},{10,11... | collective-permute-start | bytes 786440 | tf_op jit(solution)/shard_map/ppermute | solution.py:275
  122.1 3.6 %fresh.1 = f32[2048,256]{1,0:T(8,128)} custom-call(s32[2]{0:T(128)} %pad_add_fusion.place, f32[16,64,128]{2,1,0:T(8,128)} %copy-done.1, f32[16,64,128]{2,1,0:T(8,128)} %copy-done.5, f32[128,256]{1,0:T(8,128)} %w1.1), custom_call_target="tpu_custom_call" | custom-call | flops 402653184 | bytes 4194304 | tf_op jit(solution)/shard_map/fresh/pallas_call | solution.py:451
  127.6 3.7 %all-to-all-start.4 = ((f32[16,24,128]{2,1,0:T(8,128)}), f32[16,24,128]{2,1,0:T(8,128)S(1)}, u32[]{:S(2)}, u32[]{:S(2)}) async-start(f32[16,24,128]{2,1,0:T(8,128)} %broadcast_in_dim.5), calls=%async_computation.4 | async-start | bytes 393216 | tf_op jit(solution)/shard_map/all_to_all | solution.py:296
  132.1 6.2 %all-to-all-done.4 = f32[16,24,128]{2,1,0:T(8,128)S(1)} async-done(((f32[16,24,128]{2,1,0:T(8,128)}), f32[16,24,128]{2,1,0:T(8,128)S(1)}, u32[]{:S(2)}, u32[]{:S(2)}) %all-to-all-start.4) | async-done | bytes 196640 | tf_op jit(solution)/shard_map/all_to_all | solution.py:296
  138.3 4.1 %collective-permute-start.23 = (f32[384,128]{1,0:T(8,128)S(1)}, f32[384,128]{1,0:T(8,128)S(1)}, u32[]{:S(2)}, u32[]{:S(2)}) collective-permute-start(f32[384,128]{1,0:T(8,128)S(1)} %bitcast.41), channel_id=1, source_target_pairs={{0,1},{1,0},{2,3},{3,2},{4,5},{5,4},{6,7},{7,6},{8,9},{9,8},{10,11... | collective-permute-start | bytes 589832 | tf_op jit(solution)/shard_map/ppermute | solution.py:275
  (98 shorter events, 26.6 us)
Async XLA Ops:
  0.6 7.2 %collective-permute-start = (f32[256,128]{1,0:T(8,128)}, f32[256,128]{1,0:T(8,128)S(1)}, u32[]{:S(2)}, u32[]{:S(2)}) collective-permute-start(f32[256,128]{1,0:T(8,128)} %mine.1), channel_id=1, source_target_pairs={{0,1},{1,0},{2,3},{3,2},{4,5},{5,4},{6,7},{7,6},{8,9},{9,8},{10,11... | collective-permute-start | bytes 393224 | tf_op jit(solution)/shard_map/ppermute | solution.py:275
  4.0 8.2 %collective-permute-start.1 = (f32[256,128]{1,0:T(8,128)}, f32[256,128]{1,0:T(8,128)S(1)}, u32[]{:S(2)}, u32[]{:S(2)}) collective-permute-start(f32[256,128]{1,0:T(8,128)} %mine.1), channel_id=1, source_target_pairs={{0,2},{1,15},{2,4},{3,1},{4,6},{5,3},{6,8},{7,5},{8,10},{9,7},{10,... | collective-permute-start | bytes 393224 | tf_op jit(solution)/shard_map/ppermute | solution.py:284
  7.8 4.4 %collective-permute-start.2 = (f32[256,128]{1,0:T(8,128)S(1)}, f32[256,128]{1,0:T(8,128)S(1)}, u32[]{:S(2)}, u32[]{:S(2)}) collective-permute-start(f32[256,128]{1,0:T(8,128)S(1)} %collective-permute-done.other), channel_id=1, source_target_pairs={{0,2},{1,15},{2,4},{3,1},{4,6},{5,3},{6,8},{7,5},{8,10},{9,7},{10,... | collective-permute-start | bytes 393224 | tf_op jit(solution)/shard_map/ppermute | solution.py:284
  12.2 16.2 %collective-permute-start.6 = (f32[512,128]{1,0:T(8,128)S(1)}, f32[512,128]{1,0:T(8,128)S(1)}, u32[]{:S(2)}, u32[]{:S(2)}) collective-permute-start(f32[512,128]{1,0:T(8,128)S(1)} %constant_dynamic-update-slice_fusion), channel_id=1, source_target_pairs={{0,1},{1,0},{2,3},{3,2},{4,5},{5,4},{6,7},{7,6},{8,9},{9,8},{10,11... | collective-permute-start | bytes 786440 | tf_op jit(solution)/shard_map/ppermute | solution.py:275
  12.9 15.5 %collective-permute-start.4 = (f32[512,128]{1,0:T(8,128)S(1)}, f32[512,128]{1,0:T(8,128)S(1)}, u32[]{:S(2)}, u32[]{:S(2)}) collective-permute-start(f32[512,128]{1,0:T(8,128)S(1)} %constant_dynamic-update-slice_fusion), channel_id=1, source_target_pairs={{0,4},{1,13},{2,6},{3,15},{4,8},{5,1},{6,10},{7,3},{8,12},{9,5},{1... | collective-permute-start | bytes 786440 | tf_op jit(solution)/shard_map/ppermute | solution.py:284
  15.1 13.4 %collective-permute-start.3 = (f32[512,128]{1,0:T(8,128)S(1)}, f32[512,128]{1,0:T(8,128)S(1)}, u32[]{:S(2)}, u32[]{:S(2)}) collective-permute-start(f32[512,128]{1,0:T(8,128)S(1)} %constant_dynamic-update-slice_fusion), channel_id=1, source_target_pairs={{0,2},{1,15},{2,4},{3,1},{4,6},{5,3},{6,8},{7,5},{8,10},{9,7},{10,... | collective-permute-start | bytes 786440 | tf_op jit(solution)/shard_map/ppermute | solution.py:284
  15.8 19.6 %all-to-all-start = ((f32[16,64,128]{2,1,0:T(8,128)}), f32[16,64,128]{2,1,0:T(8,128)S(1)}, u32[]{:S(2)}, u32[]{:S(2)}) async-start(f32[16,64,128]{2,1,0:T(8,128)} %bitcast.38), calls=%async_computation | async-start | bytes 1048576 | tf_op jit(solution)/shard_map/all_to_all | solution.py:296
  22.5 5.9 %collective-permute-start.5 = (f32[256,128]{1,0:T(8,128)S(1)}, f32[256,128]{1,0:T(8,128)S(1)}, u32[]{:S(2)}, u32[]{:S(2)}) collective-permute-start(f32[256,128]{1,0:T(8,128)S(1)} %collective-permute-done.1), channel_id=1, source_target_pairs={{0,6},{1,11},{2,8},{3,13},{4,10},{5,15},{6,12},{7,1},{8,14},{9,3},... | collective-permute-start | bytes 393224 | tf_op jit(solution)/shard_map/ppermute | solution.py:284
  28.4 6.9 %collective-permute-start.7 = (f32[512,128]{1,0:T(8,128)S(1)}, f32[512,128]{1,0:T(8,128)S(1)}, u32[]{:S(2)}, u32[]{:S(2)}) collective-permute-start(f32[512,128]{1,0:T(8,128)S(1)} %collective-permute-done.3), channel_id=1, source_target_pairs={{0,1},{1,0},{2,3},{3,2},{4,5},{5,4},{6,7},{7,6},{8,9},{9,8},{10,11... | collective-permute-start | bytes 786440 | tf_op jit(solution)/shard_map/ppermute | solution.py:275
  35.4 2.0 %collective-permute-start.10 = (f32[16,64,128]{2,1,0:T(8,128)S(1)}, f32[16,64,128]{2,1,0:T(8,128)S(1)}, u32[]{:S(2)}, u32[]{:S(2)}) collective-permute-start(f32[16,64,128]{2,1,0:T(8,128)S(1)} %all-to-all-done.refs_10_), channel_id=1, source_target_pairs={{0,1},{1,0},{2,3},{3,2},{4,5},{5,4},{6,7},{7,6},{8,9},{9,8},{10,11... | collective-permute-start | bytes 1572872 | tf_op jit(solution)/shard_map/ppermute | solution.py:275
  44.2 2.2 %collective-permute-start.11 = (f32[512,128]{1,0:T(8,128)}, f32[512,128]{1,0:T(8,128)S(1)}, u32[]{:S(2)}, u32[]{:S(2)}) collective-permute-start(f32[512,128]{1,0:T(8,128)} %bitcast.39), channel_id=1, source_target_pairs={{0,1},{1,0},{2,3},{3,2},{4,5},{5,4},{6,7},{7,6},{8,9},{9,8},{10,11... | collective-permute-start | bytes 786440 | tf_op jit(solution)/shard_map/ppermute | solution.py:275
  49.7 5.7 %collective-permute-start.12 = (f32[512,128]{1,0:T(8,128)}, f32[512,128]{1,0:T(8,128)S(1)}, u32[]{:S(2)}, u32[]{:S(2)}) collective-permute-start(f32[512,128]{1,0:T(8,128)} %get-tuple-element.53), channel_id=1, source_target_pairs={{0,2},{1,15},{2,4},{3,1},{4,6},{5,3},{6,8},{7,5},{8,10},{9,7},{10,... | collective-permute-start | bytes 786440 | tf_op jit(solution)/shard_map/ppermute | solution.py:284
  55.4 19.7 %collective-permute-start.16 = (f32[512,128]{1,0:T(8,128)S(1)}, f32[512,128]{1,0:T(8,128)S(1)}, u32[]{:S(2)}, u32[]{:S(2)}) collective-permute-start(f32[512,128]{1,0:T(8,128)S(1)} %collective-permute-done.12), channel_id=1, source_target_pairs={{0,1},{1,0},{2,3},{3,2},{4,5},{5,4},{6,7},{7,6},{8,9},{9,8},{10,11... | collective-permute-start | bytes 786440 | tf_op jit(solution)/shard_map/ppermute | solution.py:275
  57.8 17.3 %collective-permute-start.14 = (f32[512,128]{1,0:T(8,128)S(1)}, f32[512,128]{1,0:T(8,128)S(1)}, u32[]{:S(2)}, u32[]{:S(2)}) collective-permute-start(f32[512,128]{1,0:T(8,128)S(1)} %collective-permute-done.12), channel_id=1, source_target_pairs={{0,4},{1,13},{2,6},{3,15},{4,8},{5,1},{6,10},{7,3},{8,12},{9,5},{1... | collective-permute-start | bytes 786440 | tf_op jit(solution)/shard_map/ppermute | solution.py:284
  57.9 17.3 %collective-permute-start.13 = (f32[512,128]{1,0:T(8,128)S(1)}, f32[512,128]{1,0:T(8,128)S(1)}, u32[]{:S(2)}, u32[]{:S(2)}) collective-permute-start(f32[512,128]{1,0:T(8,128)S(1)} %collective-permute-done.12), channel_id=1, source_target_pairs={{0,2},{1,15},{2,4},{3,1},{4,6},{5,3},{6,8},{7,5},{8,10},{9,7},{10,... | collective-permute-start | bytes 786440 | tf_op jit(solution)/shard_map/ppermute | solution.py:284
  59.2 19.4 %all-to-all-start.1 = ((f32[16,64,128]{2,1,0:T(8,128)}), f32[16,64,128]{2,1,0:T(8,128)S(1)}, u32[]{:S(2)}, u32[]{:S(2)}) async-start(f32[16,64,128]{2,1,0:T(8,128)} %bitcast.47), calls=%async_computation.1 | async-start | bytes 1048576 | tf_op jit(solution)/shard_map/all_to_all | solution.py:296
  67.2 7.8 %collective-permute-start.15 = (f32[256,128]{1,0:T(8,128)S(1)}, f32[256,128]{1,0:T(8,128)S(1)}, u32[]{:S(2)}, u32[]{:S(2)}) collective-permute-start(f32[256,128]{1,0:T(8,128)S(1)} %slice.9), channel_id=1, source_target_pairs={{0,6},{1,11},{2,8},{3,13},{4,10},{5,15},{6,12},{7,1},{8,14},{9,3},... | collective-permute-start | bytes 393224 | tf_op jit(solution)/shard_map/ppermute | solution.py:284
  75.1 3.5 %collective-permute-start.17 = (f32[512,128]{1,0:T(8,128)S(1)}, f32[512,128]{1,0:T(8,128)S(1)}, u32[]{:S(2)}, u32[]{:S(2)}) collective-permute-start(f32[512,128]{1,0:T(8,128)S(1)} %collective-permute-done.13), channel_id=1, source_target_pairs={{0,1},{1,0},{2,3},{3,2},{4,5},{5,4},{6,7},{7,6},{8,9},{9,8},{10,11... | collective-permute-start | bytes 786440 | tf_op jit(solution)/shard_map/ppermute | solution.py:275
  94.0 27.3 %collective-permute-start.21 = (f32[16,64,128]{2,1,0:T(8,128)S(1)}, f32[16,64,128]{2,1,0:T(8,128)S(1)}, u32[]{:S(2)}, u32[]{:S(2)}) collective-permute-start(f32[16,64,128]{2,1,0:T(8,128)S(1)} %all-to-all-done.1.mine), channel_id=1, source_target_pairs={{0,1},{1,0},{2,3},{3,2},{4,5},{5,4},{6,7},{7,6},{8,9},{9,8},{10,11... | collective-permute-start | bytes 1572872 | tf_op jit(solution)/shard_map/ppermute | solution.py:275
  95.5 2.0 %collective-permute-start.20 = (f32[384,128]{1,0:T(8,128)}, f32[384,128]{1,0:T(8,128)S(1)}, u32[]{:S(2)}, u32[]{:S(2)}) collective-permute-start(f32[384,128]{1,0:T(8,128)} %get-tuple-element.68), channel_id=1, source_target_pairs={{0,1},{1,0},{2,3},{3,2},{4,5},{5,4},{6,7},{7,6},{8,9},{9,8},{10,11... | collective-permute-start | bytes 589832 | tf_op jit(solution)/shard_map/ppermute | solution.py:275
  114.2 12.8 %all-to-all-start.3 = ((f32[8,24,128]{2,1,0:T(8,128)}), f32[8,24,128]{2,1,0:T(8,128)S(1)}, u32[]{:S(2)}, u32[]{:S(2)}) async-start(f32[8,24,128]{2,1,0:T(8,128)} %broadcast_in_dim.4), calls=%async_computation.3 | async-start | bytes 196608 | tf_op jit(solution)/shard_map/all_to_all | solution.py:463
  119.2 12.1 %collective-permute-start.22 = (f32[256,256]{1,0:T(8,128)}, f32[256,256]{1,0:T(8,128)S(1)}, u32[]{:S(2)}, u32[]{:S(2)}) collective-permute-start(f32[256,256]{1,0:T(8,128)} %get-tuple-element.72), channel_id=1, source_target_pairs={{0,1},{1,0},{2,3},{3,2},{4,5},{5,4},{6,7},{7,6},{8,9},{9,8},{10,11... | collective-permute-start | bytes 786440 | tf_op jit(solution)/shard_map/ppermute | solution.py:275
  127.6 10.7 %all-to-all-start.4 = ((f32[16,24,128]{2,1,0:T(8,128)}), f32[16,24,128]{2,1,0:T(8,128)S(1)}, u32[]{:S(2)}, u32[]{:S(2)}) async-start(f32[16,24,128]{2,1,0:T(8,128)} %broadcast_in_dim.5), calls=%async_computation.4 | async-start | bytes 393216 | tf_op jit(solution)/shard_map/all_to_all | solution.py:296
  138.3 5.2 %collective-permute-start.23 = (f32[384,128]{1,0:T(8,128)S(1)}, f32[384,128]{1,0:T(8,128)S(1)}, u32[]{:S(2)}, u32[]{:S(2)}) collective-permute-start(f32[384,128]{1,0:T(8,128)S(1)} %bitcast.41), channel_id=1, source_target_pairs={{0,1},{1,0},{2,3},{3,2},{4,5},{5,4},{6,7},{7,6},{8,9},{9,8},{10,11... | collective-permute-start | bytes 589832 | tf_op jit(solution)/shard_map/ppermute | solution.py:275
  (27 other events, 169.5 us)

commit v3 on v2

--- a/solution.py
+++ b/solution.py
@@ -63,19 +63,10 @@
         ) + got[:, 2 * TILE :]
 
 
-def pick_features_kernel(place, mine, other, idx_ref, out_ref):
+def pick_kernel(place, mine, other, idx_ref, out_ref):
     q = place[0]
     a, b = mine[...], other[...]
     panel = jnp.concatenate([jnp.where(q == 0, a, b), jnp.where(q == 0, b, a)], axis=0)
-    pick_rows(q, panel, idx_ref, out_ref)
-
-
-def pick_agg_kernel(place, mine, other, idx_ref, panel_ref, out_ref):
-    q = place[0]
-    panel = mine[...] + other[...]
-    size = panel.shape[0] // 2
-    panel_ref[:size, :] = jnp.where(q == 0, panel[:size], panel[size:])
-    panel_ref[size:, :] = jnp.where(q == 0, panel[size:], panel[:size])
     pick_rows(q, panel, idx_ref, out_ref)
 
 
@@ -180,50 +171,108 @@
     forward_tiles(rows_s, cols_s, count_s, tiles_hbm, tiles, tile_sems, x_scr, acc)
 
 
-def layer_two_kernel(place, rows_s, cols_s, count_s, *refs):
-    own, mine, theirs = refs[0], refs[1:5], refs[5:9]
-    (w1, w2, cot, hist_hbm, c_hbm, tiles_hbm) = refs[9:15]
-    (g_keep, g_send, p_keep, p_send) = refs[15:19]
-    (xf, h_scr, acc, g_one, hist, c_terms, tiles, sems, tile_sems, c_sems) = refs[19:]
-    q = place[0]
-
-    def c_copy(g):
-        part = pl.ds(g * 4, 4)
-        return pltpu.make_async_copy(c_hbm.at[part], c_terms.at[part], c_sems.at[g])
-
-    copies = piece_copies(place, (own.at[pl.ds(0, 2)], own.at[pl.ds(2, 2)]), mine, theirs, xf, sems)
-    hist_copy = pltpu.make_async_copy(hist_hbm, hist, sems.at[16])
+def hidden_step(x, terms, w_hi, w_lo, h_ref, at, n):
+    total = jnp.zeros((TILE, w_hi.shape[1]), f32)
+    for b in range(n):
+        x_b = x[b]
+        x_hi, x_lo = split2(x_b)
+        pre = mm(x_hi, w_hi, NN) + (mm(x_hi, w_lo, NN) + mm(x_lo, w_hi, NN))
+        sig = 1.0 / (1.0 + jnp.exp(-pre))
+        hi, lo = split2(pre * sig)
+        h_ref[at + b, :TILE, :] = hi
+        h_ref[at + b, TILE:, :] = lo
+        grad = terms[b] * (sig * (1.0 + pre * (1.0 - sig)))
+        total += dot3(x_b, grad, TN)
+    return total
+
+
+def early_kernel(place, own, one, their_one, w1, c_hbm, hidden, g_out, c_terms, sems):
+    q, r = place[0], place[1]
+    side = 1 - 2 * q
+    copies = []
+    for k, (row, half) in enumerate(early_parts(r, q, side)):
+        for h in (0, 1):
+            at = row * 4 + 2 * (half if h == 0 else 1 - half)
+            copies.append(
+                pltpu.make_async_copy(
+                    c_hbm.at[pl.ds(at, 2)], c_terms.at[pl.ds(4 * k + 2 * h, 2)], sems.at[2 * k + h]
+                )
+            )
     for c in copies:
         c.start()
-    for g in range(N_ROW):
+    w_hi, w_lo = split2(w1[...])
+    total = jnp.zeros(g_out.shape, f32)
+    for k, x in enumerate((own, one, their_one)):
+        copies[2 * k].wait()
+        copies[2 * k + 1].wait()
+        total += hidden_step(x, c_terms.at[pl.ds(4 * k, 4)], w_hi, w_lo, hidden, 4 * k, 4)
+    g_out[...] = total
+
+
+def early_parts(r, q, side):
+    below = lax.rem(r + N_ROW - side, N_ROW)
+    above = lax.rem(r + N_ROW + side, N_ROW)
+    return ((r, q), (below, q), (above, 1 - q))
+
+
+def layer_two_kernel(place, rows_s, cols_s, count_s, *refs):
+    mine, theirs = refs[0:3], refs[3:6]
+    (early, g_early, w1, w2, cot, hist_hbm, c_hbm, tiles_hbm) = refs[6:14]
+    grads, p_keep, p_send = refs[14:17]
+    (xf, h_scr, acc, g_one, hist, c_terms, tiles, sems, tile_sems, c_sems) = refs[17:]
+    q, r = place[0], place[1]
+    side = 1 - 2 * q
+    parts = []
+    for refs_m, way, half in ((mine, side, q), (theirs, -side, 1 - q)):
+        for n, s in ((0, 2), (1, 3)):
+            slot = lax.rem(2 * N_ROW - way * s, N_ROW) - 2
+            parts.append((refs_m[n].at[pl.ds(0, 2)], slot, half))
+            parts.append((refs_m[n].at[pl.ds(2, 2)], slot, 1 - half))
+        parts.append((refs_m[2], 2, half))
+    copies = [
+        pltpu.make_async_copy(ref, xf.at[pl.ds(slot * 4 + half * 2, 2)], sems.at[k])
+        for k, (ref, slot, half) in enumerate(parts)
+    ]
+    late = []
+    for k, (row, half) in enumerate(early_parts(r, q, side)):
+        for h in (0, 1):
+            at = row * 4 + 2 * (half if h == 0 else 1 - half)
+            late.append(
+                pltpu.make_async_copy(
+                    early.at[pl.ds(4 * k + 2 * h, 2)], h_scr.at[pl.ds(at, 2)], sems.at[10 + 2 * k + h]
+                )
+            )
+    late.append(pltpu.make_async_copy(hist_hbm, hist, sems.at[16]))
+
+    def row_of(g):
+        return lax.rem(r + 2 + g, N_ROW)
+
+    def c_copy(g):
+        return pltpu.make_async_copy(
+            c_hbm.at[pl.ds(row_of(g) * 4, 4)], c_terms.at[pl.ds(g * 4, 4)], c_sems.at[g]
+        )
+
+    for c in copies:
+        c.start()
+    for g in range(5):
         c_copy(g).start()
-    hist_copy.start()
-    for c in tile_copies(tiles_hbm, tiles, tile_sems):
+    for c in late + tile_copies(tiles_hbm, tiles, tile_sems):
         c.start()
     acc[...] = jnp.zeros_like(acc)
-    g_one[...] = jnp.zeros_like(g_one)
+    g_one[...] = g_early[...]
+    w_hi, w_lo = split2(w1[...])
     for c in copies:
         c.wait()
 
     def panel_step(g, carry):
         c_copy(g).wait()
-        w_hi, w_lo = split2(w1[...])
-        total = jnp.zeros((TILE, w1.shape[1]), f32)
-        for b in range(4):
-            x = xf[g * 4 + b]
-            x_hi, x_lo = split2(x)
-            pre = mm(x_hi, w_hi, NN) + (mm(x_hi, w_lo, NN) + mm(x_lo, w_hi, NN))
-            sig = 1.0 / (1.0 + jnp.exp(-pre))
-            hi, lo = split2(pre * sig)
-            h_scr[g * 4 + b, :TILE, :] = hi
-            h_scr[g * 4 + b, TILE:, :] = lo
-            grad = c_terms[g * 4 + b] * (sig * (1.0 + pre * (1.0 - sig)))
-            total += dot3(x, grad, TN)
-        g_one[...] += total
+        part = pl.ds(g * 4, 4)
+        g_one[...] += hidden_step(xf.at[part], c_terms.at[part], w_hi, w_lo, h_scr, row_of(g) * 4, 4)
         return carry
 
-    lax.fori_loop(0, N_ROW, panel_step, 0)
-    hist_copy.wait()
+    lax.fori_loop(0, 5, panel_step, 0)
+    for c in late:
+        c.wait()
 
     def hist_step(g, carry):
         for b in range(2):
@@ -237,10 +286,10 @@
 
     agg = acc[...].reshape(4 * TILE, -1)
     g_two = dot3(agg, cot[...], TN)
-    left = jnp.concatenate([g_one[:, :TILE], g_two[:, :TILE]], axis=0)
-    right = jnp.concatenate([g_one[:, TILE:], g_two[:, TILE:]], axis=0)
-    g_keep[...] = jnp.where(q == 0, left, right)
-    g_send[...] = jnp.where(q == 0, right, left)
+    for h in (0, 1):
+        cols = pl.ds(h * TILE, TILE)
+        grads[: g_one.shape[0] // 8, h] = g_one[:, cols].reshape(-1, 8, TILE)
+        grads[g_one.shape[0] // 8 :, h] = g_two[:, h * TILE : (h + 1) * TILE].reshape(-1, 8, TILE)
     prod = dot3(agg, w2[...], NN)
     low, high = prod[: 2 * TILE], prod[2 * TILE :]
     p_keep[...] = jnp.where(q == 0, low, high)
@@ -332,25 +381,35 @@
             cost_estimate=cost(6 * SLOTS * TILE * TILE * h_dim, 9 << 20),
         )(rows_s, cols_s, count_s, cotangent, weight_two, tiles)
 
+    def pick_call(name, mine, mine_at, other, other_at):
+        return pl.pallas_call(
+            pick_kernel,
+            name=name,
+            grid=(1,),
+            out_shape=jax.ShapeDtypeStruct((N_DOM * HALF, f_dim), f32),
+            in_specs=[
+                SMEM,
+                pl.BlockSpec((half_rows, f_dim), lambda g: mine_at),
+                pl.BlockSpec((half_rows, f_dim), lambda g: other_at),
+                VMEM,
+            ],
+            out_specs=VMEM,
+            compiler_params=params(),
+            cost_estimate=cost(1 << 20, 1 << 20),
+        )(place, mine, other, idx)
+
     other = swap(features)
     first, second = along(features, 1), along(other, 1)
-    outgoing = pl.pallas_call(
-        pick_features_kernel,
-        name="pick_features",
-        out_shape=jax.ShapeDtypeStruct((N_DOM * HALF, f_dim), f32),
-        in_specs=[SMEM, VMEM, VMEM, VMEM],
-        out_specs=VMEM,
-        compiler_params=params(),
-        cost_estimate=cost(1 << 20, 1 << 20),
-    )(place, features, other, idx)
-    first, second, outgoing = together(first, second, outgoing)
+    outgoing = pick_call("pick_features", features, (0, 0), other, (0, 0))
+    first, second, outgoing, count_b = together(first, second, outgoing, count_s)
     one = jnp.concatenate([first, second])
     halo_mine = to_all(outgoing.reshape(N_DOM, HALF, f_dim))
-    two, three, four, theirs_one = together(
+    two, three, four, theirs_one, c_terms = together(
         along(one, 1),
         along(one, 2),
         along(first, 3),
         swap(one),
+        backward(count_b),
     )
     mine = [one, two, three, four]
     theirs = [theirs_one, swap(two), swap(three), swap(four)]
@@ -382,48 +441,52 @@
         tiles,
     ).reshape(4 * TILE, f_dim)
 
-    panel, outgoing_two = pl.pallas_call(
-        pick_agg_kernel,
-        name="pick_agg",
+    total = part_one + swap(part_one)
+    low, high = total[:half_rows], total[half_rows:]
+    panel = jnp.where(q == 0, total, jnp.concatenate([high, low]))
+    outgoing_two = pick_call("pick_agg", panel, (0, 0), panel, (1, 0))
+    one, outgoing_two = together(along(panel, 1), outgoing_two)
+    fresh_mine = to_all(outgoing_two.reshape(N_DOM, HALF, f_dim))
+    theirs_one = swap(one)
+    early, g_early = pl.pallas_call(
+        early_kernel,
+        name="early",
         out_shape=(
-            jax.ShapeDtypeStruct((4 * TILE, f_dim), f32),
-            jax.ShapeDtypeStruct((N_DOM * HALF, f_dim), f32),
+            jax.ShapeDtypeStruct((12, 2 * TILE, h_dim), bf16),
+            jax.ShapeDtypeStruct((f_dim, h_dim), f32),
         ),
-        in_specs=[SMEM, VMEM, VMEM, VMEM],
+        in_specs=[SMEM, VMEM, VMEM, VMEM, VMEM, ANY],
         out_specs=(VMEM, VMEM),
+        scratch_shapes=[pltpu.VMEM((12, TILE, h_dim), f32), pltpu.SemaphoreType.DMA((6,))],
         compiler_params=params(),
-    )(place, part_one, swap(part_one), idx)
-    fresh_mine = to_all(outgoing_two.reshape(N_DOM, HALF, f_dim))
-    one, count_b = together(along(panel, 1), count_s)
-    c_terms = backward(count_b)
-    two, three, four, theirs_one, c_terms = together(
+        cost_estimate=cost(6 << 30, 4 << 20),
+    )(place, blocks(panel), blocks(one), blocks(theirs_one), weight_one, c_terms)
+    two, three, four, early = together(
         along(one, 1),
         along(one, 2),
         along(one[:half_rows], 3),
-        swap(one),
-        c_terms,
+        early,
     )
-    agg_mine = [one, two, three, four]
-    agg_theirs = [theirs_one, swap(two), swap(three), swap(four)]
+    agg_theirs = [swap(two), swap(three), swap(four)]
     fresh_mine, *agg_theirs = together(fresh_mine, *agg_theirs)
-    g_keep, g_send, p_keep, p_send = pl.pallas_call(
+
+    grads, p_keep, p_send = pl.pallas_call(
         layer_two_kernel,
         name="layer_two",
         out_shape=(
-            jax.ShapeDtypeStruct((f_dim + h_dim, TILE), f32),
-            jax.ShapeDtypeStruct((f_dim + h_dim, TILE), f32),
+            jax.ShapeDtypeStruct(((f_dim + h_dim) // 8, 2, 8, TILE), f32),
             jax.ShapeDtypeStruct((2 * TILE, h_dim), f32),
             jax.ShapeDtypeStruct((2 * TILE, h_dim), f32),
         ),
-        in_specs=[SMEM] * 4 + [ANY] * 9 + [VMEM] * 3 + [ANY] * 3,
-        out_specs=(VMEM, VMEM, VMEM, VMEM),
+        in_specs=[SMEM] * 4 + [ANY] * 7 + [VMEM] * 4 + [ANY] * 3,
+        out_specs=(VMEM, VMEM, VMEM),
         scratch_shapes=[
-            pltpu.VMEM((OWN, TILE, f_dim), f32),
+            pltpu.VMEM((20, TILE, f_dim), f32),
             pltpu.VMEM((COLS, 2 * TILE, h_dim), bf16),
             pltpu.VMEM((4, TILE, h_dim), f32),
             pltpu.VMEM((f_dim, h_dim), f32),
             pltpu.VMEM((N_DOM, TILE, h_dim), f32),
-            pltpu.VMEM((OWN, TILE, h_dim), f32),
+            pltpu.VMEM((20, TILE, h_dim), f32),
         ]
         + tile_scr
         + [pltpu.SemaphoreType.DMA((18,))]
@@ -436,7 +499,9 @@
         rows_s,
         cols_s,
         count_s,
-        *[blocks(x) for x in [panel] + agg_mine + agg_theirs],
+        *[blocks(x) for x in [two, three, four] + agg_theirs],
+        early,
+        g_early,
         weight_one,
         weight_two,
         cotangent,
@@ -445,9 +510,16 @@
         tiles,
     )
 
-    fresh_mine, g_keep = together(fresh_mine, g_keep)
+    fresh_mine, grads = together(fresh_mine, grads)
     fresh_theirs = swap(fresh_mine)
     output = p_keep + swap(p_send)
+    part = grads.reshape(N_DOM * N_REP, -1, TILE)
+    part = lax.all_to_all(part, ("dom", "rep"), split_axis=0, concat_axis=0, tiled=True)
+    part = jnp.sum(part, axis=0)
+    part = jnp.broadcast_to(part[None], (N_ROW,) + part.shape)
+    part = lax.all_to_all(part, "row", split_axis=0, concat_axis=0, tiled=True)
+    part = jnp.sum(part, axis=0)
+    part, place_late = together(part, place)
     fresh = pl.pallas_call(
         fresh_kernel,
         name="fresh",
@@ -456,19 +528,11 @@
         out_specs=VMEM,
         compiler_params=params(),
         cost_estimate=cost(6 * N_DOM * TILE * f_dim * h_dim, 4 << 20),
-    )(place, fresh_mine, fresh_theirs, weight_one)
-    part = to_all((g_keep + swap(g_send)).reshape(N_DOM, -1, TILE))
-    part = jnp.sum(part, axis=0)
-    part = jnp.broadcast_to(part[None], (N_ROW,) + part.shape)
-    part = lax.all_to_all(part, "row", split_axis=0, concat_axis=0, tiled=True)
-    part, fresh = together(part, fresh)
-    part = jnp.sum(part, axis=0)
-    part = jnp.broadcast_to(part[None], (N_DOM,) + part.shape)
-    mine_g, output = together(to_all(part).reshape(-1, TILE), output)
-    theirs_g = swap(mine_g)
-    low = jnp.where(q == 0, mine_g, theirs_g)
-    high = jnp.where(q == 0, theirs_g, mine_g)
-    grads = jnp.concatenate([low, high], axis=1)
+    )(place_late, fresh_mine, fresh_theirs, weight_one)
+    part = jnp.broadcast_to(part[None], (N_DOM * N_REP,) + part.shape)
+    part = lax.all_to_all(part, ("dom", "rep"), split_axis=0, concat_axis=0, tiled=True)
+    part, output, fresh = together(part, output, fresh)
+    grads = part.reshape(-1, 2, 8, TILE).transpose(0, 2, 1, 3).reshape(-1, h_dim)
     return (output, grads[:f_dim], grads[f_dim:], fresh)
 
 

time: 146 us -> 141 us (0.966)
  blocking collectives: 15 us -> 11.9 us
  starting transfers between devices: 61.9 us -> 60.2 us
    all_to_all x1 -> x2, waiting for transfers between devices: 1.22 us -> 13.6 us  [local(): lax.all_to_all(part, ('dom', 'rep'), split_axis=0, concat_axis=0, tiled=T...]
    all_to_all x1 -> x2, starting transfers between devices: 5.07 us -> 14.9 us  [local(): lax.all_to_all(part, ('dom', 'rep'), split_axis=0, concat_axis=0, tiled=T...]
    all_to_all x3 -> x2, waiting for transfers between devices: 7.51 us -> 0.01 us  [to_all(): return lax.all_to_all(x, 'dom', split_axis=0, concat_axis=0, tiled=True)]
    ppermute x15 -> x13, starting transfers between devices: 23.4 us -> 17.2 us  [swap(): return lax.ppermute(x, 'rep', [(0, 1), (1, 0)])]
    ppermute x9, waiting for transfers between devices: 8.41 us -> 2.45 us  [along(): return lax.ppermute(x, ('row', 'rep'), pairs)]
    pallas_call x2 -> x3, Pallas kernels: 5.2 us -> 10.5 us  [the longest x1 5.38 us: local(): pl.pallas_call(early_kernel, name='early', out_shape=(jax.ShapeDtypeStruc...]
    pallas_call x1, Pallas kernels: 14.4 us -> 10.5 us  [local(): pl.pallas_call(layer_two_kernel, name='layer_two', out_shape=(jax.ShapeDt...]
    ppermute x9, starting transfers between devices: 15 us -> 11.3 us  [along(): return lax.ppermute(x, ('row', 'rep'), pairs)]
  transfers between devices with their start and end apart: 28 -> 26, of which waited for: 11 -> 8; matrix products, arithmetic and copies ran while one was open for 3% -> 2% of each run, Pallas kernels for 8% -> 14%
where the time goes in v3:
time: 141 us; the launch traced here: 140 us
  starting transfers between devices  60.2 us (43%)
  Pallas kernels  36 us (26%)
  waiting for transfers between devices  22.6 us (16%)
  blocking collectives  11.9 us (8%)
  local copies, waits for them, and re-layouts  5.33 us (4%)
  other arithmetic  2.45 us (2%)
  between operations  1.75 us (1%)
    ppermute x13, starting transfers between devices, swap(): return lax.ppermute(x, 'rep', [(0, 1), (1, 0)])  17.2 us
    all_to_all x2, starting transfers between devices, to_all(): return lax.all_to_all(x, 'dom', split_axis=0, concat_axis=0, tiled=True)  16.7 us
    all_to_all x2, starting transfers between devices, local(): lax.all_to_all(part, ('dom', 'rep'), split_axis=0, concat_axis=0, tiled=T...  14.9 us
    all_to_all x2, waiting for transfers between devices, local(): lax.all_to_all(part, ('dom', 'rep'), split_axis=0, concat_axis=0, tiled=T...  13.6 us
    all_to_all x1, blocking collectives, local(): part = lax.all_to_all(part, 'row', split_axis=0, concat_axis=0, tiled=True)  11.9 us
    ppermute x9, starting transfers between devices, along(): return lax.ppermute(x, ('row', 'rep'), pairs)  11.3 us
    pallas_call x1, Pallas kernels, local(): pl.pallas_call(layer_two_kernel, name='layer_two', out_shape=(jax.ShapeDt...  10.5 us
    ppermute x13, waiting for transfers between devices, swap(): return lax.ppermute(x, 'rep', [(0, 1), (1, 0)])  6.54 us
  transfers between devices with their start and end apart: 26, of which 8 were waited for; matrix products, arithmetic and copies ran while one was open for 2% of the time, Pallas kernels for 14%

profile of v3, /device:TPU:1, one launch (start us, length us, event | category | flops | bytes accessed | tf_op | source)
XLA Modules:
  0.0 140.2 jit_solution(160586926443317637)
XLA Ops:
  0.6 3.3 %collective-permute-start = (f32[256,128]{1,0:T(8,128)}, f32[256,128]{1,0:T(8,128)S(1)}, u32[]{:S(2)}, u32[]{:S(2)}) collective-permute-start(f32[256,128]{1,0:T(8,128)} %mine.1), channel_id=1, source_target_pairs={{0,1},{1,0},{2,3},{3,2},{4,5},{5,4},{6,7},{7,6},{8,9},{9,8},{10,11... | collective-permute-start | bytes 393224 | tf_op jit(solution)/shard_map/ppermute | solution.py:324
  4.0 3.8 %collective-permute-start.1 = (f32[256,128]{1,0:T(8,128)}, f32[256,128]{1,0:T(8,128)S(1)}, u32[]{:S(2)}, u32[]{:S(2)}) collective-permute-start(f32[256,128]{1,0:T(8,128)} %mine.1), channel_id=1, source_target_pairs={{0,2},{1,15},{2,4},{3,1},{4,6},{5,3},{6,8},{7,5},{8,10},{9,7},{10,... | collective-permute-start | bytes 393224 | tf_op jit(solution)/shard_map/ppermute | solution.py:333
  9.7 2.6 %pick_features.1 = f32[1024,128]{1,0:T(8,128)} custom-call(s32[2]{0:T(128)} %pad_add_fusion.place, f32[256,128]{1,0:T(8,128)} %mine.1, f32[256,128]{1,0:T(8,128)} %copy-done.4, s32[16,128]{1,0:T(8,128)} %bitcast.63), custom_call_target="tpu_custom_call" | custom-call | flops 1048576 | bytes 1048576 | tf_op jit(solution)/shard_map/pick_features/pallas_call | solution.py:385
  12.9 2.2 %collective-permute-start.4 = (f32[512,128]{1,0:T(8,128)S(1)}, f32[512,128]{1,0:T(8,128)S(1)}, u32[]{:S(2)}, u32[]{:S(2)}) collective-permute-start(f32[512,128]{1,0:T(8,128)S(1)} %constant_dynamic-update-slice_fusion), channel_id=1, source_target_pairs={{0,4},{1,13},{2,6},{3,15},{4,8},{5,1},{6,10},{7,3},{8,12},{9,5},{1... | collective-permute-start | bytes 786440 | tf_op jit(solution)/shard_map/ppermute | solution.py:333
  15.8 6.8 %all-to-all-start = ((f32[16,64,128]{2,1,0:T(8,128)}), f32[16,64,128]{2,1,0:T(8,128)S(1)}, u32[]{:S(2)}, u32[]{:S(2)}) async-start(f32[16,64,128]{2,1,0:T(8,128)} %bitcast.46), calls=%async_computation | async-start | bytes 1048576 | tf_op jit(solution)/shard_map/all_to_all | solution.py:345
  23.2 1.7 %collective-permute-start.5 = (f32[256,128]{1,0:T(8,128)S(1)}, f32[256,128]{1,0:T(8,128)S(1)}, u32[]{:S(2)}, u32[]{:S(2)}) collective-permute-start(f32[256,128]{1,0:T(8,128)S(1)} %collective-permute-done.1), channel_id=1, source_target_pairs={{0,6},{1,11},{2,8},{3,13},{4,10},{5,15},{6,12},{7,1},{8,14},{9,3},... | collective-permute-start | bytes 393224 | tf_op jit(solution)/shard_map/ppermute | solution.py:333
  24.9 5.4 %backward.1.c_hbm.refs_12_ = f32[33,128,256]{2,1,0:T(8,128)} custom-call(s32[1,64]{1,0:T(1,128)} %bitcast.65, s32[1,64]{1,0:T(1,128)} %bitcast.68, s32[1,1]{1,0:T(1,128)} %bitcast.39.count_s, f32[512,256]{1,0:T(8,128)} %refs_10_.1, f32[256,256]{1,0:T(8,128)} %refs_9_.1, f32[64,128,128]{2,1,0:T(8,128)} %bitcast.42), custom_call_target="tpu_custom_call" | custom-call | flops 1610612736 | bytes 9437184 | tf_op jit(solution)/shard_map/backward/pallas_call | solution.py:373
  30.4 3.9 %collective-permute-start.7 = (f32[512,128]{1,0:T(8,128)S(1)}, f32[512,128]{1,0:T(8,128)S(1)}, u32[]{:S(2)}, u32[]{:S(2)}) collective-permute-start(f32[512,128]{1,0:T(8,128)S(1)} %collective-permute-done.3), channel_id=1, source_target_pairs={{0,1},{1,0},{2,3},{3,2},{4,5},{5,4},{6,7},{7,6},{8,9},{9,8},{10,11... | collective-permute-start | bytes 786440 | tf_op jit(solution)/shard_map/ppermute | solution.py:324
  36.5 1.5 %collective-permute-done.10.refs_11_ = f32[16,64,128]{2,1,0:T(8,128)S(1)} collective-permute-done((f32[16,64,128]{2,1,0:T(8,128)S(1)}, f32[16,64,128]{2,1,0:T(8,128)S(1)}, u32[]{:S(2)}, u32[]{:S(2)}) %collective-permute-start.10) | collective-permute-done | bytes 524320 | tf_op jit(solution)/shard_map/ppermute | solution.py:324
  38.9 6.0 %pass_one.1 = f32[4,128,128]{2,1,0:T(8,128)} custom-call(s32[2]{0:T(128)} %pad_add_fusion.place, s32[1,64]{1,0:T(1,128)} %bitcast.66, s32[1,64]{1,0:T(1,128)} %bitcast.69, s32[1,1]{1,0:T(1,128)} %bitcast.40.count_s, f32[2,128,128]{2,1,0:T(8,128)} %bitcast.52, f32[2,128,128]{2,1,0:T(8,128)} %bitcast.53, f32[4,128,128]{2,1,0:T(8,128)} %bitcast.51, ...), custom_call_target="tpu_custom_call" | custom-call | tf_op jit(solution)/shard_map/pass_one/pallas_call | solution.py:419
  46.1 1.4 collective-permute-done.11
  49.3 2.6 %pick_agg.1 = f32[1024,128]{1,0:T(8,128)} custom-call(s32[2]{0:T(128)} %pad_add_fusion.place, f32[512,128]{1,0:T(8,128)} %copy-done, f32[512,128]{1,0:T(8,128)} %copy-done, s32[16,128]{1,0:T(8,128)} %bitcast.64), custom_call_target="tpu_custom_call" | custom-call | flops 1048576 | bytes 1048576 | tf_op jit(solution)/shard_map/pick_agg/pallas_call | solution.py:385
  51.8 2.4 %collective-permute-done.12 = f32[512,128]{1,0:T(8,128)S(1)} collective-permute-done((f32[512,128]{1,0:T(8,128)S(1)}, f32[512,128]{1,0:T(8,128)S(1)}, u32[]{:S(2)}, u32[]{:S(2)}) %collective-permute-start.12) | collective-permute-done | bytes 262176 | tf_op jit(solution)/shard_map/ppermute | solution.py:333
  54.3 2.4 %collective-permute-start.16 = (f32[512,128]{1,0:T(8,128)S(1)}, f32[512,128]{1,0:T(8,128)S(1)}, u32[]{:S(2)}, u32[]{:S(2)}) collective-permute-start(f32[512,128]{1,0:T(8,128)S(1)} %collective-permute-done.12), channel_id=1, source_target_pairs={{0,1},{1,0},{2,3},{3,2},{4,5},{5,4},{6,7},{7,6},{8,9},{9,8},{10,11... | collective-permute-start | bytes 786440 | tf_op jit(solution)/shard_map/ppermute | solution.py:324
  57.5 9.9 %all-to-all-start.1 = ((f32[16,64,128]{2,1,0:T(8,128)}), f32[16,64,128]{2,1,0:T(8,128)S(1)}, u32[]{:S(2)}, u32[]{:S(2)}) async-start(f32[16,64,128]{2,1,0:T(8,128)} %bitcast.47), calls=%async_computation.1 | async-start | bytes 1048576 | tf_op jit(solution)/shard_map/all_to_all | solution.py:345
  68.3 5.4 %early.1 = (bf16[12,256,256]{2,1,0:T(8,128)(2,1)}, f32[128,256]{1,0:T(8,128)}) custom-call(s32[2]{0:T(128)} %pad_add_fusion.place, f32[4,128,128]{2,1,0:T(8,128)} %bitcast.45, f32[4,128,128]{2,1,0:T(8,128)} %bitcast.62, f32[4,128,128]{2,1,0:T(8,128)} %bitcast.76, f32[128,256]{1,0:T(8,128)} %w1.3, f32[33,128,256]{2,1,0:T(8,128)} %backward.1.c_hbm.refs_12_), custom_call_target="tpu_custom_call" | custom-call | flops 6442450944 | bytes 4194304 | tf_op jit(solution)/shard_map/early/pallas_call | solution.py:451
  73.8 3.6 %collective-permute-start.17 = (f32[512,128]{1,0:T(8,128)S(1)}, f32[512,128]{1,0:T(8,128)S(1)}, u32[]{:S(2)}, u32[]{:S(2)}) collective-permute-start(f32[512,128]{1,0:T(8,128)S(1)} %collective-permute-done.13), channel_id=1, source_target_pairs={{0,1},{1,0},{2,3},{3,2},{4,5},{5,4},{6,7},{7,6},{8,9},{9,8},{10,11... | collective-permute-start | bytes 786440 | tf_op jit(solution)/shard_map/ppermute | solution.py:324
  79.9 10.5 %layer_two.1 = (f32[48,2,8,128]{3,2,1,0:T(8,128)}, f32[256,256]{1,0:T(8,128)}, f32[256,256]{1,0:T(8,128)}) custom-call(s32[2]{0:T(128)} %pad_add_fusion.place, s32[1,64]{1,0:T(1,128)} %bitcast.67, s32[1,64]{1,0:T(1,128)} %bitcast.70, s32[1,1]{1,0:T(1,128)} %bitcast.41.count_s, f32[4,128,128]{2,1,0:T(8,128)} %bitcast.73, f32[4,128,128]{2,1,0:T(8,128)} %bitcast.72, ...), custom_call_target="tpu_custom_call" | custom-call | flops 8589934592 | bytes 16777216 | tf_op jit(solution)/shard_map/layer_two/pallas_call | solution.py:473
  90.4 10.0 %all-to-all-start.2 = ((f32[32,24,128]{2,1,0:T(8,128)}), f32[32,24,128]{2,1,0:T(8,128)S(1)}, u32[]{:S(2)}, u32[]{:S(2)}) async-start(f32[32,24,128]{2,1,0:T(8,128)} %bitcast.54), calls=%async_computation.2 | async-start | bytes 786432 | tf_op jit(solution)/shard_map/all_to_all | solution.py:517
  100.8 10.0 %all-to-all-done.2 = f32[32,24,128]{2,1,0:T(8,128)S(1)} async-done(((f32[32,24,128]{2,1,0:T(8,128)}), f32[32,24,128]{2,1,0:T(8,128)S(1)}, u32[]{:S(2)}, u32[]{:S(2)}) %all-to-all-start.2) | async-done | bytes 393248 | tf_op jit(solution)/shard_map/all_to_all | solution.py:517
  110.8 11.9 %all_to_all.25 = f32[8,24,128]{2,1,0:T(8,128)S(1)} all-to-all(f32[8,24,128]{2,1,0:T(8,128)S(1)} %broadcast_in_dim.4), channel_id=1, replica_groups=mesh['dom'=16,'row'=8,'rep'=2] {'row'}, dimensions={0} | all-to-all | bytes 196608 | tf_op jit(solution)/shard_map/all_to_all | solution.py:520
  123.5 4.9 %all-to-all-start.4 = ((f32[32,24,128]{2,1,0:T(8,128)}), f32[32,24,128]{2,1,0:T(8,128)S(1)}, u32[]{:S(2)}, u32[]{:S(2)}) async-start(f32[32,24,128]{2,1,0:T(8,128)} %broadcast_in_dim.5), calls=%async_computation.4 | async-start | bytes 786432 | tf_op jit(solution)/shard_map/all_to_all | solution.py:533
  131.6 3.6 %fresh.1 = f32[2048,256]{1,0:T(8,128)} custom-call(s32[2]{0:T(128)} %pad_add_fusion.place, f32[16,64,128]{2,1,0:T(8,128)} %copy-done.2, f32[16,64,128]{2,1,0:T(8,128)} %copy-done.6, f32[128,256]{1,0:T(8,128)} %w1.3), custom_call_target="tpu_custom_call" | custom-call | flops 402653184 | bytes 4194304 | tf_op jit(solution)/shard_map/fresh/pallas_call | solution.py:523
  135.2 3.7 %all-to-all-done.4 = f32[32,24,128]{2,1,0:T(8,128)S(1)} async-done(((f32[32,24,128]{2,1,0:T(8,128)}), f32[32,24,128]{2,1,0:T(8,128)S(1)}, u32[]{:S(2)}, u32[]{:S(2)}) %all-to-all-start.4) | async-done | bytes 393248 | tf_op jit(solution)/shard_map/all_to_all | solution.py:533
  (98 shorter events, 19.0 us)
Async XLA Ops:
  0.6 7.2 %collective-permute-start = (f32[256,128]{1,0:T(8,128)}, f32[256,128]{1,0:T(8,128)S(1)}, u32[]{:S(2)}, u32[]{:S(2)}) collective-permute-start(f32[256,128]{1,0:T(8,128)} %mine.1), channel_id=1, source_target_pairs={{0,1},{1,0},{2,3},{3,2},{4,5},{5,4},{6,7},{7,6},{8,9},{9,8},{10,11... | collective-permute-start | bytes 393224 | tf_op jit(solution)/shard_map/ppermute | solution.py:324
  4.0 8.3 %collective-permute-start.1 = (f32[256,128]{1,0:T(8,128)}, f32[256,128]{1,0:T(8,128)S(1)}, u32[]{:S(2)}, u32[]{:S(2)}) collective-permute-start(f32[256,128]{1,0:T(8,128)} %mine.1), channel_id=1, source_target_pairs={{0,2},{1,15},{2,4},{3,1},{4,6},{5,3},{6,8},{7,5},{8,10},{9,7},{10,... | collective-permute-start | bytes 393224 | tf_op jit(solution)/shard_map/ppermute | solution.py:333
  7.8 4.4 %collective-permute-start.2 = (f32[256,128]{1,0:T(8,128)S(1)}, f32[256,128]{1,0:T(8,128)S(1)}, u32[]{:S(2)}, u32[]{:S(2)}) collective-permute-start(f32[256,128]{1,0:T(8,128)S(1)} %collective-permute-done.other), channel_id=1, source_target_pairs={{0,2},{1,15},{2,4},{3,1},{4,6},{5,3},{6,8},{7,5},{8,10},{9,7},{10,... | collective-permute-start | bytes 393224 | tf_op jit(solution)/shard_map/ppermute | solution.py:333
  12.3 18.1 %collective-permute-start.6 = (f32[512,128]{1,0:T(8,128)S(1)}, f32[512,128]{1,0:T(8,128)S(1)}, u32[]{:S(2)}, u32[]{:S(2)}) collective-permute-start(f32[512,128]{1,0:T(8,128)S(1)} %constant_dynamic-update-slice_fusion), channel_id=1, source_target_pairs={{0,1},{1,0},{2,3},{3,2},{4,5},{5,4},{6,7},{7,6},{8,9},{9,8},{10,11... | collective-permute-start | bytes 786440 | tf_op jit(solution)/shard_map/ppermute | solution.py:324
  12.9 17.5 %collective-permute-start.4 = (f32[512,128]{1,0:T(8,128)S(1)}, f32[512,128]{1,0:T(8,128)S(1)}, u32[]{:S(2)}, u32[]{:S(2)}) collective-permute-start(f32[512,128]{1,0:T(8,128)S(1)} %constant_dynamic-update-slice_fusion), channel_id=1, source_target_pairs={{0,4},{1,13},{2,6},{3,15},{4,8},{5,1},{6,10},{7,3},{8,12},{9,5},{1... | collective-permute-start | bytes 786440 | tf_op jit(solution)/shard_map/ppermute | solution.py:333
  15.1 15.3 %collective-permute-start.3 = (f32[512,128]{1,0:T(8,128)S(1)}, f32[512,128]{1,0:T(8,128)S(1)}, u32[]{:S(2)}, u32[]{:S(2)}) collective-permute-start(f32[512,128]{1,0:T(8,128)S(1)} %constant_dynamic-update-slice_fusion), channel_id=1, source_target_pairs={{0,2},{1,15},{2,4},{3,1},{4,6},{5,3},{6,8},{7,5},{8,10},{9,7},{10,... | collective-permute-start | bytes 786440 | tf_op jit(solution)/shard_map/ppermute | solution.py:333
  15.8 20.2 %all-to-all-start = ((f32[16,64,128]{2,1,0:T(8,128)}), f32[16,64,128]{2,1,0:T(8,128)S(1)}, u32[]{:S(2)}, u32[]{:S(2)}) async-start(f32[16,64,128]{2,1,0:T(8,128)} %bitcast.46), calls=%async_computation | async-start | bytes 1048576 | tf_op jit(solution)/shard_map/all_to_all | solution.py:345
  23.2 7.1 %collective-permute-start.5 = (f32[256,128]{1,0:T(8,128)S(1)}, f32[256,128]{1,0:T(8,128)S(1)}, u32[]{:S(2)}, u32[]{:S(2)}) collective-permute-start(f32[256,128]{1,0:T(8,128)S(1)} %collective-permute-done.1), channel_id=1, source_target_pairs={{0,6},{1,11},{2,8},{3,13},{4,10},{5,15},{6,12},{7,1},{8,14},{9,3},... | collective-permute-start | bytes 393224 | tf_op jit(solution)/shard_map/ppermute | solution.py:333
  30.4 5.6 %collective-permute-start.7 = (f32[512,128]{1,0:T(8,128)S(1)}, f32[512,128]{1,0:T(8,128)S(1)}, u32[]{:S(2)}, u32[]{:S(2)}) collective-permute-start(f32[512,128]{1,0:T(8,128)S(1)} %collective-permute-done.3), channel_id=1, source_target_pairs={{0,1},{1,0},{2,3},{3,2},{4,5},{5,4},{6,7},{7,6},{8,9},{9,8},{10,11... | collective-permute-start | bytes 786440 | tf_op jit(solution)/shard_map/ppermute | solution.py:324
  34.3 1.8 %collective-permute-start.8 = (f32[512,128]{1,0:T(8,128)S(1)}, f32[512,128]{1,0:T(8,128)S(1)}, u32[]{:S(2)}, u32[]{:S(2)}) collective-permute-start(f32[512,128]{1,0:T(8,128)S(1)} %collective-permute-done.4), channel_id=1, source_target_pairs={{0,1},{1,0},{2,3},{3,2},{4,5},{5,4},{6,7},{7,6},{8,9},{9,8},{10,11... | collective-permute-start | bytes 786440 | tf_op jit(solution)/shard_map/ppermute | solution.py:324
  34.4 1.6 %collective-permute-start.9 = (f32[256,128]{1,0:T(8,128)S(1)}, f32[256,128]{1,0:T(8,128)S(1)}, u32[]{:S(2)}, u32[]{:S(2)}) collective-permute-start(f32[256,128]{1,0:T(8,128)S(1)} %collective-permute-done.5), channel_id=1, source_target_pairs={{0,1},{1,0},{2,3},{3,2},{4,5},{5,4},{6,7},{7,6},{8,9},{9,8},{10,11... | collective-permute-start | bytes 393224 | tf_op jit(solution)/shard_map/ppermute | solution.py:324
  36.1 2.0 %collective-permute-start.10 = (f32[16,64,128]{2,1,0:T(8,128)S(1)}, f32[16,64,128]{2,1,0:T(8,128)S(1)}, u32[]{:S(2)}, u32[]{:S(2)}) collective-permute-start(f32[16,64,128]{2,1,0:T(8,128)S(1)} %all-to-all-done.refs_10_), channel_id=1, source_target_pairs={{0,1},{1,0},{2,3},{3,2},{4,5},{5,4},{6,7},{7,6},{8,9},{9,8},{10,11... | collective-permute-start | bytes 1572872 | tf_op jit(solution)/shard_map/ppermute | solution.py:324
  44.9 2.6 %collective-permute-start.11 = (f32[512,128]{1,0:T(8,128)}, f32[512,128]{1,0:T(8,128)S(1)}, u32[]{:S(2)}, u32[]{:S(2)}) collective-permute-start(f32[512,128]{1,0:T(8,128)} %bitcast.50), channel_id=1, source_target_pairs={{0,1},{1,0},{2,3},{3,2},{4,5},{5,4},{6,7},{7,6},{8,9},{9,8},{10,11... | collective-permute-start | bytes 786440 | tf_op jit(solution)/shard_map/ppermute | solution.py:324
  48.5 5.8 %collective-permute-start.12 = (f32[512,128]{1,0:T(8,128)S(1)}, f32[512,128]{1,0:T(8,128)S(1)}, u32[]{:S(2)}, u32[]{:S(2)}) collective-permute-start(f32[512,128]{1,0:T(8,128)S(1)} %maximum_select_fusion.mine.other), channel_id=1, source_target_pairs={{0,2},{1,15},{2,4},{3,1},{4,6},{5,3},{6,8},{7,5},{8,10},{9,7},{10,... | collective-permute-start | bytes 786440 | tf_op jit(solution)/shard_map/ppermute | solution.py:333
  54.3 13.3 %collective-permute-start.16 = (f32[512,128]{1,0:T(8,128)S(1)}, f32[512,128]{1,0:T(8,128)S(1)}, u32[]{:S(2)}, u32[]{:S(2)}) collective-permute-start(f32[512,128]{1,0:T(8,128)S(1)} %collective-permute-done.12), channel_id=1, source_target_pairs={{0,1},{1,0},{2,3},{3,2},{4,5},{5,4},{6,7},{7,6},{8,9},{9,8},{10,11... | collective-permute-start | bytes 786440 | tf_op jit(solution)/shard_map/ppermute | solution.py:324
  56.7 17.0 %collective-permute-start.14 = (f32[512,128]{1,0:T(8,128)S(1)}, f32[512,128]{1,0:T(8,128)S(1)}, u32[]{:S(2)}, u32[]{:S(2)}) collective-permute-start(f32[512,128]{1,0:T(8,128)S(1)} %collective-permute-done.12), channel_id=1, source_target_pairs={{0,4},{1,13},{2,6},{3,15},{4,8},{5,1},{6,10},{7,3},{8,12},{9,5},{1... | collective-permute-start | bytes 786440 | tf_op jit(solution)/shard_map/ppermute | solution.py:333
  56.8 16.9 %collective-permute-start.13 = (f32[512,128]{1,0:T(8,128)S(1)}, f32[512,128]{1,0:T(8,128)S(1)}, u32[]{:S(2)}, u32[]{:S(2)}) collective-permute-start(f32[512,128]{1,0:T(8,128)S(1)} %collective-permute-done.12), channel_id=1, source_target_pairs={{0,2},{1,15},{2,4},{3,1},{4,6},{5,3},{6,8},{7,5},{8,10},{9,7},{10,... | collective-permute-start | bytes 786440 | tf_op jit(solution)/shard_map/ppermute | solution.py:333
  57.5 21.5 %all-to-all-start.1 = ((f32[16,64,128]{2,1,0:T(8,128)}), f32[16,64,128]{2,1,0:T(8,128)S(1)}, u32[]{:S(2)}, u32[]{:S(2)}) async-start(f32[16,64,128]{2,1,0:T(8,128)} %bitcast.47), calls=%async_computation.1 | async-start | bytes 1048576 | tf_op jit(solution)/shard_map/all_to_all | solution.py:345
  67.5 6.2 %collective-permute-start.15 = (f32[256,128]{1,0:T(8,128)S(1)}, f32[256,128]{1,0:T(8,128)S(1)}, u32[]{:S(2)}, u32[]{:S(2)}) collective-permute-start(f32[256,128]{1,0:T(8,128)S(1)} %slice.23), channel_id=1, source_target_pairs={{0,6},{1,11},{2,8},{3,13},{4,10},{5,15},{6,12},{7,1},{8,14},{9,3},... | collective-permute-start | bytes 393224 | tf_op jit(solution)/shard_map/ppermute | solution.py:333
  73.8 5.3 %collective-permute-start.17 = (f32[512,128]{1,0:T(8,128)S(1)}, f32[512,128]{1,0:T(8,128)S(1)}, u32[]{:S(2)}, u32[]{:S(2)}) collective-permute-start(f32[512,128]{1,0:T(8,128)S(1)} %collective-permute-done.13), channel_id=1, source_target_pairs={{0,1},{1,0},{2,3},{3,2},{4,5},{5,4},{6,7},{7,6},{8,9},{9,8},{10,11... | collective-permute-start | bytes 786440 | tf_op jit(solution)/shard_map/ppermute | solution.py:324
  77.3 1.8 %collective-permute-start.18 = (f32[512,128]{1,0:T(8,128)S(1)}, f32[512,128]{1,0:T(8,128)S(1)}, u32[]{:S(2)}, u32[]{:S(2)}) collective-permute-start(f32[512,128]{1,0:T(8,128)S(1)} %collective-permute-done.14), channel_id=1, source_target_pairs={{0,1},{1,0},{2,3},{3,2},{4,5},{5,4},{6,7},{7,6},{8,9},{9,8},{10,11... | collective-permute-start | bytes 786440 | tf_op jit(solution)/shard_map/ppermute | solution.py:324
  90.4 20.3 %all-to-all-start.2 = ((f32[32,24,128]{2,1,0:T(8,128)}), f32[32,24,128]{2,1,0:T(8,128)S(1)}, u32[]{:S(2)}, u32[]{:S(2)}) async-start(f32[32,24,128]{2,1,0:T(8,128)} %bitcast.54), calls=%async_computation.2 | async-start | bytes 786432 | tf_op jit(solution)/shard_map/all_to_all | solution.py:517
  100.4 30.4 %collective-permute-start.21 = (f32[16,64,128]{2,1,0:T(8,128)S(1)}, f32[16,64,128]{2,1,0:T(8,128)S(1)}, u32[]{:S(2)}, u32[]{:S(2)}) collective-permute-start(f32[16,64,128]{2,1,0:T(8,128)S(1)} %all-to-all-done.1.mine), channel_id=1, source_target_pairs={{0,1},{1,0},{2,3},{3,2},{4,5},{5,4},{6,7},{7,6},{8,9},{9,8},{10,11... | collective-permute-start | bytes 1572872 | tf_op jit(solution)/shard_map/ppermute | solution.py:324
  123.5 15.3 %all-to-all-start.4 = ((f32[32,24,128]{2,1,0:T(8,128)}), f32[32,24,128]{2,1,0:T(8,128)S(1)}, u32[]{:S(2)}, u32[]{:S(2)}) async-start(f32[32,24,128]{2,1,0:T(8,128)} %broadcast_in_dim.5), calls=%async_computation.4 | async-start | bytes 786432 | tf_op jit(solution)/shard_map/all_to_all | solution.py:533
  (26 other events, 196.1 us)

commit v4 on v3

--- a/solution.py
+++ b/solution.py
@@ -17,7 +17,7 @@
 NN = (((1,), (0,)), ((), ()))
 TN = (((0,), (0,)), ((), ()))
 NT = (((1,), (1,)), ((), ()))
-VMEM_LIMIT = 56 * 1024 * 1024
+VMEM_LIMIT = 63 * 1024 * 1024
 
 
 def split2(x):
@@ -309,7 +309,7 @@
 
 SMEM = pl.BlockSpec(memory_space=pltpu.SMEM)
 VMEM = pl.BlockSpec(memory_space=pltpu.VMEM)
-ANY = pl.BlockSpec(memory_space=pl.ANY)
+ANY = pl.BlockSpec(memory_space=pltpu.HBM)
 
 
 def params():
@@ -446,8 +446,8 @@
     panel = jnp.where(q == 0, total, jnp.concatenate([high, low]))
     outgoing_two = pick_call("pick_agg", panel, (0, 0), panel, (1, 0))
     one, outgoing_two = together(along(panel, 1), outgoing_two)
+    theirs_one, outgoing_two = together(swap(one), outgoing_two)
     fresh_mine = to_all(outgoing_two.reshape(N_DOM, HALF, f_dim))
-    theirs_one = swap(one)
     early, g_early = pl.pallas_call(
         early_kernel,
         name="early",

time: 141 us -> 140 us (level)
  waiting for transfers between devices: 22.6 us -> 25.7 us
  starting transfers between devices: 60.2 us -> 57.6 us
    all_to_all x2, waiting for transfers between devices: 0.01 us -> 1.97 us  [to_all(): return lax.all_to_all(x, 'dom', split_axis=0, concat_axis=0, tiled=True)]
    unnamed x49 -> x37, local copies, waits for them, and re-layouts: 3.1 us -> 1.99 us
  transfers between devices with their start and end apart: 26 -> 26, of which waited for: 8 -> 9; matrix products, arithmetic and copies ran while one was open for 2% -> 2% of each run, Pallas kernels for 14% -> 14%
where the time goes in v4:
time: 140 us; the launch traced here: 139 us
  starting transfers between devices  57.6 us (41%)
  Pallas kernels  36.1 us (26%)
  waiting for transfers between devices  25.7 us (18%)
  blocking collectives  11.5 us (8%)
  local copies, waits for them, and re-layouts  4.21 us (3%)
  other arithmetic  2.39 us (2%)
  between operations  1.62 us (1%)
    ppermute x13, starting transfers between devices, swap(): return lax.ppermute(x, 'rep', [(0, 1), (1, 0)])  16.3 us
    all_to_all x2, starting transfers between devices, to_all(): return lax.all_to_all(x, 'dom', split_axis=0, concat_axis=0, tiled=True)  15.6 us
    all_to_all x2, waiting for transfers between devices, local(): lax.all_to_all(part, ('dom', 'rep'), split_axis=0, concat_axis=0, tiled=T...  14.4 us
    all_to_all x2, starting transfers between devices, local(): lax.all_to_all(part, ('dom', 'rep'), split_axis=0, concat_axis=0, tiled=T...  14.1 us
    ppermute x9, starting transfers between devices, along(): return lax.ppermute(x, ('row', 'rep'), pairs)  11.6 us
    all_to_all x1, blocking collectives, local(): part = lax.all_to_all(part, 'row', split_axis=0, concat_axis=0, tiled=True)  11.5 us
    pallas_call x1, Pallas kernels, local(): pl.pallas_call(layer_two_kernel, name='layer_two', out_shape=(jax.ShapeDt...  10.7 us
    ppermute x13, waiting for transfers between devices, swap(): return lax.ppermute(x, 'rep', [(0, 1), (1, 0)])  6.75 us
  transfers between devices with their start and end apart: 26, of which 9 were waited for; matrix products, arithmetic and copies ran while one was open for 2% of the time, Pallas kernels for 14%

profile of v4, /device:TPU:1, one launch (start us, length us, event | category | flops | bytes accessed | tf_op | source)
XLA Modules:
  0.0 139.1 jit_solution(14184401604367618990)
XLA Ops:
  0.6 3.3 %collective-permute-start = (f32[256,128]{1,0:T(8,128)}, f32[256,128]{1,0:T(8,128)S(1)}, u32[]{:S(2)}, u32[]{:S(2)}) collective-permute-start(f32[256,128]{1,0:T(8,128)} %mine.1), channel_id=1, source_target_pairs={{0,1},{1,0},{2,3},{3,2},{4,5},{5,4},{6,7},{7,6},{8,9},{9,8},{10,11... | collective-permute-start | bytes 393224 | tf_op jit(solution)/shard_map/ppermute | solution.py:324
  4.0 3.8 %collective-permute-start.1 = (f32[256,128]{1,0:T(8,128)}, f32[256,128]{1,0:T(8,128)S(1)}, u32[]{:S(2)}, u32[]{:S(2)}) collective-permute-start(f32[256,128]{1,0:T(8,128)} %mine.1), channel_id=1, source_target_pairs={{0,2},{1,15},{2,4},{3,1},{4,6},{5,3},{6,8},{7,5},{8,10},{9,7},{10,... | collective-permute-start | bytes 393224 | tf_op jit(solution)/shard_map/ppermute | solution.py:333
  9.6 2.6 %pick_features.1 = f32[1024,128]{1,0:T(8,128)} custom-call(s32[2]{0:T(128)} %pad_add_fusion.place, f32[256,128]{1,0:T(8,128)} %mine.1, f32[256,128]{1,0:T(8,128)} %copy-done.4, s32[16,128]{1,0:T(8,128)} %bitcast.60), custom_call_target="tpu_custom_call" | custom-call | flops 1048576 | bytes 1048576 | tf_op jit(solution)/shard_map/pick_features/pallas_call | solution.py:385
  12.9 2.2 %collective-permute-start.4 = (f32[512,128]{1,0:T(8,128)S(1)}, f32[512,128]{1,0:T(8,128)}, u32[]{:S(2)}, u32[]{:S(2)}) collective-permute-start(f32[512,128]{1,0:T(8,128)S(1)} %constant_dynamic-update-slice_fusion), channel_id=1, source_target_pairs={{0,4},{1,13},{2,6},{3,15},{4,8},{5,1},{6,10},{7,3},{8,12},{9,5},{1... | collective-permute-start | bytes 786440 | tf_op jit(solution)/shard_map/ppermute | solution.py:333
  15.8 6.8 %all-to-all-start = ((f32[16,64,128]{2,1,0:T(8,128)}), f32[16,64,128]{2,1,0:T(8,128)S(1)}, u32[]{:S(2)}, u32[]{:S(2)}) async-start(f32[16,64,128]{2,1,0:T(8,128)} %bitcast.47), calls=%async_computation | async-start | bytes 1048576 | tf_op jit(solution)/shard_map/all_to_all | solution.py:345
  23.2 1.7 %collective-permute-start.5 = (f32[256,128]{1,0:T(8,128)}, f32[256,128]{1,0:T(8,128)S(1)}, u32[]{:S(2)}, u32[]{:S(2)}) collective-permute-start(f32[256,128]{1,0:T(8,128)} %copy-done.11), channel_id=1, source_target_pairs={{0,6},{1,11},{2,8},{3,13},{4,10},{5,15},{6,12},{7,1},{8,14},{9,3},... | collective-permute-start | bytes 393224 | tf_op jit(solution)/shard_map/ppermute | solution.py:333
  24.9 5.4 %backward.1.c_hbm.refs_12_ = f32[33,128,256]{2,1,0:T(8,128)} custom-call(s32[1,64]{1,0:T(1,128)} %bitcast.62, s32[1,64]{1,0:T(1,128)} %bitcast.65, s32[1,1]{1,0:T(1,128)} %bitcast.39.count_s, f32[512,256]{1,0:T(8,128)} %refs_10_.1, f32[256,256]{1,0:T(8,128)} %refs_9_.1, f32[64,128,128]{2,1,0:T(8,128)} %bitcast.42), custom_call_target="tpu_custom_call" | custom-call | flops 1610612736 | bytes 9437184 | tf_op jit(solution)/shard_map/backward/pallas_call | solution.py:373
  30.4 4.1 %collective-permute-start.7 = (f32[512,128]{1,0:T(8,128)}, f32[512,128]{1,0:T(8,128)S(1)}, u32[]{:S(2)}, u32[]{:S(2)}) collective-permute-start(f32[512,128]{1,0:T(8,128)} %collective-permute-done.3), channel_id=1, source_target_pairs={{0,1},{1,0},{2,3},{3,2},{4,5},{5,4},{6,7},{7,6},{8,9},{9,8},{10,11... | collective-permute-start | bytes 786440 | tf_op jit(solution)/shard_map/ppermute | solution.py:324
  36.7 1.5 %collective-permute-done.10.refs_11_ = f32[16,64,128]{2,1,0:T(8,128)S(1)} collective-permute-done((f32[16,64,128]{2,1,0:T(8,128)S(1)}, f32[16,64,128]{2,1,0:T(8,128)S(1)}, u32[]{:S(2)}, u32[]{:S(2)}) %collective-permute-start.10) | collective-permute-done | bytes 524320 | tf_op jit(solution)/shard_map/ppermute | solution.py:324
  39.0 6.0 %pass_one.1 = f32[4,128,128]{2,1,0:T(8,128)} custom-call(s32[2]{0:T(128)} %pad_add_fusion.place, s32[1,64]{1,0:T(1,128)} %bitcast.63, s32[1,64]{1,0:T(1,128)} %bitcast.66, s32[1,1]{1,0:T(1,128)} %bitcast.40.count_s, f32[2,128,128]{2,1,0:T(8,128)} %bitcast.52, f32[2,128,128]{2,1,0:T(8,128)} %bitcast.53, f32[4,128,128]{2,1,0:T(8,128)} %bitcast.51, ...), custom_call_target="tpu_custom_call" | custom-call | tf_op jit(solution)/shard_map/pass_one/pallas_call | solution.py:419
  45.0 2.7 %collective-permute-start.11 = (f32[512,128]{1,0:T(8,128)}, f32[512,128]{1,0:T(8,128)S(1)}, u32[]{:S(2)}, u32[]{:S(2)}) collective-permute-start(f32[512,128]{1,0:T(8,128)} %bitcast.50), channel_id=1, source_target_pairs={{0,1},{1,0},{2,3},{3,2},{4,5},{5,4},{6,7},{7,6},{8,9},{9,8},{10,11... | collective-permute-start | bytes 786440 | tf_op jit(solution)/shard_map/ppermute | solution.py:324
  50.8 2.6 %pick_agg.1 = f32[1024,128]{1,0:T(8,128)} custom-call(s32[2]{0:T(128)} %pad_add_fusion.place, f32[512,128]{1,0:T(8,128)} %copy-done, f32[512,128]{1,0:T(8,128)} %copy-done, s32[16,128]{1,0:T(8,128)} %bitcast.61), custom_call_target="tpu_custom_call" | custom-call | flops 1048576 | bytes 1048576 | tf_op jit(solution)/shard_map/pick_agg/pallas_call | solution.py:385
  53.4 2.5 %collective-permute-done.12 = f32[512,128]{1,0:T(8,128)S(1)} collective-permute-done((f32[512,128]{1,0:T(8,128)S(1)}, f32[512,128]{1,0:T(8,128)S(1)}, u32[]{:S(2)}, u32[]{:S(2)}) %collective-permute-start.12) | collective-permute-done | bytes 262176 | tf_op jit(solution)/shard_map/ppermute | solution.py:333
  55.9 2.4 %collective-permute-start.13 = (f32[512,128]{1,0:T(8,128)S(1)}, f32[512,128]{1,0:T(8,128)S(1)}, u32[]{:S(2)}, u32[]{:S(2)}) collective-permute-start(f32[512,128]{1,0:T(8,128)S(1)} %collective-permute-done.12), channel_id=1, source_target_pairs={{0,1},{1,0},{2,3},{3,2},{4,5},{5,4},{6,7},{7,6},{8,9},{9,8},{10,11... | collective-permute-start | bytes 786440 | tf_op jit(solution)/shard_map/ppermute | solution.py:324
  60.7 8.9 %all-to-all-start.1 = ((f32[16,64,128]{2,1,0:T(8,128)}), f32[16,64,128]{2,1,0:T(8,128)S(1)}, u32[]{:S(2)}, u32[]{:S(2)}) async-start(f32[16,64,128]{2,1,0:T(8,128)} %bitcast.46), calls=%async_computation.1 | async-start | bytes 1048576 | tf_op jit(solution)/shard_map/all_to_all | solution.py:345
  69.6 5.4 %early.1 = (bf16[12,256,256]{2,1,0:T(8,128)(2,1)}, f32[128,256]{1,0:T(8,128)}) custom-call(s32[2]{0:T(128)} %pad_add_fusion.place, f32[4,128,128]{2,1,0:T(8,128)} %bitcast.45, f32[4,128,128]{2,1,0:T(8,128)} %bitcast.59, f32[4,128,128]{2,1,0:T(8,128)} %bitcast.71, f32[128,256]{1,0:T(8,128)} %w1.3, f32[33,128,256]{2,1,0:T(8,128)} %backward.1.c_hbm.refs_12_), custom_call_target="tpu_custom_call" | custom-call | flops 6442450944 | bytes 4194304 | tf_op jit(solution)/shard_map/early/pallas_call | solution.py:451
  77.9 2.0 %all-to-all-done.1.mine = f32[16,64,128]{2,1,0:T(8,128)S(1)} async-done(((f32[16,64,128]{2,1,0:T(8,128)}), f32[16,64,128]{2,1,0:T(8,128)S(1)}, u32[]{:S(2)}, u32[]{:S(2)}) %all-to-all-start.1) | async-done | bytes 524320 | tf_op jit(solution)/shard_map/all_to_all | solution.py:345
  79.9 10.7 %layer_two.1 = (f32[48,2,8,128]{3,2,1,0:T(8,128)}, f32[256,256]{1,0:T(8,128)}, f32[256,256]{1,0:T(8,128)}) custom-call(s32[2]{0:T(128)} %pad_add_fusion.place, s32[1,64]{1,0:T(1,128)} %bitcast.64, s32[1,64]{1,0:T(1,128)} %bitcast.67, s32[1,1]{1,0:T(1,128)} %bitcast.41.count_s, f32[4,128,128]{2,1,0:T(8,128)} %bitcast.23.refs_0_, ...), custom_call_target="tpu_custom_call" | custom-call | flops 8589934592 | bytes 16777216 | tf_op jit(solution)/shard_map/layer_two/pallas_call | solution.py:473
  90.6 9.2 %all-to-all-start.2 = ((f32[32,24,128]{2,1,0:T(8,128)}), f32[32,24,128]{2,1,0:T(8,128)S(1)}, u32[]{:S(2)}, u32[]{:S(2)}) async-start(f32[32,24,128]{2,1,0:T(8,128)} %bitcast.54), calls=%async_computation.2 | async-start | bytes 786432 | tf_op jit(solution)/shard_map/all_to_all | solution.py:517
  100.1 10.0 %all-to-all-done.2 = f32[32,24,128]{2,1,0:T(8,128)S(1)} async-done(((f32[32,24,128]{2,1,0:T(8,128)}), f32[32,24,128]{2,1,0:T(8,128)S(1)}, u32[]{:S(2)}, u32[]{:S(2)}) %all-to-all-start.2) | async-done | bytes 393248 | tf_op jit(solution)/shard_map/all_to_all | solution.py:517
  110.1 11.5 %all_to_all.25 = f32[8,24,128]{2,1,0:T(8,128)S(1)} all-to-all(f32[8,24,128]{2,1,0:T(8,128)S(1)} %broadcast_in_dim.4), channel_id=1, replica_groups=mesh['dom'=16,'row'=8,'rep'=2] {'row'}, dimensions={0} | all-to-all | bytes 196608 | tf_op jit(solution)/shard_map/all_to_all | solution.py:520
  122.4 4.9 %all-to-all-start.4 = ((f32[32,24,128]{2,1,0:T(8,128)}), f32[32,24,128]{2,1,0:T(8,128)S(1)}, u32[]{:S(2)}, u32[]{:S(2)}) async-start(f32[32,24,128]{2,1,0:T(8,128)} %broadcast_in_dim.5), calls=%async_computation.4 | async-start | bytes 786432 | tf_op jit(solution)/shard_map/all_to_all | solution.py:533
  129.7 3.6 %fresh.1 = f32[2048,256]{1,0:T(8,128)} custom-call(s32[2]{0:T(128)} %pad_add_fusion.place, f32[16,64,128]{2,1,0:T(8,128)} %copy-done.2, f32[16,64,128]{2,1,0:T(8,128)} %collective-permute-done.21.theirs, f32[128,256]{1,0:T(8,128)} %w1.3), custom_call_target="tpu_custom_call" | custom-call | flops 402653184 | bytes 4194304 | tf_op jit(solution)/shard_map/fresh/pallas_call | solution.py:523
  133.3 4.5 %all-to-all-done.4 = f32[32,24,128]{2,1,0:T(8,128)S(1)} async-done(((f32[32,24,128]{2,1,0:T(8,128)}), f32[32,24,128]{2,1,0:T(8,128)S(1)}, u32[]{:S(2)}, u32[]{:S(2)}) %all-to-all-start.4) | async-done | bytes 393248 | tf_op jit(solution)/shard_map/all_to_all | solution.py:533
  (86 shorter events, 19.5 us)
Async XLA Ops:
  0.6 7.2 %collective-permute-start = (f32[256,128]{1,0:T(8,128)}, f32[256,128]{1,0:T(8,128)S(1)}, u32[]{:S(2)}, u32[]{:S(2)}) collective-permute-start(f32[256,128]{1,0:T(8,128)} %mine.1), channel_id=1, source_target_pairs={{0,1},{1,0},{2,3},{3,2},{4,5},{5,4},{6,7},{7,6},{8,9},{9,8},{10,11... | collective-permute-start | bytes 393224 | tf_op jit(solution)/shard_map/ppermute | solution.py:324
  4.0 8.2 %collective-permute-start.1 = (f32[256,128]{1,0:T(8,128)}, f32[256,128]{1,0:T(8,128)S(1)}, u32[]{:S(2)}, u32[]{:S(2)}) collective-permute-start(f32[256,128]{1,0:T(8,128)} %mine.1), channel_id=1, source_target_pairs={{0,2},{1,15},{2,4},{3,1},{4,6},{5,3},{6,8},{7,5},{8,10},{9,7},{10,... | collective-permute-start | bytes 393224 | tf_op jit(solution)/shard_map/ppermute | solution.py:333
  7.8 4.4 %collective-permute-start.2 = (f32[256,128]{1,0:T(8,128)S(1)}, f32[256,128]{1,0:T(8,128)S(1)}, u32[]{:S(2)}, u32[]{:S(2)}) collective-permute-start(f32[256,128]{1,0:T(8,128)S(1)} %collective-permute-done.other), channel_id=1, source_target_pairs={{0,2},{1,15},{2,4},{3,1},{4,6},{5,3},{6,8},{7,5},{8,10},{9,7},{10,... | collective-permute-start | bytes 393224 | tf_op jit(solution)/shard_map/ppermute | solution.py:333
  12.2 18.1 %collective-permute-start.6 = (f32[512,128]{1,0:T(8,128)S(1)}, f32[512,128]{1,0:T(8,128)}, u32[]{:S(2)}, u32[]{:S(2)}) collective-permute-start(f32[512,128]{1,0:T(8,128)S(1)} %constant_dynamic-update-slice_fusion), channel_id=1, source_target_pairs={{0,1},{1,0},{2,3},{3,2},{4,5},{5,4},{6,7},{7,6},{8,9},{9,8},{10,11... | collective-permute-start | bytes 786440 | tf_op jit(solution)/shard_map/ppermute | solution.py:324
  12.9 17.5 %collective-permute-start.4 = (f32[512,128]{1,0:T(8,128)S(1)}, f32[512,128]{1,0:T(8,128)}, u32[]{:S(2)}, u32[]{:S(2)}) collective-permute-start(f32[512,128]{1,0:T(8,128)S(1)} %constant_dynamic-update-slice_fusion), channel_id=1, source_target_pairs={{0,4},{1,13},{2,6},{3,15},{4,8},{5,1},{6,10},{7,3},{8,12},{9,5},{1... | collective-permute-start | bytes 786440 | tf_op jit(solution)/shard_map/ppermute | solution.py:333
  15.1 15.3 %collective-permute-start.3 = (f32[512,128]{1,0:T(8,128)S(1)}, f32[512,128]{1,0:T(8,128)}, u32[]{:S(2)}, u32[]{:S(2)}) collective-permute-start(f32[512,128]{1,0:T(8,128)S(1)} %constant_dynamic-update-slice_fusion), channel_id=1, source_target_pairs={{0,2},{1,15},{2,4},{3,1},{4,6},{5,3},{6,8},{7,5},{8,10},{9,7},{10,... | collective-permute-start | bytes 786440 | tf_op jit(solution)/shard_map/ppermute | solution.py:333
  15.8 20.4 %all-to-all-start = ((f32[16,64,128]{2,1,0:T(8,128)}), f32[16,64,128]{2,1,0:T(8,128)S(1)}, u32[]{:S(2)}, u32[]{:S(2)}) async-start(f32[16,64,128]{2,1,0:T(8,128)} %bitcast.47), calls=%async_computation | async-start | bytes 1048576 | tf_op jit(solution)/shard_map/all_to_all | solution.py:345
  23.2 7.1 %collective-permute-start.5 = (f32[256,128]{1,0:T(8,128)}, f32[256,128]{1,0:T(8,128)S(1)}, u32[]{:S(2)}, u32[]{:S(2)}) collective-permute-start(f32[256,128]{1,0:T(8,128)} %copy-done.11), channel_id=1, source_target_pairs={{0,6},{1,11},{2,8},{3,13},{4,10},{5,15},{6,12},{7,1},{8,14},{9,3},... | collective-permute-start | bytes 393224 | tf_op jit(solution)/shard_map/ppermute | solution.py:333
  30.4 5.8 %collective-permute-start.7 = (f32[512,128]{1,0:T(8,128)}, f32[512,128]{1,0:T(8,128)S(1)}, u32[]{:S(2)}, u32[]{:S(2)}) collective-permute-start(f32[512,128]{1,0:T(8,128)} %collective-permute-done.3), channel_id=1, source_target_pairs={{0,1},{1,0},{2,3},{3,2},{4,5},{5,4},{6,7},{7,6},{8,9},{9,8},{10,11... | collective-permute-start | bytes 786440 | tf_op jit(solution)/shard_map/ppermute | solution.py:324
  34.4 1.8 %collective-permute-start.8 = (f32[512,128]{1,0:T(8,128)}, f32[512,128]{1,0:T(8,128)S(1)}, u32[]{:S(2)}, u32[]{:S(2)}) collective-permute-start(f32[512,128]{1,0:T(8,128)} %collective-permute-done.4), channel_id=1, source_target_pairs={{0,1},{1,0},{2,3},{3,2},{4,5},{5,4},{6,7},{7,6},{8,9},{9,8},{10,11... | collective-permute-start | bytes 786440 | tf_op jit(solution)/shard_map/ppermute | solution.py:324
  36.2 2.0 %collective-permute-start.10 = (f32[16,64,128]{2,1,0:T(8,128)S(1)}, f32[16,64,128]{2,1,0:T(8,128)S(1)}, u32[]{:S(2)}, u32[]{:S(2)}) collective-permute-start(f32[16,64,128]{2,1,0:T(8,128)S(1)} %all-to-all-done.refs_10_), channel_id=1, source_target_pairs={{0,1},{1,0},{2,3},{3,2},{4,5},{5,4},{6,7},{7,6},{8,9},{9,8},{10,11... | collective-permute-start | bytes 1572872 | tf_op jit(solution)/shard_map/ppermute | solution.py:324
  45.0 4.0 %collective-permute-start.11 = (f32[512,128]{1,0:T(8,128)}, f32[512,128]{1,0:T(8,128)S(1)}, u32[]{:S(2)}, u32[]{:S(2)}) collective-permute-start(f32[512,128]{1,0:T(8,128)} %bitcast.50), channel_id=1, source_target_pairs={{0,1},{1,0},{2,3},{3,2},{4,5},{5,4},{6,7},{7,6},{8,9},{9,8},{10,11... | collective-permute-start | bytes 786440 | tf_op jit(solution)/shard_map/ppermute | solution.py:324
  50.1 5.8 %collective-permute-start.12 = (f32[512,128]{1,0:T(8,128)S(1)}, f32[512,128]{1,0:T(8,128)S(1)}, u32[]{:S(2)}, u32[]{:S(2)}) collective-permute-start(f32[512,128]{1,0:T(8,128)S(1)} %maximum_select_fusion.mine.other), channel_id=1, source_target_pairs={{0,2},{1,15},{2,4},{3,1},{4,6},{5,3},{6,8},{7,5},{8,10},{9,7},{10,... | collective-permute-start | bytes 786440 | tf_op jit(solution)/shard_map/ppermute | solution.py:333
  55.9 4.1 %collective-permute-start.13 = (f32[512,128]{1,0:T(8,128)S(1)}, f32[512,128]{1,0:T(8,128)S(1)}, u32[]{:S(2)}, u32[]{:S(2)}) collective-permute-start(f32[512,128]{1,0:T(8,128)S(1)} %collective-permute-done.12), channel_id=1, source_target_pairs={{0,1},{1,0},{2,3},{3,2},{4,5},{5,4},{6,7},{7,6},{8,9},{9,8},{10,11... | collective-permute-start | bytes 786440 | tf_op jit(solution)/shard_map/ppermute | solution.py:324
  58.3 16.6 %collective-permute-start.15 = (f32[512,128]{1,0:T(8,128)S(1)}, f32[512,128]{1,0:T(8,128)}, u32[]{:S(2)}, u32[]{:S(2)}) collective-permute-start(f32[512,128]{1,0:T(8,128)S(1)} %collective-permute-done.12), channel_id=1, source_target_pairs={{0,4},{1,13},{2,6},{3,15},{4,8},{5,1},{6,10},{7,3},{8,12},{9,5},{1... | collective-permute-start | bytes 786440 | tf_op jit(solution)/shard_map/ppermute | solution.py:333
  58.4 16.6 %collective-permute-start.14 = (f32[512,128]{1,0:T(8,128)S(1)}, f32[512,128]{1,0:T(8,128)}, u32[]{:S(2)}, u32[]{:S(2)}) collective-permute-start(f32[512,128]{1,0:T(8,128)S(1)} %collective-permute-done.12), channel_id=1, source_target_pairs={{0,2},{1,15},{2,4},{3,1},{4,6},{5,3},{6,8},{7,5},{8,10},{9,7},{10,... | collective-permute-start | bytes 786440 | tf_op jit(solution)/shard_map/ppermute | solution.py:333
  59.3 15.7 %collective-permute-start.16 = (f32[256,128]{1,0:T(8,128)S(1)}, f32[256,128]{1,0:T(8,128)}, u32[]{:S(2)}, u32[]{:S(2)}) collective-permute-start(f32[256,128]{1,0:T(8,128)S(1)} %slice.23), channel_id=1, source_target_pairs={{0,6},{1,11},{2,8},{3,13},{4,10},{5,15},{6,12},{7,1},{8,14},{9,3},... | collective-permute-start | bytes 393224 | tf_op jit(solution)/shard_map/ppermute | solution.py:333
  60.7 19.2 %all-to-all-start.1 = ((f32[16,64,128]{2,1,0:T(8,128)}), f32[16,64,128]{2,1,0:T(8,128)S(1)}, u32[]{:S(2)}, u32[]{:S(2)}) async-start(f32[16,64,128]{2,1,0:T(8,128)} %bitcast.46), calls=%async_computation.1 | async-start | bytes 1048576 | tf_op jit(solution)/shard_map/all_to_all | solution.py:345
  75.0 2.9 %collective-permute-start.17 = (f32[512,128]{1,0:T(8,128)}, f32[512,128]{1,0:T(8,128)S(1)}, u32[]{:S(2)}, u32[]{:S(2)}) collective-permute-start(f32[512,128]{1,0:T(8,128)} %collective-permute-done.14), channel_id=1, source_target_pairs={{0,1},{1,0},{2,3},{3,2},{4,5},{5,4},{6,7},{7,6},{8,9},{9,8},{10,11... | collective-permute-start | bytes 786440 | tf_op jit(solution)/shard_map/ppermute | solution.py:324
  75.9 1.9 %collective-permute-start.18 = (f32[512,128]{1,0:T(8,128)}, f32[512,128]{1,0:T(8,128)S(1)}, u32[]{:S(2)}, u32[]{:S(2)}) collective-permute-start(f32[512,128]{1,0:T(8,128)} %collective-permute-done.15), channel_id=1, source_target_pairs={{0,1},{1,0},{2,3},{3,2},{4,5},{5,4},{6,7},{7,6},{8,9},{9,8},{10,11... | collective-permute-start | bytes 786440 | tf_op jit(solution)/shard_map/ppermute | solution.py:324
  76.0 1.8 %collective-permute-start.19 = (f32[256,128]{1,0:T(8,128)}, f32[256,128]{1,0:T(8,128)S(1)}, u32[]{:S(2)}, u32[]{:S(2)}) collective-permute-start(f32[256,128]{1,0:T(8,128)} %collective-permute-done.16), channel_id=1, source_target_pairs={{0,1},{1,0},{2,3},{3,2},{4,5},{5,4},{6,7},{7,6},{8,9},{9,8},{10,11... | collective-permute-start | bytes 393224 | tf_op jit(solution)/shard_map/ppermute | solution.py:324
  90.6 19.5 %all-to-all-start.2 = ((f32[32,24,128]{2,1,0:T(8,128)}), f32[32,24,128]{2,1,0:T(8,128)S(1)}, u32[]{:S(2)}, u32[]{:S(2)}) async-start(f32[32,24,128]{2,1,0:T(8,128)} %bitcast.54), calls=%async_computation.2 | async-start | bytes 786432 | tf_op jit(solution)/shard_map/all_to_all | solution.py:517
  99.8 29.9 %collective-permute-start.21 = (f32[16,64,128]{2,1,0:T(8,128)S(1)}, f32[16,64,128]{2,1,0:T(8,128)}, u32[]{:S(2)}, u32[]{:S(2)}) collective-permute-start(f32[16,64,128]{2,1,0:T(8,128)S(1)} %all-to-all-done.1.mine), channel_id=1, source_target_pairs={{0,1},{1,0},{2,3},{3,2},{4,5},{5,4},{6,7},{7,6},{8,9},{9,8},{10,11... | collective-permute-start | bytes 1572872 | tf_op jit(solution)/shard_map/ppermute | solution.py:324
  122.4 15.3 %all-to-all-start.4 = ((f32[32,24,128]{2,1,0:T(8,128)}), f32[32,24,128]{2,1,0:T(8,128)S(1)}, u32[]{:S(2)}, u32[]{:S(2)}) async-start(f32[32,24,128]{2,1,0:T(8,128)} %broadcast_in_dim.5), calls=%async_computation.4 | async-start | bytes 786432 | tf_op jit(solution)/shard_map/all_to_all | solution.py:533
  (20 other events, 163.6 us)
